TPU v7x, 32 devices: a whole 2x2x4 slice. The times are simulated.
32 devices in a mesh: dp: 4 (over z), row: 4 (over y, x), col: 2 (over core).
Axes of the slice: x: 2, y: 2, z: 4, core: 2. Of those that a mesh axis runs over, the one named last changes fastest.
Arguments:
- inputs: bfloat16 [4096, 2560], P(('dp', 'col'), 'row'), may hold values from -6 to 6
- positions: int32 [4096], P(('dp', 'row')), may hold values from 0 to 767, as said below
- branch_matrix: float32 [2560, 2560], P(('row', 'dp'), 'col'), may hold values from -0.125 to 0.125
- gelu_matrix: float32 [2560, 2560], P(('row', 'dp'), 'col'), may hold values from -0.125 to 0.125
- output_matrix: float32 [2560, 2560], P(('col', 'dp'), 'row'), may hold values from -0.5 to 0.5
- gate_matrix: float32 [2560, 7680], P(('row', 'dp'), 'col'), may hold values from -0.125 to 0.125
- up_matrix: float32 [2560, 7680], P(('row', 'dp'), 'col'), may hold values from -0.125 to 0.125
- down_matrix: float32 [7680, 2560], P(('col', 'dp'), 'row'), may hold values from -0.09375 to 0.09375
- input_blocks: float32 [10, 256, 256], P('col', 'dp'), may hold values from -0.375 to 0.375
- decay_blocks: float32 [10, 256, 256], P('col', 'dp'), may hold values from -0.375 to 0.375
- conv_taps: float32 [4, 2560], P(None, ('col', 'dp')), may hold values from -3 to 3
- conv_bias: float32 [2560], P(('col', 'dp')), may hold values from -3 to 3
- branch_bias: float32 [2560], P(('col', 'dp')), may hold values from -3 to 3
- gelu_bias: float32 [2560], P(('col', 'dp')), may hold values from -3 to 3
- input_bias: float32 [2560], P(('col', 'dp')), may hold values from -3 to 3
- decay_bias: float32 [2560], P(('col', 'dp')), may hold values from -3 to 3
- decay_param: float32 [2560], P(('col', 'dp')), may hold values from -11 to -2.5
- output_bias: float32 [2560], P(('row', 'dp')), may hold values from -3 to 3
- gate_bias: float32 [7680], P(('col', 'dp')), may hold values from -3 to 3
- up_bias: float32 [7680], P(('col', 'dp')), may hold values from -3 to 3
- down_bias: float32 [2560], P(('row', 'dp')), may hold values from -3 to 3
- norm_first: float32 [2560], P(('row', 'dp')), may hold values from -3 to 3
- norm_second: float32 [2560], P(('row', 'dp')), may hold values from -3 to 3
- cotangent: bfloat16 [4096, 2560], P(('dp', 'col'), 'row'), may hold values from -6 to 6
Outputs:
- layer_out: bfloat16 [4096, 2560], P(('dp', 'col'), 'row')
- input_grad: float32 [4096, 2560], P(('dp', 'col'), 'row')
- branch_matrix_grad: float32 [2560, 2560], P(('row', 'dp'), 'col')
- gelu_matrix_grad: float32 [2560, 2560], P(('row', 'dp'), 'col')
- output_matrix_grad: float32 [2560, 2560], P(('col', 'dp'), 'row')
- gate_matrix_grad: float32 [2560, 7680], P(('row', 'dp'), 'col')
- up_matrix_grad: float32 [2560, 7680], P(('row', 'dp'), 'col')
- down_matrix_grad: float32 [7680, 2560], P(('col', 'dp'), 'row')
- input_blocks_grad: float32 [10, 256, 256], P('col', 'dp')
- decay_blocks_grad: float32 [10, 256, 256], P('col', 'dp')
- conv_taps_grad: float32 [4, 2560], P(None, ('col', 'dp'))
- conv_bias_grad: float32 [2560], P(('col', 'dp'))
- branch_bias_grad: float32 [2560], P(('col', 'dp'))
- gelu_bias_grad: float32 [2560], P(('col', 'dp'))
- input_bias_grad: float32 [2560], P(('col', 'dp'))
- decay_bias_grad: float32 [2560], P(('col', 'dp'))
- decay_param_grad: float32 [2560], P(('col', 'dp'))
- output_bias_grad: float32 [2560], P(('row', 'dp'))
- gate_bias_grad: float32 [7680], P(('col', 'dp'))
- up_bias_grad: float32 [7680], P(('col', 'dp'))
- down_bias_grad: float32 [2560], P(('row', 'dp'))
- norm_first_grad: float32 [2560], P(('row', 'dp'))
- norm_second_grad: float32 [2560], P(('row', 'dp'))
Inputs may be any that keep to these rules, and one draw needn't show every extreme that they name: `positions`: within each aligned block of 1024 tokens of one index of dp the first position is 0, and each next one is the previous plus one or 0, where a sequence starts; each such block of 1024 tokens holds three sequences, the second of them 1024 - 256 tokens long.
All inputs are finite; a program needn't handle non-finite values.
Results may differ from a plain program's by a relative error of at most 0.0075.
The roundings to bfloat16 on the way count: a program that leaves them out, or rounds other values in their place, can miss the bound.
Values may be sent and summed in bfloat16 or wider, within the bound.
A program may use at most 256 MiB of HBM per device.

v0:
```python
import jax
import jax.numpy as jnp
from jax import lax
from jax.sharding import PartitionSpec as P

D = 2560


epsilon = 1e-06


def shifted(shard, axis, by):
    count = lax.axis_size(axis)
    pairs = [(i, i + by) for i in range(count) if 0 <= i + by < count]
    return lax.ppermute(shard, axis, pairs)


def entering(shard, axis, combine, identity, reverse):
    count, place = (lax.axis_size(axis), lax.axis_index(axis))
    everything = jax.tree.map(lambda part: lax.all_gather(part, axis), shard)
    start = jax.tree.map(
        lambda part, zero: jnp.broadcast_to(jnp.asarray(zero, part.dtype), part.shape),
        shard,
        identity,
    )

    def lap(k, before):
        at = count - 1 - k if reverse else k
        reached = at > place if reverse else at < place
        new = combine(before, jax.tree.map(lambda part: part[at], everything))
        return jax.tree.map(lambda a, b: jnp.where(reached, a, b), new, before)

    return lax.fori_loop(0, count, lap, start)


def combine(earlier, later):
    return (earlier[0] * later[0], later[0] * earlier[1] + later[1])


def gate_math(conv, logit_in, logit_decay, input_bias, decay_bias, decay_param, starting):
    input_gate = jax.nn.sigmoid(logit_in + input_bias)
    decay_gate = jax.nn.sigmoid(logit_decay + decay_bias)
    log_decay = -8.0 * decay_gate * jax.nn.softplus(decay_param)
    decay = jnp.where(starting, 0.0, jnp.exp(log_decay))
    multiplier = jnp.where(starting, 1.0, jnp.sqrt(-jnp.expm1(2.0 * log_decay)))
    return (decay, multiplier * input_gate * conv)


def contract(piece, matrix, flipped):
    if flipped:
        return lax.dot_general(
            piece, matrix, (((1,), (1,)), ((), ())), preferred_element_type=jnp.float32
        )
    return jnp.dot(piece, matrix, preferred_element_type=jnp.float32)


def left_product(left, right):
    return lax.dot_general(
        left, right, (((0,), (0,)), ((), ())), preferred_element_type=jnp.float32
    )


def row_total(values):
    return lax.psum(values, "row")


def spread_col(values):
    return lax.all_gather(values, "col", axis=0, tiled=True)


def spread_row(values):
    return lax.all_gather(values, "row", axis=0, tiled=True)


def reduce_row(whole, matrix, flipped):
    rows_here = whole.shape[0] // lax.axis_size("row")

    def term(start, count):
        return contract(whole, matrix, flipped)

    return lax.psum_scatter(
        term(jnp.int32(0), lax.axis_size("row") * rows_here), "row", scatter_dimension=0, tiled=True
    )


def reduce_col(whole, matrix, flipped):
    rows_here = whole.shape[0] // lax.axis_size("col")

    def term(start, count):
        return contract(whole, matrix, flipped)

    return lax.psum_scatter(
        term(jnp.int32(0), lax.axis_size("col") * rows_here), "col", scatter_dimension=0, tiled=True
    )


def norm_forward(resid, gain):
    total = row_total(jnp.sum(resid * resid, axis=1))
    inverse = lax.rsqrt(total / D + epsilon)[:, None]
    return ((resid * inverse * (1.0 + gain)).astype(jnp.bfloat16), inverse)


def norm_backward(grad, resid, inverse, gain):
    scaled = grad * (1.0 + gain)
    inner = row_total(jnp.sum(scaled * resid, axis=1))[:, None]
    back = inverse * scaled - resid * inverse**3 * inner / D
    gain_grad = jnp.sum(grad * resid * inverse, axis=0)
    return (back, gain_grad)


def fetch_first(masters):
    copies = [master.astype(jnp.bfloat16) for master in masters]
    return (
        lax.all_gather(copies[0], "dp", axis=0, tiled=True),
        lax.all_gather(copies[1], "dp", axis=0, tiled=True),
        lax.all_gather(copies[2], "dp", axis=0, tiled=True),
        lax.all_gather(copies[3], "dp", axis=0, tiled=True),
        lax.all_gather(copies[4], "dp", axis=0, tiled=True),
        lax.all_gather(copies[5], "dp", axis=0, tiled=True),
        lax.all_gather(copies[6], "dp", axis=1, tiled=True),
        lax.all_gather(copies[7], "dp", axis=1, tiled=True),
        lax.all_gather(copies[8], "dp", axis=1, tiled=True),
        lax.all_gather(copies[9], "dp", axis=0, tiled=True),
        lax.all_gather(copies[10], "dp", axis=0, tiled=True),
        lax.all_gather(copies[11], "dp", axis=0, tiled=True),
        lax.all_gather(copies[12], "dp", axis=0, tiled=True),
        lax.all_gather(copies[13], "dp", axis=0, tiled=True),
        lax.all_gather(copies[14], "dp", axis=0, tiled=True),
        lax.all_gather(copies[15], "dp", axis=0, tiled=True),
        lax.all_gather(copies[16], "dp", axis=0, tiled=True),
        lax.all_gather(copies[17], "dp", axis=0, tiled=True),
        lax.all_gather(copies[18], "dp", axis=0, tiled=True),
        lax.all_gather(copies[19], "dp", axis=0, tiled=True),
        lax.all_gather(copies[20], "dp", axis=0, tiled=True),
    )


def shards(
    inputs,
    positions,
    branch_matrix,
    gelu_matrix,
    output_matrix,
    gate_matrix,
    up_matrix,
    down_matrix,
    input_blocks,
    decay_blocks,
    conv_taps,
    conv_bias,
    branch_bias,
    gelu_bias,
    input_bias,
    decay_bias,
    decay_param,
    output_bias,
    gate_bias,
    up_bias,
    down_bias,
    norm_first,
    norm_second,
    cotangent,
):
    masters = (
        branch_matrix,
        gelu_matrix,
        output_matrix,
        gate_matrix,
        up_matrix,
        down_matrix,
        input_blocks,
        decay_blocks,
        conv_taps,
        conv_bias,
        branch_bias,
        gelu_bias,
        input_bias,
        decay_bias,
        decay_param,
        output_bias,
        gate_bias,
        up_bias,
        down_bias,
        norm_first,
        norm_second,
    )
    full = fetch_first(masters)
    xy_matrix = jnp.concatenate((full[0], full[1]), axis=1)
    gu_matrix = jnp.concatenate((full[3], full[4]), axis=1)
    vectors = [value.astype(jnp.float32) for value in full[8:]]
    (
        tap_weights,
        conv_shift,
        branch_shift,
        gelu_shift,
        input_shift,
        decay_shift,
        decay_raw,
        output_shift,
        gate_shift,
        up_shift,
        down_shift,
        gain_first,
        gain_second,
    ) = vectors
    width = full[0].shape[1]
    hidden_width = full[3].shape[1]
    heads_here = full[6].shape[0]
    block_width = full[6].shape[2]
    conv_width = tap_weights.shape[0]
    resid = inputs.astype(jnp.float32)
    normed_first, inverse_first = norm_forward(resid, gain_first)
    normed_first_all = spread_col(normed_first)
    projected = reduce_row(normed_first_all, xy_matrix, False)
    steps_count = projected.shape[0]
    branch = projected[:, :width] + branch_shift
    gelu_in = projected[:, width:] + gelu_shift
    side, gelu_pull = jax.vjp(jax.nn.gelu, gelu_in)
    spots = positions[:, None]
    starting = spots == 0
    masks = [(spots >= k).astype(jnp.float32) for k in range(conv_width)]
    lower = shifted(branch[steps_count - conv_width + 1 :], "row", 1)
    padded = jnp.concatenate((lower, branch), axis=0)
    conv = conv_shift + sum(
        (
            tap_weights[k]
            * padded[conv_width - 1 - k : conv_width - 1 - k + steps_count]
            * masks[k]
            for k in range(conv_width)
        )
    )
    conv_low = conv.astype(jnp.bfloat16).reshape(steps_count, heads_here, block_width)
    logit_in = jnp.einsum(
        "thi,hij->thj", conv_low, full[6], preferred_element_type=jnp.float32
    ).reshape(steps_count, width)
    logit_decay = jnp.einsum(
        "thi,hij->thj", conv_low, full[7], preferred_element_type=jnp.float32
    ).reshape(steps_count, width)

    def gates(conv_value, in_value, decay_value, in_bias, dec_bias, raw_value):
        return gate_math(conv_value, in_value, decay_value, in_bias, dec_bias, raw_value, starting)

    (decay, pushed), gate_pull = jax.vjp(
        gates, conv, logit_in, logit_decay, input_shift, decay_shift, decay_raw
    )
    running, local_state = lax.associative_scan(combine, (decay, pushed), axis=0)
    ones_row = jnp.ones((width,), jnp.float32)
    zeros_row = jnp.zeros((width,), jnp.float32)
    carried = entering((running[-1], local_state[-1]), "row", combine, (ones_row, zeros_row), False)
    state_in = carried[1]
    state = local_state + running * state_in
    mixed = (state * side).astype(jnp.bfloat16)
    mixed_all = spread_row(mixed)
    middle = resid + reduce_col(mixed_all, full[2], False) + output_shift
    normed_second, inverse_second = norm_forward(middle, gain_second)
    normed_second_all = spread_col(normed_second)
    gate_up = reduce_row(normed_second_all, gu_matrix, False)

    def feed(gate_value, up_value):
        return jax.nn.gelu(gate_value) * up_value

    hidden_value, feed_pull = jax.vjp(
        feed, gate_up[:, :hidden_width] + gate_shift, gate_up[:, hidden_width:] + up_shift
    )
    hidden = hidden_value.astype(jnp.bfloat16)
    hidden_all = spread_row(hidden)
    layer_out = (middle + reduce_col(hidden_all, full[5], False) + down_shift).astype(jnp.bfloat16)
    grad_out = cotangent.astype(jnp.float32)
    grad_out_all = spread_col(cotangent)
    down_grad = left_product(hidden_all, grad_out_all)
    down_bias_grad = jnp.sum(grad_out, axis=0)
    grad_hidden = reduce_row(grad_out_all, full[5], True)
    grad_gate, grad_up = feed_pull(grad_hidden)
    gate_bias_grad = jnp.sum(grad_gate, axis=0)
    up_bias_grad = jnp.sum(grad_up, axis=0)
    grad_gate_up = jnp.concatenate((grad_gate, grad_up), axis=1).astype(jnp.bfloat16)
    grad_gate_up_all = spread_row(grad_gate_up)
    gate_up_grad = left_product(normed_second_all, grad_gate_up_all)
    grad_normed_second = reduce_col(grad_gate_up_all, gu_matrix, True)
    back_second, norm_second_grad = norm_backward(
        grad_normed_second, middle, inverse_second, gain_second
    )
    grad_middle = grad_out + back_second
    output_bias_grad = jnp.sum(grad_middle, axis=0)
    grad_middle_all = spread_col(grad_middle.astype(jnp.bfloat16))
    output_grad = left_product(mixed_all, grad_middle_all)
    grad_mixed = reduce_row(grad_middle_all, full[2], True)
    grad_direct = grad_mixed * side
    grad_side = grad_mixed * state
    next_decay = jnp.concatenate((decay[1:], jnp.ones((1, width), jnp.float32)), axis=0)
    reach, local_grad = lax.associative_scan(
        combine, (next_decay, grad_direct), reverse=True, axis=0
    )
    later_carry = entering(
        (decay[0] * reach[0], decay[0] * local_grad[0]), "row", combine, (ones_row, zeros_row), True
    )
    grad_state = local_grad + reach * later_carry[1]
    previous_state = jnp.concatenate((state_in[None, :], state[:-1]), axis=0)
    grad_decay = grad_state * previous_state
    (
        grad_conv,
        grad_logit_in,
        grad_logit_decay,
        input_bias_grad,
        decay_bias_grad,
        decay_param_grad,
    ) = gate_pull((grad_decay, grad_state))
    low_in = grad_logit_in.astype(jnp.bfloat16).reshape(steps_count, heads_here, block_width)
    low_decay = grad_logit_decay.astype(jnp.bfloat16).reshape(steps_count, heads_here, block_width)
    input_blocks_grad = jnp.einsum(
        "thi,thj->hij", conv_low, low_in, preferred_element_type=jnp.float32
    )
    decay_blocks_grad = jnp.einsum(
        "thi,thj->hij", conv_low, low_decay, preferred_element_type=jnp.float32
    )
    grad_conv = grad_conv + jnp.einsum(
        "thj,hij->thi", low_in, full[6], preferred_element_type=jnp.float32
    ).reshape(steps_count, width)
    grad_conv = grad_conv + jnp.einsum(
        "thj,hij->thi", low_decay, full[7], preferred_element_type=jnp.float32
    ).reshape(steps_count, width)
    conv_bias_grad = jnp.sum(grad_conv, axis=0)
    masked = [grad_conv * tap_weights[k] * masks[k] for k in range(conv_width)]
    spread_back = sum(
        (jnp.pad(masked[k], ((conv_width - 1 - k, k), (0, 0))) for k in range(conv_width))
    )
    upper = shifted(spread_back[: conv_width - 1], "row", -1)
    grad_branch = spread_back[conv_width - 1 :] + jnp.concatenate(
        (jnp.zeros((steps_count - conv_width + 1, width), jnp.float32), upper), axis=0
    )
    tap_grad = jnp.stack(
        [
            jnp.sum(
                grad_conv
                * padded[conv_width - 1 - k : conv_width - 1 - k + steps_count]
                * masks[k],
                axis=0,
            )
            for k in range(conv_width)
        ]
    )
    branch_bias_grad = jnp.sum(grad_branch, axis=0)
    grad_gelu_in = gelu_pull(grad_side)[0]
    gelu_bias_grad = jnp.sum(grad_gelu_in, axis=0)
    grad_projected = jnp.concatenate((grad_branch, grad_gelu_in), axis=1).astype(jnp.bfloat16)
    grad_projected_all = spread_row(grad_projected)
    projection_grad = left_product(normed_first_all, grad_projected_all)
    grad_normed_first = reduce_col(grad_projected_all, xy_matrix, True)
    back_first, norm_first_grad = norm_backward(grad_normed_first, resid, inverse_first, gain_first)
    input_grad = grad_middle + back_first
    row_sums = lax.psum(
        (
            tap_grad,
            conv_bias_grad,
            branch_bias_grad,
            gelu_bias_grad,
            input_bias_grad,
            decay_bias_grad,
            decay_param_grad,
            gate_bias_grad,
            up_bias_grad,
            input_blocks_grad,
            decay_blocks_grad,
        ),
        "row",
    )
    col_sums = lax.psum(
        (output_bias_grad, down_bias_grad, norm_first_grad, norm_second_grad), "col"
    )
    reduced = (
        lax.psum_scatter(projection_grad[:, :width], "dp", scatter_dimension=0, tiled=True),
        lax.psum_scatter(projection_grad[:, width:], "dp", scatter_dimension=0, tiled=True),
        lax.psum_scatter(output_grad, "dp", scatter_dimension=0, tiled=True),
        lax.psum_scatter(gate_up_grad[:, :hidden_width], "dp", scatter_dimension=0, tiled=True),
        lax.psum_scatter(gate_up_grad[:, hidden_width:], "dp", scatter_dimension=0, tiled=True),
        lax.psum_scatter(down_grad, "dp", scatter_dimension=0, tiled=True),
        lax.psum_scatter(row_sums[9], "dp", scatter_dimension=1, tiled=True),
        lax.psum_scatter(row_sums[10], "dp", scatter_dimension=1, tiled=True),
        lax.psum_scatter(row_sums[0], "dp", scatter_dimension=1, tiled=True),
        lax.psum_scatter(row_sums[1], "dp", scatter_dimension=0, tiled=True),
        lax.psum_scatter(row_sums[2], "dp", scatter_dimension=0, tiled=True),
        lax.psum_scatter(row_sums[3], "dp", scatter_dimension=0, tiled=True),
        lax.psum_scatter(row_sums[4], "dp", scatter_dimension=0, tiled=True),
        lax.psum_scatter(row_sums[5], "dp", scatter_dimension=0, tiled=True),
        lax.psum_scatter(row_sums[6], "dp", scatter_dimension=0, tiled=True),
        lax.psum_scatter(col_sums[0], "dp", scatter_dimension=0, tiled=True),
        lax.psum_scatter(row_sums[7], "dp", scatter_dimension=0, tiled=True),
        lax.psum_scatter(row_sums[8], "dp", scatter_dimension=0, tiled=True),
        lax.psum_scatter(col_sums[1], "dp", scatter_dimension=0, tiled=True),
        lax.psum_scatter(col_sums[2], "dp", scatter_dimension=0, tiled=True),
        lax.psum_scatter(col_sums[3], "dp", scatter_dimension=0, tiled=True),
    )
    return (layer_out, input_grad) + tuple(reduced)


def solution(mesh):
    in_specs = (
        P(("dp", "col"), "row"),
        P(("dp", "row")),
        P(("row", "dp"), "col"),
        P(("row", "dp"), "col"),
        P(("col", "dp"), "row"),
        P(("row", "dp"), "col"),
        P(("row", "dp"), "col"),
        P(("col", "dp"), "row"),
        P("col", "dp", None),
        P("col", "dp", None),
        P(None, ("col", "dp")),
        P(("col", "dp")),
        P(("col", "dp")),
        P(("col", "dp")),
        P(("col", "dp")),
        P(("col", "dp")),
        P(("col", "dp")),
        P(("row", "dp")),
        P(("col", "dp")),
        P(("col", "dp")),
        P(("row", "dp")),
        P(("row", "dp")),
        P(("row", "dp")),
        P(("dp", "col"), "row"),
    )
    out_specs = (
        P(("dp", "col"), "row"),
        P(("dp", "col"), "row"),
        P(("row", "dp"), "col"),
        P(("row", "dp"), "col"),
        P(("col", "dp"), "row"),
        P(("row", "dp"), "col"),
        P(("row", "dp"), "col"),
        P(("col", "dp"), "row"),
        P("col", "dp", None),
        P("col", "dp", None),
        P(None, ("col", "dp")),
        P(("col", "dp")),
        P(("col", "dp")),
        P(("col", "dp")),
        P(("col", "dp")),
        P(("col", "dp")),
        P(("col", "dp")),
        P(("row", "dp")),
        P(("col", "dp")),
        P(("col", "dp")),
        P(("row", "dp")),
        P(("row", "dp")),
        P(("row", "dp")),
    )
    return jax.shard_map(shards, mesh=mesh, in_specs=in_specs, out_specs=out_specs, check_vma=False)
```

profile of v0, /device:TPU:0, one launch (start us, length us, event | category | flops | bytes accessed | tf_op | source)
XLA Modules:
  0.0 2685.7 jit_solution(14002178088598580612)
XLA Ops:
  16.0 11.4 psum.133
  27.4 21.7 all-reduce.99
  55.4 36.4 %all-gather.24.cloned.1.call-done = bf16[640,1280]{1,0:T(8,128)(2,1)} async-done(((bf16[160,1280]{1,0:T(8,128)(2,1)}), bf16[640,1280]{1,0:T(8,128)(2,1)}) %all-gather.24.cloned.1.call-update) | async-done | bytes 1638416 | tf_op jit(solution)/shard_map/all_gather | solution.py:115
  94.6 7.7 all-gather.20.cloned.1.call-done
  102.3 10.4 fusion.90
  114.9 13.3 all-gather
  128.3 16.9 all_gather.108
  145.2 17.4 all_gather.111
  163.2 54.4 %reduce-scatter.20.cloned.1.call-done = f32[256,2560]{1,0:T(8,128)} async-done(((f32[1024,2560]{1,0:T(8,128)}), f32[256,2560]{1,0:T(8,128)}) %reduce-scatter.20.cloned.1.call-update) | async-done | bytes 2621456 | tf_op jit(solution)/shard_map/reduce_scatter | solution.py:81
  322.2 9.9 all-gather.2
  340.7 6.6 all-gather.1
  352.5 40.1 %all-gather.26.cloned.1.call-done = bf16[1024,1280]{1,0:T(8,128)(2,1)} async-done(((bf16[256,1280]{1,0:T(8,128)(2,1)}), bf16[1024,1280]{1,0:T(8,128)(2,1)}) %all-gather.26.cloned.1.call-update) | async-done | bytes 2621456 | tf_op jit(solution)/shard_map/all_gather | solution.py:72
  410.4 10.2 psum.134
  421.7 95.5 %all-gather.38.cloned.1.call-done = bf16[3840,640]{1,0:T(8,128)(2,1)} async-done(((bf16[960,640]{1,0:T(8,128)(2,1)}), bf16[3840,640]{1,0:T(8,128)(2,1)}) %all-gather.38.cloned.1.call-update) | async-done | bytes 4915216 | tf_op jit(solution)/shard_map/all_gather | solution.py:119
  517.2 12.3 fusion.96
  529.6 80.8 %all-gather.32.cloned.1.call-done = bf16[640,3840]{1,0:T(8,128)(2,1)} async-done(((bf16[160,3840]{1,0:T(8,128)(2,1)}), bf16[640,3840]{1,0:T(8,128)(2,1)}) %all-gather.32.cloned.1.call-update) | async-done | bytes 4915216 | tf_op jit(solution)/shard_map/all_gather | solution.py:117
  615.3 87.8 %all-gather.34.cloned.1.call-done = bf16[640,3840]{1,0:T(8,128)(2,1)} async-done(((bf16[160,3840]{1,0:T(8,128)(2,1)}), bf16[640,3840]{1,0:T(8,128)(2,1)}) %all-gather.34.cloned.1.call-update) | async-done | bytes 4915216 | tf_op jit(solution)/shard_map/all_gather | solution.py:118
  713.1 21.2 fusion.94
  735.0 129.2 %reduce-scatter.28.cloned.1.call-done = f32[256,3840]{1,0:T(8,128)} async-done(((f32[1024,3840]{1,0:T(8,128)}), f32[256,3840]{1,0:T(8,128)}) %reduce-scatter.28.cloned.1.call-update) | async-done | bytes 3932176 | tf_op jit(solution)/shard_map/reduce_scatter | solution.py:81
  864.2 276.2 %reduce-scatter.24.cloned.1.call-done = f32[256,7680]{1,0:T(8,128)} async-done(((f32[1024,7680]{1,0:T(8,128)}), f32[256,7680]{1,0:T(8,128)}) %reduce-scatter.24.cloned.1.call-update) | async-done | bytes 7864336 | tf_op jit(solution)/shard_map/reduce_scatter | solution.py:81
  1140.4 8.2 multiply_reduce_fusion
  1151.4 148.2 %all-gather.42.cloned.1.call-done = bf16[1024,7680]{1,0:T(8,128)(2,1)} async-done(((bf16[256,7680]{1,0:T(8,128)(2,1)}), bf16[1024,7680]{1,0:T(8,128)(2,1)}) %all-gather.42.cloned.1.call-update) | async-done | bytes 15728656 | tf_op jit(solution)/shard_map/all_gather | solution.py:72
  1299.6 18.3 fusion.97
  1317.9 67.2 %all-gather.36.cloned.1.call-done = bf16[1024,3840]{1,0:T(8,128)(2,1)} async-done(((bf16[256,3840]{1,0:T(8,128)(2,1)}), bf16[1024,3840]{1,0:T(8,128)(2,1)}) %all-gather.36.cloned.1.call-update) | async-done | bytes 7864336 | tf_op jit(solution)/shard_map/all_gather | solution.py:72
  1385.1 11.1 fusion.95
  1399.7 10.1 psum.135
  1416.8 10.8 all-gather.44.cloned.1.call-done
  1454.7 41.6 %reduce-scatter.32.cloned.1.call-done = f32[256,1280]{1,0:T(8,128)} async-done(((f32[1024,1280]{1,0:T(8,128)}), f32[256,1280]{1,0:T(8,128)}) %reduce-scatter.32.cloned.1.call-update) | async-done | bytes 1310736 | tf_op jit(solution)/shard_map/reduce_scatter | solution.py:81
  1630.0 8.0 all-gather.4
  1638.0 7.5 all-gather.3
  1652.5 10.8 rev.8
  1687.2 6.8 multiply_reduce_fusion.5
  1702.4 62.3 %all-gather.46.cloned.1.call-done = bf16[1024,2560]{1,0:T(8,128)(2,1)} async-done(((bf16[256,2560]{1,0:T(8,128)(2,1)}), bf16[1024,2560]{1,0:T(8,128)(2,1)}) %all-gather.46.cloned.1.call-update) | async-done | bytes 5242896 | tf_op jit(solution)/shard_map/all_gather | solution.py:72
  1764.7 8.2 fusion.99
  1786.1 11.0 fusion.103
  1805.5 17.7 fusion.102
  1823.1 15.0 fusion.77
  1838.8 12.3 reduce-scatter.50.cloned.1.call-done
  1863.1 11.4 reduce-scatter.52.cloned.1.call-done
  1875.5 38.9 %all-reduce.105.cloned.1.call-done = (f32[1280]{0:T(1024)}, f32[1280]{0:T(1024)}, f32[1280]{0:T(1024)}, f32[1280]{0:T(1024)}, f32[1280]{0:T(1024)}, /*index=5*/f...) async-done(((f32[1280]{0:T(1024)}, f32[1280]{0:T(1024)}, f32[1280]{0:T(1024)}, ...) | async-done | bytes 71696
  1926.6 16.9 all-reduce.95
  1945.0 139.6 %reduce-scatter.46.cloned.1.call-done = f32[960,640]{1,0:T(8,128)} async-done(((f32[3840,640]{1,0:T(8,128)}), f32[960,640]{1,0:T(8,128)}) %reduce-scatter.46.cloned.1.call-update) | async-done | bytes 2457616 | tf_op jit(solution)/shard_map/reduce_scatter | solution.py:376
  2084.6 66.3 %reduce-scatter.40.cloned.1.call-done = f32[320,640]{1,0:T(8,128)} async-done(((f32[1280,640]{1,0:T(8,128)}), f32[320,640]{1,0:T(8,128)}) %reduce-scatter.40.cloned.1.call-update) | async-done | bytes 819216 | tf_op jit(solution)/shard_map/reduce_scatter | solution.py:373
  2150.9 170.7 %reduce-scatter.42.cloned.1.call-done = f32[160,3840]{1,0:T(8,128)} async-done(((f32[640,3840]{1,0:T(8,128)}), f32[160,3840]{1,0:T(8,128)}) %reduce-scatter.42.cloned.1.call-update) | async-done | bytes 2457616 | tf_op jit(solution)/shard_map/reduce_scatter | solution.py:374
  2321.6 171.3 %reduce-scatter.44.cloned.1.call-done = f32[160,3840]{1,0:T(8,128)} async-done(((f32[640,3840]{1,0:T(8,128)}), f32[160,3840]{1,0:T(8,128)}) %reduce-scatter.44.cloned.1.call-update) | async-done | bytes 2457616 | tf_op jit(solution)/shard_map/reduce_scatter | solution.py:375
  2492.9 51.4 %all-reduce.103.cloned.1.call-done = (f32[5,64,256]{2,1,0:T(8,128)}, f32[5,64,256]{2,1,0:T(8,128)}) async-done(((f32[5,64,256]{2,1,0:T(8,128)}, f32[5,64,256]{2,1,0:T(8,128)}), (f32[5,64,256]{2,1,0:T(8,128)}, f32[5,64,256]{2,1,0:T(8,128)})) %all-reduce.103.cloned.1.call-update) | async-done | bytes 655376 | tf_op jit(solution)/shard_map/psum | solution.py:351
  2544.3 65.3 %reduce-scatter.36.cloned.1.call-done = f32[160,1280]{1,0:T(8,128)} async-done(((f32[640,1280]{1,0:T(8,128)}), f32[160,1280]{1,0:T(8,128)}) %reduce-scatter.36.cloned.1.call-update) | async-done | bytes 819216 | tf_op jit(solution)/shard_map/reduce_scatter | solution.py:371
  2609.6 65.3 %reduce-scatter.38.cloned.1.call-done = f32[160,1280]{1,0:T(8,128)} async-done(((f32[640,1280]{1,0:T(8,128)}), f32[160,1280]{1,0:T(8,128)}) %reduce-scatter.38.cloned.1.call-update) | async-done | bytes 819216 | tf_op jit(solution)/shard_map/reduce_scatter | solution.py:372
  (787 shorter events, 432.5 us)
Async XLA Ops:
  7.2 45.5 %all-gather.22.cloned.1.call-start = ((), (), s32[]{:S(2)}) async-start(), calls=%async_computation.18 | async-start | bytes 2048000 | tf_op jit(solution)/shard_map/all_gather | solution.py:114
  9.4 82.4 %all-gather.24.cloned.1.call-start = ((), (), s32[]{:S(2)}) async-start(), calls=%async_computation.19 | async-start | bytes 2048000 | tf_op jit(solution)/shard_map/all_gather | solution.py:115
  10.3 92.0 %all-gather.20.cloned.1.call-start = ((), (), s32[]{:S(2)}) async-start(), calls=%async_computation.17 | async-start | bytes 1966080 | tf_op jit(solution)/shard_map/all_gather | solution.py:68
  49.1 113.5 %copy-start.112 = (bf16[1280]{0:T(1024)(128)(2,1)}, bf16[1280]{0:T(1024)(128)(2,1)S(1)}, u32[]{:S(2)}) copy-start(bf16[1280]{0:T(1024)(128)(2,1)S(1)} %get-tuple-element.350) | copy-start | bytes 7684
  51.4 166.3 %reduce-scatter.20.cloned.1.call-start = ((), (), s32[]{:S(2)}) async-start(), calls=%async_computation.20 | async-start | bytes 13107200 | tf_op jit(solution)/shard_map/reduce_scatter | solution.py:81
  112.8 239.6 %all-gather.28.cloned.1.call-start = ((), (), s32[]{:S(2)}) async-start(), calls=%async_computation.22 | async-start | bytes 2048000 | tf_op jit(solution)/shard_map/all_gather | solution.py:116
  114.7 277.9 %all-gather.26.cloned.1.call-start = ((), (), s32[]{:S(2)}) async-start(), calls=%async_computation.21 | async-start | bytes 3276800 | tf_op jit(solution)/shard_map/all_gather | solution.py:72
  114.8 109.0 %copy-start.114 = (f32[256]{0:T(256)}, f32[256]{0:T(256)S(1)}, u32[]{:S(2)}) copy-start(f32[256]{0:T(256)S(1)} %get-tuple-element.480) | copy-start | bytes 3076
  114.8 109.0 %copy-start.116 = (f32[256]{0:T(256)}, f32[256]{0:T(256)S(1)}, u32[]{:S(2)}) copy-start(f32[256]{0:T(256)S(1)} %get-tuple-element.481) | copy-start | bytes 3076
  114.8 109.0 %copy-start.118 = (f32[256]{0:T(256)}, f32[256]{0:T(256)S(1)}, u32[]{:S(2)}) copy-start(f32[256]{0:T(256)S(1)} %get-tuple-element.483) | copy-start | bytes 3076
  114.8 109.0 %copy-start.120 = (f32[256]{0:T(256)}, f32[256]{0:T(256)S(1)}, u32[]{:S(2)}) copy-start(f32[256]{0:T(256)S(1)} %get-tuple-element.484) | copy-start | bytes 3076
  114.8 119.1 %copy-start.122 = (pred[256]{0:T(512)(128)(4,1)}, pred[256]{0:T(512)(128)(4,1)S(1)}, u32[]{:S(2)}) copy-start(pred[256]{0:T(512)(128)(4,1)S(1)} %get-tuple-element.482) | copy-start | bytes 772
  145.2 82.3 %copy-start.17 = (bf16[5,256,256]{2,1,0:T(8,128)(2,1)}, bf16[5,256,256]{2,1,0:T(8,128)(2,1)S(1)}, u32[]{:S(2)}) copy-start(bf16[5,256,256]{2,1,0:T(8,128)(2,1)S(1)} %all_gather.108) | copy-start | bytes 1966084
  163.2 70.8 %copy-start.60 = (f32[1280]{0:T(1024)}, f32[1280]{0:T(1024)S(1)}, u32[]{:S(2)}) copy-start(f32[1280]{0:T(1024)S(1)} %get-tuple-element.475) | copy-start | bytes 15364
  219.1 4.7 collective-permute-start
  352.2 56.6 %reduce-scatter.22.cloned.1.call-start = ((), (), s32[]{:S(2)}) async-start(), calls=%async_computation.23 | async-start | bytes 3932160 | tf_op jit(solution)/shard_map/reduce_scatter | solution.py:92
  398.4 23.2 all-gather.40.cloned.1.call-start
  399.2 118.0 %all-gather.38.cloned.1.call-start = ((), (), s32[]{:S(2)}) async-start(), calls=%async_computation.29 | async-start | bytes 6144000 | tf_op jit(solution)/shard_map/all_gather | solution.py:119
  402.1 208.2 %all-gather.32.cloned.1.call-start = ((), (), s32[]{:S(2)}) async-start(), calls=%async_computation.25 | async-start | bytes 6144000 | tf_op jit(solution)/shard_map/all_gather | solution.py:117
  405.1 298.1 %all-gather.34.cloned.1.call-start = ((), (), s32[]{:S(2)}) async-start(), calls=%async_computation.26 | async-start | bytes 6144000 | tf_op jit(solution)/shard_map/all_gather | solution.py:118
  408.1 305.0 %all-gather.30.cloned.1.call-start = ((), (), s32[]{:S(2)}) async-start(), calls=%async_computation.24 | async-start | bytes 1966080 | tf_op jit(solution)/shard_map/all_gather | solution.py:68
  421.6 442.6 %reduce-scatter.28.cloned.1.call-start = ((), (), s32[]{:S(2)}) async-start(), calls=%async_computation.32 | async-start | bytes 19660800 | tf_op jit(solution)/shard_map/reduce_scatter | solution.py:81
  529.5 610.9 %reduce-scatter.24.cloned.1.call-start = ((), (), s32[]{:S(2)}) async-start(), calls=%async_computation.27 | async-start | bytes 39321600 | tf_op jit(solution)/shard_map/reduce_scatter | solution.py:81
  734.3 565.2 %all-gather.42.cloned.1.call-start = ((), (), s32[]{:S(2)}) async-start(), calls=%async_computation.33 | async-start | bytes 19660800 | tf_op jit(solution)/shard_map/all_gather | solution.py:72
  1150.7 234.4 %all-gather.36.cloned.1.call-start = ((), (), s32[]{:S(2)}) async-start(), calls=%async_computation.28 | async-start | bytes 9830400 | tf_op jit(solution)/shard_map/all_gather | solution.py:72
  1151.3 246.1 %reduce-scatter.30.cloned.1.call-start = ((), (), s32[]{:S(2)}) async-start(), calls=%async_computation.34 | async-start | bytes 3932160 | tf_op jit(solution)/shard_map/reduce_scatter | solution.py:92
  1317.9 93.2 %reduce-scatter.26.cloned.1.call-start = ((), (), s32[]{:S(2)}) async-start(), calls=%async_computation.30 | async-start | bytes 3932160 | tf_op jit(solution)/shard_map/reduce_scatter | solution.py:92
  1396.2 31.4 %all-gather.44.cloned.1.call-start = ((), (), s32[]{:S(2)}) async-start(), calls=%async_computation.35 | async-start | bytes 1966080 | tf_op jit(solution)/shard_map/all_gather | solution.py:68
  1416.8 79.5 %reduce-scatter.32.cloned.1.call-start = ((), (), s32[]{:S(2)}) async-start(), calls=%async_computation.36 | async-start | bytes 6553600 | tf_op jit(solution)/shard_map/reduce_scatter | solution.py:81
  1433.6 331.2 %all-gather.46.cloned.1.call-start = ((), (), s32[]{:S(2)}) async-start(), calls=%async_computation.37 | async-start | bytes 6553600 | tf_op jit(solution)/shard_map/all_gather | solution.py:72
  1445.4 50.9 %copy-start.14 = (f32[256,1280]{1,0:T(8,128)S(1)}, f32[256,1280]{1,0:T(8,128)}, u32[]{:S(2)}) copy-start(f32[256,1280]{1,0:T(8,128)} %get-tuple-element.376) | copy-start | bytes 3932164
  1694.7 5.7 collective-permute-start.1
  1701.2 63.6 %copy-start.50 = (bf16[640,2560]{1,0:T(8,128)(2,1)S(1)}, bf16[640,2560]{1,0:T(8,128)(2,1)}, u32[]{:S(2)}) copy-start(bf16[640,2560]{1,0:T(8,128)(2,1)} %constant_dynamic-update-slice_fusion) | copy-start | bytes 9830404
  1702.4 81.0 %reduce-scatter.34.cloned.1.call-start = ((), (), s32[]{:S(2)}) async-start(), calls=%async_computation.38 | async-start | bytes 3932160 | tf_op jit(solution)/shard_map/reduce_scatter | solution.py:92
  1773.0 65.8 %reduce-scatter.48.cloned.1.call-start = ((), (), s32[]{:S(2)}) async-start(), calls=%async_computation.45 | async-start | bytes 1638400 | tf_op jit(solution)/shard_map/reduce_scatter | solution.py:377
  1775.7 75.4 %reduce-scatter.50.cloned.1.call-start = ((), (), s32[]{:S(2)}) async-start(), calls=%async_computation.46 | async-start | bytes 1638400 | tf_op jit(solution)/shard_map/reduce_scatter | solution.py:378
  1778.3 96.2 %reduce-scatter.52.cloned.1.call-start = ((), (), s32[]{:S(2)}) async-start(), calls=%async_computation.47 | async-start | bytes 819200
  1780.2 134.2 %all-reduce.105.cloned.1.call-start = ((), (), s32[]{:S(2)}) async-start(), calls=%async_computation.49 | async-start | bytes 196608
  1785.8 298.8 %reduce-scatter.46.cloned.1.call-start = ((), (), s32[]{:S(2)}) async-start(), calls=%async_computation.44 | async-start | bytes 12288000 | tf_op jit(solution)/shard_map/reduce_scatter | solution.py:376
  1797.1 353.8 %reduce-scatter.40.cloned.1.call-start = ((), (), s32[]{:S(2)}) async-start(), calls=%async_computation.41 | async-start | bytes 4096000 | tf_op jit(solution)/shard_map/reduce_scatter | solution.py:373
  1804.2 517.5 %reduce-scatter.42.cloned.1.call-start = ((), (), s32[]{:S(2)}) async-start(), calls=%async_computation.42 | async-start | bytes 12288000 | tf_op jit(solution)/shard_map/reduce_scatter | solution.py:374
  1838.2 654.7 %reduce-scatter.44.cloned.1.call-start = ((), (), s32[]{:S(2)}) async-start(), calls=%async_computation.43 | async-start | bytes 12288000 | tf_op jit(solution)/shard_map/reduce_scatter | solution.py:375
  1838.8 705.5 %all-reduce.103.cloned.1.call-start = ((), (), s32[]{:S(2)}) async-start(), calls=%async_computation.48 | async-start | bytes 1310720 | tf_op jit(solution)/shard_map/psum | solution.py:351
  1851.1 758.5 %reduce-scatter.36.cloned.1.call-start = ((), (), s32[]{:S(2)}) async-start(), calls=%async_computation.39 | async-start | bytes 4096000 | tf_op jit(solution)/shard_map/reduce_scatter | solution.py:371
  1860.3 814.6 %reduce-scatter.38.cloned.1.call-start = ((), (), s32[]{:S(2)}) async-start(), calls=%async_computation.40 | async-start | bytes 4096000 | tf_op jit(solution)/shard_map/reduce_scatter | solution.py:372
  1860.4 83.1 %copy-start.13 = (f32[512,640]{1,0:T(8,128)S(1)}, f32[512,640]{1,0:T(8,128)}, u32[]{:S(2)}) copy-start(f32[512,640]{1,0:T(8,128)} %copy-done.12) | copy-start | bytes 3932164
  1860.4 83.1 %copy-start.30 = (f32[512,640]{1,0:T(8,128)S(1)}, f32[512,640]{1,0:T(8,128)}, u32[]{:S(2)}) copy-start(f32[512,640]{1,0:T(8,128)} %reduce-scatter.34.cloned.1.call-done) | copy-start | bytes 3932164
  1860.4 83.1 %copy-start.124 = (f32[512]{0:T(512)S(1)}, f32[512]{0:T(512)}, u32[]{:S(2)}) copy-start(f32[512]{0:T(512)} %get-tuple-element.476) | copy-start | bytes 6148
  (134 other events, 672.4 us)
Sparse Core Ops, SparseCore 0:
  10.2 42.4 all-gather.21
  54.8 37.0 all-gather.23
  94.0 8.2 all-gather.19
  112.9 104.7 reduce-scatter.19
  219.1 38.1 all-gather.27
  352.3 40.2 all-gather.25
  398.6 10.1 reduce-scatter.21
  410.4 10.6 all-gather.39
  423.3 93.8 all-gather.37
  519.2 91.0 all-gather.31
  612.0 91.0 all-gather.33
  705.2 7.8 all-gather.29
  716.5 147.6 reduce-scatter.27
  867.4 272.9 reduce-scatter.23
  1150.9 148.6 all-gather.41
  1301.8 83.2 all-gather.35
  1387.2 10.1 reduce-scatter.29
  1399.6 11.4 reduce-scatter.25
  1416.9 10.6 all-gather.43
  1433.7 62.5 reduce-scatter.31
  1702.5 62.2 all-gather.45
  1773.1 10.1 reduce-scatter.33
  1786.3 32.4 reduce-scatter.47
  1821.1 29.9 reduce-scatter.49
  1853.5 20.9 reduce-scatter.51
  1879.2 35.1 all-reduce.104
  1917.2 167.3 reduce-scatter.45
  2087.6 63.2 reduce-scatter.39
  2154.0 167.6 reduce-scatter.41
  2324.4 168.4 reduce-scatter.43
  2496.2 48.0 all-reduce.102
  2547.3 62.2 reduce-scatter.35
  2612.5 62.3 reduce-scatter.37
where the time goes:
time: 2700 us; the launch traced here: 2690 us
  waiting for transfers between devices  1950 us (72%)
  local copies, waits for them, and re-layouts  284 us (11%)
  blocking collectives  153 us (6%)
  matrix products  144 us (5%)
  other arithmetic  126 us (5%)
    reduce_scatter x4, waiting for transfers between devices, reduce_row(): lax.psum_scatter(term(jnp.int32(0), lax.axis_size('row') * rows_here), 'r...  501 us
    all_gather x4, waiting for transfers between devices, spread_row(): return lax.all_gather(values, 'row', axis=0, tiled=True)  318 us
    reduce_scatter x1, waiting for transfers between devices, shards(): lax.psum_scatter(gate_up_grad[:, hidden_width:], 'dp', scatter_dimension=...  171 us
    reduce_scatter x1, waiting for transfers between devices, shards(): lax.psum_scatter(gate_up_grad[:, :hidden_width], 'dp', scatter_dimension=...  171 us
    reduce_scatter x1, waiting for transfers between devices, shards(): lax.psum_scatter(down_grad, 'dp', scatter_dimension=0, tiled=True)  140 us
    slice x57, local copies, waits for them, and re-layouts, shards(): lax.associative_scan(combine, (next_decay, grad_direct), reverse=True, ax...  99.7 us
    all_gather x1, waiting for transfers between devices, fetch_first(): lax.all_gather(copies[5], 'dp', axis=0, tiled=True)  95.5 us
    all_gather x1, waiting for transfers between devices, fetch_first(): lax.all_gather(copies[4], 'dp', axis=0, tiled=True)  87.8 us
  transfers between devices with their start and end apart: 35, of which 32 were waited for; matrix products, arithmetic and copies ran while one was open for 12% of the time, Pallas kernels for 0%

commit v1 on v0

v1 whole, which is shorter than its diff:
```python
import functools

import jax
import jax.numpy as jnp
from jax import lax
from jax.experimental import pallas as pl
from jax.experimental.pallas import tpu as pltpu
from jax.sharding import PartitionSpec as P

D = 2560
epsilon = 1e-06
LOW = jnp.bfloat16
WIDE = jnp.float32


def flip(values, offset):
    count = lax.axis_size("row")
    return lax.ppermute(values, "row", [(i, i ^ offset) for i in range(count)])


def swap(values):
    return lax.ppermute(values, "col", [(0, 1), (1, 0)])


def gather_rows(block):
    half = block.shape[0] // 2
    first, second = block[:half], block[half:]
    first_1 = flip(first, 1)
    second_2 = flip(second, 2)
    second_1 = flip(second, 1)
    first_2 = flip(first, 2)
    first_3 = flip(first_1, 2)
    second_3 = flip(second_2, 1)
    return [
        block,
        jnp.concatenate((first_1, second_1), axis=0),
        jnp.concatenate((first_2, second_2), axis=0),
        jnp.concatenate((first_3, second_3), axis=0),
    ]


def scatter_rows(blocks):
    half = blocks[0].shape[0] // 2
    first = [block[:half] for block in blocks]
    second = [block[half:] for block in blocks]
    first_2 = flip(first[2].astype(LOW), 2)
    first_3 = flip(first[3].astype(LOW), 2)
    second_1 = flip(second[1].astype(LOW), 1)
    second_3 = flip(second[3].astype(LOW), 1)
    first_far = flip((first[1] + first_3.astype(WIDE)).astype(LOW), 1)
    second_far = flip((second[2] + second_3.astype(WIDE)).astype(LOW), 2)
    return jnp.concatenate(
        (
            first[0] + first_2.astype(WIDE) + first_far.astype(WIDE),
            second[0] + second_1.astype(WIDE) + second_far.astype(WIDE),
        ),
        axis=0,
    )


def exchange_rows(blocks):
    return [blocks[0]] + [flip(blocks[k], k) for k in range(1, len(blocks))]


def step_up(values, first, last):
    count = lax.axis_size("dp")
    return lax.ppermute(values, "dp", [(i, i + 1) for i in range(count - 1) if first <= i <= last])


def step_down(values, first, last):
    count = lax.axis_size("dp")
    pairs = [(count - 1 - i, count - 2 - i) for i in range(count - 1) if first <= i <= last]
    return lax.ppermute(values, "dp", pairs)


def gather_line(block):
    count, place = lax.axis_size("dp"), lax.axis_index("dp")
    up, down = [block], [block]
    for step in range(1, count):
        up.append(step_up(up[-1], step - 1, count))
        down.append(step_down(down[-1], step - 1, count))
    return [block] + [jnp.where(place >= s, up[s], down[count - s]) for s in range(1, count)]


def scatter_line(blocks):
    count = lax.axis_size("dp")
    up, down = None, None
    for step in range(1, count):
        rising, falling = blocks[step], blocks[count - step]
        if up is not None:
            rising, falling = rising + up.astype(WIDE), falling + down.astype(WIDE)
        up = step_up(rising.astype(LOW), 0, step - 1)
        down = step_down(falling.astype(LOW), 0, step - 1)
    return blocks[0] + up.astype(WIDE) + down.astype(WIDE)


def turned(step):
    count = lax.axis_size("dp")
    return lax.rem(lax.axis_index("dp") + count - step, count)


def in_order(blocks, axis):
    size = blocks[0].shape[axis]
    shape = list(blocks[0].shape)
    shape[axis] = size * len(blocks)
    whole = jnp.zeros(shape, blocks[0].dtype)
    for s, block in enumerate(blocks):
        whole = lax.dynamic_update_slice_in_dim(whole, block, turned(s) * size, axis)
    return whole


def cut(whole, axis):
    count = lax.axis_size("dp")
    size = whole.shape[axis] // count
    return [lax.dynamic_slice_in_dim(whole, turned(s) * size, size, axis) for s in range(count)]


def exchange_line(blocks):
    count = lax.axis_size("dp")
    arrived = [blocks[0]] + [None] * (count - 1)
    for s in range(1, count):
        moved = lax.ppermute(blocks[s], "dp", [(i, (i + count - s) % count) for i in range(count)])
        arrived[count - s] = moved
    return arrived


def rows_in_order(blocks, axis):
    place = lax.axis_index("row")
    size = blocks[0].shape[axis]
    shape = list(blocks[0].shape)
    shape[axis] = size * len(blocks)
    whole = jnp.zeros(shape, blocks[0].dtype)
    for k, block in enumerate(blocks):
        whole = lax.dynamic_update_slice_in_dim(whole, block, (place ^ k) * size, axis)
    return whole


def rows_cut(whole, axis):
    count, place = lax.axis_size("row"), lax.axis_index("row")
    size = whole.shape[axis] // count
    return [
        lax.dynamic_slice_in_dim(whole, (place ^ k) * size, size, axis) for k in range(count)
    ]


def gather_cols(block):
    other = swap(block)
    first = lax.axis_index("col") == 0
    return jnp.concatenate(
        (jnp.where(first, block, other), jnp.where(first, other, block)), axis=0
    )


def scatter_cols(whole, kind):
    half = whole.shape[0] // 2
    place = lax.axis_index("col")
    mine = lax.dynamic_slice_in_dim(whole, place * half, half, 0)
    theirs = lax.dynamic_slice_in_dim(whole, (1 - place) * half, half, 0)
    return mine + swap(theirs.astype(kind)).astype(WIDE)


def shifted(shard, axis, by):
    count = lax.axis_size(axis)
    pairs = [(i, i + by) for i in range(count) if 0 <= i + by < count]
    return lax.ppermute(shard, axis, pairs)


def entering(shard, combine, identity, reverse):
    count, place = lax.axis_size("row"), lax.axis_index("row")
    decay, value = shard
    packed = jnp.stack((decay, value))
    everything = [packed] + [flip(packed, k) for k in range(1, count)]
    table = jnp.stack(everything)
    before = identity
    for k in range(count):
        at = count - 1 - k if reverse else k
        reached = at > place if reverse else at < place
        entry = lax.dynamic_index_in_dim(table, place ^ at, 0, keepdims=False)
        new = combine(before, (entry[0], entry[1]))
        before = tuple(jnp.where(reached, a, b) for a, b in zip(new, before))
    return before


def combine(earlier, later):
    return (earlier[0] * later[0], later[0] * earlier[1] + later[1])


def scan_rows(decay, value, reverse):
    count = decay.shape[0]
    rows = lax.broadcasted_iota(jnp.int32, decay.shape, 0)
    reach = 1
    while reach < count:
        turn = count - reach if reverse else reach
        inside = rows < count - reach if reverse else rows >= reach
        decay_far = jnp.where(inside, pltpu.roll(decay, turn, 0), 1.0)
        value_far = jnp.where(inside, pltpu.roll(value, turn, 0), 0.0)
        value = decay * value_far + value
        decay = decay * decay_far
        reach *= 2
    return decay, value


def minus_expm1(v):
    series = 1.0 + v / 9.0
    for k in range(8, 1, -1):
        series = 1.0 + (v / k) * series
    return jnp.where(v > -0.5, -v * series, 1.0 - jnp.exp(v))


def recurrence_forward(
    taps_count, proj, halo, spots, vectors, input_full, decay_full, conv_out, in_out, dec_out,
    running_out, local_out, padded,
):
    count = proj.shape[0]
    conv_shift, branch_shift, _, input_shift, decay_shift, rate = (
        vectors[taps_count + i : taps_count + i + 1, :] for i in range(6)
    )
    padded[8 - halo.shape[0] : 8, :] = halo[...] + branch_shift
    padded[8 : 8 + count, :] = proj[...] + branch_shift
    spot = spots[...]
    conv = conv_shift + vectors[0:1, :] * padded[8 : 8 + count, :]
    for k in range(1, taps_count):
        earlier = padded[8 - k : 8 - k + count, :]
        conv = conv + vectors[k : k + 1, :] * jnp.where(spot >= k, earlier, 0.0)
    conv_out[...] = conv
    low = conv.astype(LOW)
    input_gate = jax.nn.sigmoid(
        jnp.dot(low, input_full[0], preferred_element_type=WIDE) + input_shift
    )
    decay_gate = jax.nn.sigmoid(
        jnp.dot(low, decay_full[0], preferred_element_type=WIDE) + decay_shift
    )
    in_out[...] = input_gate
    dec_out[...] = decay_gate
    log_decay = rate * decay_gate
    starting = spot == 0
    decay = jnp.where(starting, 0.0, jnp.exp(log_decay))
    multiplier = jnp.where(starting, 1.0, jnp.sqrt(minus_expm1(2.0 * log_decay)))
    running, local = scan_rows(decay, multiplier * input_gate * conv, False)
    running_out[...] = running
    local_out[...] = local


def recurrence_turn(dec_gate, spots, rate, grad_direct, reach_out, local_out, first_out, padded):
    count = dec_gate.shape[0]
    decay = jnp.where(spots[...] == 0, 0.0, jnp.exp(rate[...] * dec_gate[...]))
    padded[0:count, :] = decay
    padded[count : count + 8, :] = jnp.ones((8, decay.shape[1]), WIDE)
    following = padded[1 : count + 1, :]
    reach, local = scan_rows(following, grad_direct[...], True)
    reach_out[...] = reach
    local_out[...] = local
    first_out[0:1, :] = decay[0:1, :] * reach[0:1, :]
    first_out[1:2, :] = decay[0:1, :] * local[0:1, :]


def recurrence_backward(
    taps_count, proj, halo, spots, vectors, input_full, decay_full, conv_in, in_gate, dec_gate,
    running, local, state_in, reach, local_grad, carry, branch_out, head_out, sums_out, in_grad_out,
    dec_grad_out, padded, spread,
):
    count, width = proj.shape
    branch_shift, rate = vectors[taps_count + 1 : taps_count + 2, :], vectors[taps_count + 5 :, :]
    spot = spots[...]
    entering_state = state_in[...]
    grad_state = local_grad[...] + reach[...] * carry[...]
    state = local[...] + running[...] * entering_state
    padded[8:, :] = state
    padded[7:8, :] = entering_state
    grad_decay = grad_state * padded[7 : 7 + count, :]
    input_gate, decay_gate, conv = in_gate[...], dec_gate[...], conv_in[...]
    starting = spot == 0
    log_decay = rate * decay_gate
    decay = jnp.exp(log_decay)
    multiplier = jnp.where(starting, 1.0, jnp.sqrt(minus_expm1(2.0 * log_decay)))
    grad_gated = grad_state * conv
    grad_log = jnp.where(
        starting, 0.0, decay * (grad_decay - grad_gated * input_gate * (decay / multiplier))
    )
    grad_in = grad_gated * multiplier * (input_gate * (1.0 - input_gate))
    grad_gate = grad_log * decay_gate
    grad_dec = grad_gate * rate * (1.0 - decay_gate)
    low = conv.astype(LOW)
    low_in, low_dec = grad_in.astype(LOW), grad_dec.astype(LOW)
    across = (((1,), (1,)), ((), ()))
    along = (((0,), (0,)), ((), ()))
    grad_conv = (
        grad_state * multiplier * input_gate
        + lax.dot_general(low_in, input_full[0], across, preferred_element_type=WIDE)
        + lax.dot_general(low_dec, decay_full[0], across, preferred_element_type=WIDE)
    )
    in_grad_out[0] = lax.dot_general(low, low_in, along, preferred_element_type=WIDE)
    dec_grad_out[0] = lax.dot_general(low, low_dec, along, preferred_element_type=WIDE)
    padded[8 - halo.shape[0] : 8, :] = halo[...] + branch_shift
    padded[8:, :] = proj[...] + branch_shift
    spread[0:8, :] = jnp.zeros((8, width), WIDE)
    spread[8:, :] = vectors[0:1, :] * grad_conv
    sums_out[0:1, :] = jnp.sum(grad_conv * padded[8:, :], axis=0, keepdims=True)
    for k in range(1, taps_count):
        kept = jnp.where(spot >= k, grad_conv, 0.0)
        sums_out[k : k + 1, :] = jnp.sum(
            kept * padded[8 - k : 8 - k + count, :], axis=0, keepdims=True
        )
        spread[8 - k : 8 - k + count, :] += vectors[k : k + 1, :] * kept
    branch = spread[8:, :]
    branch_out[...] = branch
    head = spread[0:8, :]
    head_out[...] = head
    sums_out[taps_count : taps_count + 1, :] = jnp.sum(grad_conv, axis=0, keepdims=True)
    sums_out[taps_count + 1 : taps_count + 2, :] = jnp.sum(
        branch, axis=0, keepdims=True
    ) + jnp.sum(head, axis=0, keepdims=True)
    sums_out[taps_count + 2 : taps_count + 3, :] = jnp.sum(grad_in, axis=0, keepdims=True)
    sums_out[taps_count + 3 : taps_count + 4, :] = jnp.sum(grad_dec, axis=0, keepdims=True)
    sums_out[taps_count + 4 : taps_count + 5, :] = jnp.sum(grad_gate, axis=0, keepdims=True)


def by_head(rows, width):
    return pl.BlockSpec((rows, width), lambda h: (0, h))


def by_block(width):
    return pl.BlockSpec((1, width, width), lambda h: (h, 0, 0))


def whole_column(rows):
    return pl.BlockSpec((rows, 1), lambda h: (0, 0))


def wide_shape(*shape):
    return jax.ShapeDtypeStruct(shape, WIDE)


kernel_params = pltpu.CompilerParams(vmem_limit_bytes=40 * 1024 * 1024)


def times(piece, matrix):
    return jnp.dot(piece, matrix, preferred_element_type=WIDE)


def times_flipped(piece, matrix):
    return lax.dot_general(piece, matrix, (((1,), (1,)), ((), ())), preferred_element_type=WIDE)


def left_product(left, right):
    return lax.dot_general(left, right, (((0,), (0,)), ((), ())), preferred_element_type=WIDE)


def shards(
    inputs,
    positions,
    branch_matrix,
    gelu_matrix,
    output_matrix,
    gate_matrix,
    up_matrix,
    down_matrix,
    input_blocks,
    decay_blocks,
    conv_taps,
    conv_bias,
    branch_bias,
    gelu_bias,
    input_bias,
    decay_bias,
    decay_param,
    output_bias,
    gate_bias,
    up_bias,
    down_bias,
    norm_first,
    norm_second,
    cotangent,
):
    count_dp, count_row = lax.axis_size("dp"), lax.axis_size("row")
    place_dp, place_row = lax.axis_index("dp"), lax.axis_index("row")
    width = branch_matrix.shape[1]
    hidden_part = down_matrix.shape[0]
    block_width = input_blocks.shape[2]
    heads_here = input_blocks.shape[0]
    conv_width = conv_taps.shape[0]

    channel_pack = jnp.concatenate(
        (
            conv_taps,
            jnp.stack((conv_bias, branch_bias, gelu_bias, input_bias, decay_bias, decay_param)),
        ),
        axis=0,
    ).astype(LOW)
    channel_vectors = (
        lax.all_gather(channel_pack, "dp", axis=0)
        .transpose(1, 0, 2)
        .reshape(channel_pack.shape[0], width)
        .astype(WIDE)
    )
    gelu_shift, decay_raw = channel_vectors[conv_width + 2], channel_vectors[-1]
    width_pack = jnp.stack((norm_first, output_bias, down_bias, norm_second)).astype(LOW)
    width_here = (
        lax.all_gather(width_pack, "dp", axis=0)
        .transpose(1, 0, 2)
        .reshape(width_pack.shape[0], width_pack.shape[1] * count_dp)
    )
    width_all = jnp.concatenate(
        [width_here] + [flip(width_here, k) for k in range(1, count_row)], axis=1
    ).astype(WIDE)
    gain_first = width_here[0].astype(WIDE)
    output_shift, down_shift, gain_second = width_all[1], width_all[2], width_all[3]

    resid = inputs.astype(WIDE)
    total_first = lax.psum(jnp.sum(resid * resid, axis=1), "row")
    inverse_first = lax.rsqrt(total_first / D + epsilon)[:, None]
    normed_first = (resid * inverse_first * (1.0 + gain_first)).astype(LOW)
    normed_first_all = gather_cols(normed_first)

    branch_full = in_order(gather_line(branch_matrix.astype(LOW)), 0)
    gelu_full = in_order(gather_line(gelu_matrix.astype(LOW)), 0)
    branch = scatter_rows(rows_cut(times(normed_first_all, branch_full), 0))
    gelu_in = scatter_rows(rows_cut(times(normed_first_all, gelu_full), 0)) + gelu_shift
    side, gelu_pull = jax.vjp(jax.nn.gelu, gelu_in)

    block_pack = jnp.concatenate((input_blocks, decay_blocks), axis=0).astype(LOW)
    block_count, block_part = block_pack.shape[0], block_pack.shape[1]
    share = block_part // count_row
    own_share = lax.dynamic_slice_in_dim(block_pack, place_row * share, share, 1)
    line_shares = jnp.concatenate(
        gather_line(own_share.reshape(block_count * share, block_width)), axis=0
    )
    blocks_full = jnp.zeros((block_count, block_width, block_width), LOW)
    for k, arrived in enumerate(gather_rows(line_shares)):
        for s in range(count_dp):
            piece = arrived[s * block_count * share : (s + 1) * block_count * share]
            blocks_full = lax.dynamic_update_slice_in_dim(
                blocks_full,
                piece.reshape(block_count, share, block_width),
                turned(s) * block_part + (place_row ^ k) * share,
                1,
            )
    input_full, decay_full = blocks_full[:heads_here], blocks_full[heads_here:]

    def hidden_columns(matrix):
        part = in_order(exchange_line(cut(matrix.astype(LOW), 1)), 0)
        return jnp.concatenate(gather_rows(part), axis=0)

    gate_full = hidden_columns(gate_matrix)
    up_full = hidden_columns(up_matrix)
    down_full = jnp.concatenate(gather_rows(down_matrix.astype(LOW)), axis=1)
    output_full = in_order(gather_line(output_matrix.astype(LOW)), 0)

    cot_own = jnp.concatenate(exchange_rows(rows_cut(cotangent, 0)), axis=1)
    cot_line = gather_line(cot_own)

    def both_cores(line):
        stacked = jnp.concatenate(line, axis=0)
        return gather_cols(stacked)

    cot_all = both_cores(cot_line)

    steps_count = branch.shape[0]
    spots = positions[:, None]
    lower = shifted(branch[steps_count - conv_width + 1 :], "row", 1)
    rate = -8.0 * jax.nn.softplus(decay_raw)
    vectors = jnp.concatenate((channel_vectors[:-1], rate[None, :]), axis=0)
    grid = (heads_here,)
    head_rows = by_head(steps_count, block_width)
    vector_rows = by_head(vectors.shape[0], block_width)
    halo_rows = by_head(conv_width - 1, block_width)
    one_row = by_head(1, block_width)
    tokens_shape = wide_shape(steps_count, width)
    conv, input_gate, decay_gate, running, local_state = pl.pallas_call(
        functools.partial(recurrence_forward, conv_width),
        grid=grid,
        in_specs=[
            head_rows, halo_rows, whole_column(steps_count), vector_rows, by_block(block_width),
            by_block(block_width),
        ],
        out_specs=[head_rows] * 5,
        out_shape=[tokens_shape] * 5,
        scratch_shapes=[pltpu.VMEM((8 + steps_count, block_width), WIDE)],
        compiler_params=kernel_params,
        name="recurrence_forward",
    )(branch, lower, spots, vectors, input_full, decay_full)
    ones_row = jnp.ones((width,), WIDE)
    zeros_row = jnp.zeros((width,), WIDE)
    carried = entering((running[-1], local_state[-1]), combine, (ones_row, zeros_row), False)
    state_in = carried[1][None, :]
    state = local_state + running * state_in
    mixed = (state * side).astype(LOW)
    mixed_all = rows_in_order(gather_rows(mixed), 0)

    delta = scatter_cols(times(mixed_all, output_full), WIDE)
    middle = jnp.concatenate(exchange_rows(rows_cut(resid + delta, 0)), axis=1) + output_shift
    inverse_second = lax.rsqrt(jnp.mean(middle * middle, axis=1, keepdims=True) + epsilon)
    normed_second = (middle * inverse_second * (1.0 + gain_second)).astype(LOW)
    normed_second_all = both_cores(gather_line(normed_second))

    def feed(gate_value, up_value):
        return jax.nn.gelu(gate_value) * up_value

    hidden_value, feed_pull = jax.vjp(
        feed,
        times(normed_second_all, gate_full) + gate_bias.astype(LOW).astype(WIDE),
        times(normed_second_all, up_full) + up_bias.astype(LOW).astype(WIDE),
    )
    hidden = hidden_value.astype(LOW)
    grad_hidden = times_flipped(cot_all, down_full)
    grad_gate, grad_up = feed_pull(grad_hidden)
    grad_gate_low, grad_up_low = grad_gate.astype(LOW), grad_up.astype(LOW)

    def to_owner(partial):
        own = scatter_cols(partial, LOW)
        size = own.shape[0] // count_dp
        return scatter_line([own[s * size : (s + 1) * size] for s in range(count_dp)])

    grad_normed_second = to_owner(
        times_flipped(grad_gate_low, gate_full) + times_flipped(grad_up_low, up_full)
    )
    forward_sum = to_owner(times(hidden, down_full))
    layer_low = (middle + forward_sum + down_shift).astype(LOW)
    size = layer_low.shape[1] // count_row
    layer_out = rows_in_order(
        exchange_rows([layer_low[:, k * size : (k + 1) * size] for k in range(count_row)]), 0
    )

    def row_blocks(partial):
        size = partial.shape[0] // count_row
        return [partial[k * size : (k + 1) * size] for k in range(count_row)]

    down_partial = left_product(hidden, cot_all)
    down_grad = scatter_rows(
        [down_partial[:, k * size : (k + 1) * size] for k in range(count_row)]
    )

    def to_columns(partial):
        own = scatter_rows(row_blocks(partial)).astype(LOW)
        return in_order(exchange_line(cut(own, 0)), 1).astype(WIDE)

    gate_grad = to_columns(left_product(normed_second_all, grad_gate_low))
    up_grad = to_columns(left_product(normed_second_all, grad_up_low))
    hidden_sums = lax.psum(jnp.stack((jnp.sum(grad_gate, axis=0), jnp.sum(grad_up, axis=0))), "row")

    scaled = grad_normed_second * (1.0 + gain_second)
    inner = jnp.sum(scaled * middle, axis=1, keepdims=True)
    back_second = inverse_second * scaled - middle * inverse_second**3 * inner / D
    norm_second_sum = jnp.sum(grad_normed_second * middle * inverse_second, axis=0)
    grad_middle = cot_own.astype(WIDE) + back_second
    output_bias_sum = jnp.sum(grad_middle, axis=0)
    grad_middle_here = rows_in_order(
        exchange_rows([grad_middle[:, k * size : (k + 1) * size] for k in range(count_row)]), 0
    )
    grad_middle_all = gather_cols(grad_middle_here.astype(LOW))
    output_grad = scatter_line(cut(left_product(mixed_all, grad_middle_all), 0))
    grad_mixed = scatter_rows(rows_cut(times_flipped(grad_middle_all, output_full), 0))

    grad_direct = grad_mixed * side
    grad_side = grad_mixed * state
    reach, local_grad, first_row = pl.pallas_call(
        recurrence_turn,
        grid=grid,
        in_specs=[head_rows, whole_column(steps_count), one_row, head_rows],
        out_specs=[head_rows, head_rows, by_head(2, block_width)],
        out_shape=[tokens_shape, tokens_shape, wide_shape(2, width)],
        scratch_shapes=[pltpu.VMEM((steps_count + 8, block_width), WIDE)],
        compiler_params=kernel_params,
        name="recurrence_turn",
    )(decay_gate, spots, rate[None, :], grad_direct)
    later_carry = entering((first_row[0], first_row[1]), combine, (ones_row, zeros_row), True)
    grad_branch, head_rows_out, channel_part, input_blocks_grad, decay_blocks_grad = pl.pallas_call(
        functools.partial(recurrence_backward, conv_width),
        grid=grid,
        in_specs=[
            head_rows, halo_rows, whole_column(steps_count), vector_rows, by_block(block_width),
            by_block(block_width), head_rows, head_rows, head_rows, head_rows, head_rows, one_row,
            head_rows, head_rows, one_row,
        ],
        out_specs=[
            head_rows, by_head(8, block_width), by_head(conv_width + 5, block_width),
            by_block(block_width), by_block(block_width),
        ],
        out_shape=[
            tokens_shape, wide_shape(8, width), wide_shape(conv_width + 5, width),
            wide_shape(heads_here, block_width, block_width),
            wide_shape(heads_here, block_width, block_width),
        ],
        scratch_shapes=[pltpu.VMEM((8 + steps_count, block_width), WIDE)] * 2,
        compiler_params=kernel_params,
        name="recurrence_backward",
    )(
        branch, lower, spots, vectors, input_full, decay_full, conv, input_gate, decay_gate,
        running, local_state, state_in, reach, local_grad, later_carry[1][None, :],
    )
    upper = shifted(head_rows_out[8 - conv_width + 1 :], "row", -1)
    grad_branch = grad_branch + jnp.concatenate(
        (jnp.zeros((steps_count - conv_width + 1, width), WIDE), upper), axis=0
    )
    grad_gelu_in = lax.optimization_barrier(gelu_pull(grad_side)[0])
    gelu_bias_grad = jnp.sum(grad_gelu_in, axis=0)

    grad_gelu_all = rows_in_order(gather_rows(grad_gelu_in.astype(LOW)), 0)
    gelu_grad = scatter_line(cut(left_product(normed_first_all, grad_gelu_all), 0))
    grad_branch_all = rows_in_order(gather_rows(grad_branch.astype(LOW)), 0)
    branch_grad = scatter_line(cut(left_product(normed_first_all, grad_branch_all), 0))

    block_sums = jnp.concatenate((input_blocks_grad, decay_blocks_grad), axis=0)

    def share_sums(s, k):
        at = turned(s) * block_part + (place_row ^ k) * share
        piece = lax.dynamic_slice_in_dim(block_sums, at, share, 1)
        return piece.reshape(block_count * share, block_width)

    share_total = scatter_rows(
        [
            jnp.concatenate([share_sums(s, k) for s in range(count_dp)], axis=0)
            for k in range(count_row)
        ]
    )
    length = block_count * share
    share_total = scatter_line(
        [share_total[s * length : (s + 1) * length] for s in range(count_dp)]
    )
    block_grads = rows_in_order(
        [
            piece.reshape(block_count, share, block_width)
            for piece in gather_rows(share_total.astype(LOW))
        ],
        1,
    ).astype(WIDE)

    grad_normed_first = scatter_cols(
        times_flipped(grad_branch_all, branch_full) + times_flipped(grad_gelu_all, gelu_full), WIDE
    )
    scaled = grad_normed_first * (1.0 + gain_first)
    inner = lax.psum(jnp.sum(scaled * resid, axis=1), "row")[:, None]
    back_first = inverse_first * scaled - resid * inverse_first**3 * inner / D
    norm_first_sum = jnp.sum(grad_normed_first * resid * inverse_first, axis=0)
    input_grad = grad_middle_here + back_first

    conv_bias_grad, branch_bias_grad, input_bias_grad, decay_bias_grad, rate_grad = channel_part[
        conv_width:
    ]
    decay_param_grad = -8.0 * rate_grad * jax.nn.sigmoid(decay_raw)
    channel_sums = lax.psum(
        jnp.concatenate(
            (
                channel_part[:conv_width],
                jnp.stack(
                    (
                        conv_bias_grad,
                        branch_bias_grad,
                        gelu_bias_grad,
                        input_bias_grad,
                        decay_bias_grad,
                        decay_param_grad,
                    )
                ),
            ),
            axis=0,
        ),
        ("row", "dp"),
    )
    channel_size = width // count_dp
    channel_sums = lax.dynamic_slice_in_dim(channel_sums, place_dp * channel_size, channel_size, 1)
    wide_sums = jnp.stack((output_bias_sum, norm_second_sum))
    wide_parts = exchange_rows([wide_sums[:, k * size : (k + 1) * size] for k in range(count_row)])
    width_sums = lax.psum(
        jnp.concatenate(
            (
                sum(wide_parts),
                jnp.stack((jnp.sum(cotangent.astype(WIDE), axis=0), norm_first_sum)),
            ),
            axis=0,
        ),
        ("dp", "col"),
    )
    width_size = width_sums.shape[1] // count_dp
    width_sums = lax.dynamic_slice_in_dim(width_sums, place_dp * width_size, width_size, 1)

    return (
        layer_out,
        input_grad,
        branch_grad,
        gelu_grad,
        output_grad,
        gate_grad,
        up_grad,
        down_grad,
        block_grads[:heads_here],
        block_grads[heads_here:],
        channel_sums[:conv_width],
        channel_sums[conv_width],
        channel_sums[conv_width + 1],
        channel_sums[conv_width + 2],
        channel_sums[conv_width + 3],
        channel_sums[conv_width + 4],
        channel_sums[conv_width + 5],
        width_sums[0],
        hidden_sums[0],
        hidden_sums[1],
        width_sums[2],
        width_sums[3],
        width_sums[1],
    )


def solution(mesh):
    in_specs = (
        P(("dp", "col"), "row"),
        P(("dp", "row")),
        P(("row", "dp"), "col"),
        P(("row", "dp"), "col"),
        P(("col", "dp"), "row"),
        P(("row", "dp"), "col"),
        P(("row", "dp"), "col"),
        P(("col", "dp"), "row"),
        P("col", "dp", None),
        P("col", "dp", None),
        P(None, ("col", "dp")),
        P(("col", "dp")),
        P(("col", "dp")),
        P(("col", "dp")),
        P(("col", "dp")),
        P(("col", "dp")),
        P(("col", "dp")),
        P(("row", "dp")),
        P(("col", "dp")),
        P(("col", "dp")),
        P(("row", "dp")),
        P(("row", "dp")),
        P(("row", "dp")),
        P(("dp", "col"), "row"),
    )
    out_specs = (
        P(("dp", "col"), "row"),
        P(("dp", "col"), "row"),
        P(("row", "dp"), "col"),
        P(("row", "dp"), "col"),
        P(("col", "dp"), "row"),
        P(("row", "dp"), "col"),
        P(("row", "dp"), "col"),
        P(("col", "dp"), "row"),
        P("col", "dp", None),
        P("col", "dp", None),
        P(None, ("col", "dp")),
        P(("col", "dp")),
        P(("col", "dp")),
        P(("col", "dp")),
        P(("col", "dp")),
        P(("col", "dp")),
        P(("col", "dp")),
        P(("row", "dp")),
        P(("col", "dp")),
        P(("col", "dp")),
        P(("row", "dp")),
        P(("row", "dp")),
        P(("row", "dp")),
    )
    return jax.shard_map(shards, mesh=mesh, in_specs=in_specs, out_specs=out_specs, check_vma=False)
```

time: 2700 us -> 1410 us (0.52)
  waiting for transfers between devices: 1950 us -> 432 us
  starting transfers between devices: 7.39 us -> 373 us
  local copies, waits for them, and re-layouts: 284 us -> 164 us
    reduce_scatter x16 -> x0, waiting for transfers between devices: 1200 us -> none  [the longest x4 501 us: reduce_row(): lax.psum_scatter(term(jnp.int32(0), lax.axis_size('row') * rows_here), 'r...]
    all_gather x14 -> x0, waiting for transfers between devices: 643 us -> none  [the longest x4 318 us: spread_row(): return lax.all_gather(values, 'row', axis=0, tiled=True)]
    ppermute x0 -> x206, waiting for transfers between devices: none -> 431 us  [the longest x114 245 us: flip(): return lax.ppermute(values, 'row', [(i, i ^ offset) for i in range(count)])]
    ppermute x0 -> x206, starting transfers between devices: none -> 361 us  [the longest x114 142 us: flip(): return lax.ppermute(values, 'row', [(i, i ^ offset) for i in range(count)])]
    slice x113 -> x50, local copies, waits for them, and re-layouts: 163 us -> 50.7 us  [the longest x8 30.4 us: scatter_rows(): second = [block[half:] for block in blocks]]
    psum x5 -> x4, blocking collectives: 51.6 us -> 142 us  [the longest x1 79.7 us: shards(): lax.psum(jnp.concatenate((channel_part[:conv_width], jnp.stack((conv_bias...]
    unnamed x35 -> x0, waiting for transfers between devices: 53 us -> none
    all_gather x7 -> x2, blocking collectives: 79.6 us -> 26.7 us  [the longest x1 13.5 us: shards(): lax.all_gather(width_pack, 'dp', axis=0).transpose(1, 0, 2)]
  transfers between devices with their start and end apart: 35 -> 208, of which waited for: 32 -> 78; matrix products, arithmetic and copies ran while one was open for 12% -> 18% of each run, Pallas kernels for 0% -> 1%
where the time goes in v1:
time: 1410 us; the launch traced here: 1400 us
  waiting for transfers between devices  432 us (31%)
  starting transfers between devices  373 us (26%)
  blocking collectives  168 us (12%)
  local copies, waits for them, and re-layouts  164 us (12%)
  matrix products  119 us (8%)
  other arithmetic  114 us (8%)
  Pallas kernels  20.2 us (1%)
    ppermute x114, waiting for transfers between devices, flip(): return lax.ppermute(values, 'row', [(i, i ^ offset) for i in range(count)])  245 us
    ppermute x114, starting transfers between devices, flip(): return lax.ppermute(values, 'row', [(i, i ^ offset) for i in range(count)])  142 us
    ppermute x36, starting transfers between devices, step_up(): lax.ppermute(values, 'dp', [(i, i + 1) for i in range(count - 1) if first...  98 us
    ppermute x36, waiting for transfers between devices, step_down(): return lax.ppermute(values, 'dp', pairs)  91.4 us
    psum x1, blocking collectives, shards(): lax.psum(jnp.concatenate((channel_part[:conv_width], jnp.stack((conv_bias...  79.7 us
    ppermute x12, starting transfers between devices, exchange_line(): lax.ppermute(blocks[s], 'dp', [(i, (i + count - s) % count) for i in rang...  72.1 us
    ppermute x36, waiting for transfers between devices, step_up(): lax.ppermute(values, 'dp', [(i, i + 1) for i in range(count - 1) if first...  72.1 us
    unnamed x403, local copies, waits for them, and re-layouts  51.1 us
  transfers between devices with their start and end apart: 208, of which 78 were waited for; matrix products, arithmetic and copies ran while one was open for 18% of the time, Pallas kernels for 1%

profile of v1, /device:TPU:0, one launch (start us, length us, event | category | flops | bytes accessed | tf_op | source)
XLA Modules:
  0.0 1395.7 jit_solution(5964769716121793090)
XLA Ops:
  3.5 13.5 all_gather.8
  30.6 13.1 all_gather.9
  44.1 9.9 psum.35
  84.3 7.7 collective-permute-start.29
  151.9 10.1 collective-permute-done.31
  185.0 14.3 %collective-permute-done.49 = bf16[320,640]{1,0:T(8,128)(2,1)S(1)} collective-permute-done((bf16[320,640]{1,0:T(8,128)(2,1)S(1)}, bf16[320,640]{1,0:T(8,128)(2,1)S(1)}, u32[]{:S(2)}, u32[]{:S(2)}) %collective-permute-start.49) | collective-permute-done | bytes 409632 | tf_op jit(solution)/shard_map/ppermute | solution.py:73
  232.9 13.0 collective-permute-start.39
  248.3 8.0 collective-permute-done.39
  256.5 6.8 collective-permute-done.37
  265.7 11.2 collective-permute-done.10
  350.6 6.9 collective-permute-done.68
  385.4 14.0 %collective-permute-done.106 = bf16[128,2560]{0,1:T(8,128)(2,1)S(1)} collective-permute-done((bf16[128,2560]{0,1:T(8,128)(2,1)S(1)}, bf16[128,2560]{0,1:T(8,128)(2,1)S(1)}, u32[]{:S(2)}, u32[]{:S(2)}) %collective-permute-start.106) | collective-permute-done | bytes 655392 | tf_op jit(solution)/shard_map/ppermute | solution.py:73
  441.0 9.0 collective-permute-done.62
  453.7 12.7 collective-permute-done.63
  470.2 13.8 collective-permute-done.71
  486.7 11.4 collective-permute-done.73
  499.0 13.1 collective-permute-done.83
  514.2 11.9 collective-permute-done.74
  528.9 10.4 collective-permute-done.88
  543.3 7.2 broadcast_select_fusion.1
  553.0 7.5 fusion.111
  560.5 7.6 fusion.110
  568.9 15.1 %multiply_reduce_fusion = (f32[960]{0:T(1024)S(1)}, bf16[1024,960]{0,1:T(8,128)(2,1)}, bf16[1024,960]{0,1:T(8,128)(2,1)}, f32[960]{0:T(1024)S(1)}, bf16[1024,960]{0,1:T(8,128)(2,1)}) fusion(f32[1024,960]{0,1:T(8,128)} %fusion.111, f32[960]{0:T(1024)S(1)} %get-tuple-element.365, f32[1024,960]{0,1:T(8,128)} %fusion.110, f32[960]{0:T(1024)S(1)} %get-tuple-element.364, ...), kind=kOutput, calls=%fused_computation.51 | convolution fusion | flops 5107546112 | bytes 23936000 | tf_op jit(solution)/shard_map/dot_general | solution.py:342
  584.0 11.1 fusion.151
  595.2 8.6 fusion.147
  603.8 8.7 fusion.146
  612.5 8.6 convolution_add_fusion
  628.5 8.6 fusion.148
  637.1 20.5 %fusion.112 = f32[1024,2560]{0,1:T(8,128)S(1)} fusion(bf16[1024,960]{0,1:T(8,128)(2,1)S(1)} %copy-done.178, bf16[480,640]{1,0:T(8,128)(2,1)} %collective-permute-done.90, bf16[480,640]{1,0:T(8,128)(2,1)} %collective-permute-done.89, bf16[480,640]{1,0:T(8,128)(2,1)S(1)} %collective-permute-done.88, bf16[480,640]{1,0:T(8,128)(2,1)S(1)} %collective-permute-done.87, ...), kind=kOutput, calls=%fused_computation.460 | convolution fusion | flops 5067571200 | bytes 17367040 | tf_op jit(solution)/shard_map/dot_general | solution.py:338
  659.5 9.6 fusion.118
  733.9 8.3 collective-permute-done.182
  749.5 10.8 collective-permute-done.166
  762.2 7.7 collective-permute-done.168
  776.5 11.6 collective-permute-done.175
  801.9 10.9 collective-permute-done.112
  817.5 11.8 collective-permute-done.92
  834.8 10.0 collective-permute-done.113
  850.7 12.3 collective-permute-done.93
  866.8 20.3 %collective-permute-start.170 = (bf16[160,960]{1,0:T(8,128)(2,1)S(1)}, bf16[160,960]{1,0:T(8,128)(2,1)S(1)}, u32[]{:S(2)}, u32[]{:S(2)}) collective-permute-start(bf16[160,960]{1,0:T(8,128)(2,1)S(1)} %copy-done.130), channel_id=1, source_target_pairs={{0,16},{8,24},{16,0},{24,8},{1,17},{9,25},{17,1},{25,9},{2,18},{10... | collective-permute-start | bytes 921608 | tf_op jit(solution)/shard_map/ppermute | solution.py:122
  887.4 29.4 %collective-permute-start.178 = (bf16[160,960]{1,0:T(8,128)(2,1)S(1)}, bf16[160,960]{1,0:T(8,128)(2,1)S(1)}, u32[]{:S(2)}, u32[]{:S(2)}) collective-permute-start(bf16[160,960]{1,0:T(8,128)(2,1)S(1)} %copy-done.132), channel_id=1, source_target_pairs={{0,8},{8,16},{16,24},{24,0},{1,9},{9,17},{17,25},{25,1},{2,10},{10... | collective-permute-start | bytes 921608 | tf_op jit(solution)/shard_map/ppermute | solution.py:122
  940.9 8.7 collective-permute-start.180
  991.4 8.4 fusion.113
  1093.2 7.7 recurrence_backward.1
  1109.7 79.7 %psum.37 = f32[10,1280]{1,0:T(8,128)S(1)} all-reduce(f32[10,1280]{1,0:T(8,128)S(1)} %pad_maximum_fusion.24), channel_id=1, replica_groups=mesh['dp'=4,'row'=4,'col'=2] {'row','dp'}, use_global_device_ids=true, to_apply=%region_7.8 | all-reduce | flops 12800 | bytes 102400 | tf_op jit(solution)/shard_map/psum | solution.py:641
  1218.1 10.1 collective-permute-done.189
  1296.9 6.8 collective-permute-done.145
  1334.3 15.9 %all-reduce.1 = (f32[512]{0:T(512)S(1)}, f32[2,960]{1,0:T(2,128)S(1)}) all-reduce(f32[512]{0:T(512)S(1)} %get-tuple-element.144, f32[2,960]{1,0:T(2,128)S(1)} %pad_maximum_fusion.32), channel_id=1, replica_groups=mesh['dp'=4,'row'=4,'col'=2] {'row'}, use_global_device_ids=true, to_apply=%region_5.6 | all-reduce | flops 2432 | bytes 19456 | tf_op jit(solution)/shard_map/psum | solution.py:632
  1353.4 36.0 %psum.38 = f32[4,640]{1,0:T(4,128)S(1)} all-reduce(f32[4,640]{1,0:T(4,128)S(1)} %pad_maximum_fusion.31), channel_id=1, replica_groups=mesh['dp'=4,'row'=4,'col'=2] {'dp','col'}, use_global_device_ids=true, to_apply=%region_12.13 | all-reduce | flops 2560 | bytes 20480 | tf_op jit(solution)/shard_map/psum | solution.py:664
  (1107 shorter events, 759.4 us)
Async XLA Ops:
  17.2 67.2 %collective-permute-start.59 = (bf16[4,640]{1,0:T(4,128)(2,1)S(1)}, bf16[4,640]{1,0:T(4,128)(2,1)S(1)}, u32[]{:S(2)}, u32[]{:S(2)}) collective-permute-start(bf16[4,640]{1,0:T(4,128)(2,1)S(1)} %reshape.632), channel_id=1, source_target_pairs={{0,6},{2,4},{4,2},{6,0},{1,7},{3,5},{5,3},{7,1},{8,14},{10,12},{12... | collective-permute-start | bytes 15368 | tf_op jit(solution)/shard_map/ppermute | solution.py:18
  19.7 72.4 %collective-permute-start.58 = (bf16[4,640]{1,0:T(4,128)(2,1)S(1)}, bf16[4,640]{1,0:T(4,128)(2,1)S(1)}, u32[]{:S(2)}, u32[]{:S(2)}) collective-permute-start(bf16[4,640]{1,0:T(4,128)(2,1)S(1)} %reshape.632), channel_id=1, source_target_pairs={{0,4},{2,6},{4,0},{6,2},{1,5},{3,7},{5,1},{7,3},{8,12},{10,14},{12... | collective-permute-start | bytes 15368 | tf_op jit(solution)/shard_map/ppermute | solution.py:18
  20.2 73.2 %collective-permute-start.57 = (bf16[4,640]{1,0:T(4,128)(2,1)S(1)}, bf16[4,640]{1,0:T(4,128)(2,1)S(1)}, u32[]{:S(2)}, u32[]{:S(2)}) collective-permute-start(bf16[4,640]{1,0:T(4,128)(2,1)S(1)} %reshape.632), channel_id=1, source_target_pairs={{0,2},{2,0},{4,6},{6,4},{1,3},{3,1},{5,7},{7,5},{8,10},{10,8},{12,... | collective-permute-start | bytes 15368 | tf_op jit(solution)/shard_map/ppermute | solution.py:18
  24.6 49.9 %collective-permute-start.14 = (bf16[160,256]{1,0:T(8,128)(2,1)S(1)}, bf16[160,256]{1,0:T(8,128)(2,1)}, u32[]{:S(2)}, u32[]{:S(2)}) collective-permute-start(bf16[160,256]{1,0:T(8,128)(2,1)S(1)} %bitcast.212), channel_id=1, source_target_pairs={{0,8},{8,16},{16,24},{1,9},{9,17},{17,25},{2,10},{10,18},{18,26},{... | collective-permute-start | bytes 245768 | tf_op jit(solution)/shard_map/ppermute | solution.py:67
  28.7 44.4 %collective-permute-start.15 = (bf16[160,256]{1,0:T(8,128)(2,1)S(1)}, bf16[160,256]{1,0:T(8,128)(2,1)}, u32[]{:S(2)}, u32[]{:S(2)}) collective-permute-start(bf16[160,256]{1,0:T(8,128)(2,1)S(1)} %bitcast.213), channel_id=1, source_target_pairs={{24,16},{16,8},{8,0},{25,17},{17,9},{9,1},{26,18},{18,10},{10,2},{... | collective-permute-start | bytes 245768 | tf_op jit(solution)/shard_map/ppermute | solution.py:73
  84.3 61.0 %collective-permute-start.29 = (bf16[160,1280]{1,0:T(8,128)(2,1)}, bf16[160,1280]{1,0:T(8,128)(2,1)S(1)}, u32[]{:S(2)}, u32[]{:S(2)}) collective-permute-start(bf16[160,1280]{1,0:T(8,128)(2,1)} %get-tuple-element.179), channel_id=1, source_target_pairs={{0,8},{8,16},{16,24},{1,9},{9,17},{17,25},{2,10},{10,18},{18,26},{... | collective-permute-start | bytes 1228808 | tf_op jit(solution)/shard_map/ppermute | solution.py:67
  92.1 46.9 %collective-permute-start.30 = (bf16[160,1280]{1,0:T(8,128)(2,1)}, bf16[160,1280]{1,0:T(8,128)(2,1)S(1)}, u32[]{:S(2)}, u32[]{:S(2)}) collective-permute-start(bf16[160,1280]{1,0:T(8,128)(2,1)} %get-tuple-element.179), channel_id=1, source_target_pairs={{24,16},{16,8},{8,0},{25,17},{17,9},{9,1},{26,18},{18,10},{10,2},{... | collective-permute-start | bytes 1228808 | tf_op jit(solution)/shard_map/ppermute | solution.py:73
  93.4 57.8 %collective-permute-start = (bf16[512,640]{0,1:T(8,128)(2,1)}, bf16[512,640]{0,1:T(8,128)(2,1)S(1)}, u32[]{:S(2)}, u32[]{:S(2)}) collective-permute-start(bf16[512,640]{0,1:T(8,128)(2,1)} %fusion.16), channel_id=1, source_target_pairs={{0,1},{1,0},{2,3},{3,2},{4,5},{5,4},{6,7},{7,6},{8,9},{9,8},{10,11... | collective-permute-start | bytes 1966088 | tf_op jit(solution)/shard_map/ppermute | solution.py:22
  94.1 55.8 %collective-permute-start.1 = (bf16[160,1280]{1,0:T(8,128)(2,1)}, bf16[160,1280]{1,0:T(8,128)(2,1)S(1)}, u32[]{:S(2)}, u32[]{:S(2)}) collective-permute-start(bf16[160,1280]{1,0:T(8,128)(2,1)} %get-tuple-element.183), channel_id=1, source_target_pairs={{0,8},{8,16},{16,24},{1,9},{9,17},{17,25},{2,10},{10,18},{18,26},{... | collective-permute-start | bytes 1228808 | tf_op jit(solution)/shard_map/ppermute | solution.py:67
  183.5 158.5 %collective-permute-start.76 = (bf16[160,960]{1,0:T(8,128)(2,1)}, bf16[160,960]{1,0:T(8,128)(2,1)}, u32[]{:S(2)}, u32[]{:S(2)}) collective-permute-start(bf16[160,960]{1,0:T(8,128)(2,1)} %get-tuple-element.301), channel_id=1, source_target_pairs={{0,8},{8,16},{16,24},{24,0},{1,9},{9,17},{17,25},{25,1},{2,10},{10... | collective-permute-start | bytes 921608 | tf_op jit(solution)/shard_map/ppermute | solution.py:122
  201.3 105.4 %collective-permute-start.52 = (bf16[320,640]{1,0:T(8,128)(2,1)}, bf16[320,640]{1,0:T(8,128)(2,1)}, u32[]{:S(2)}, u32[]{:S(2)}) collective-permute-start(bf16[320,640]{1,0:T(8,128)(2,1)} %collective-permute-done.51), channel_id=1, source_target_pairs={{16,24},{17,25},{18,26},{19,27},{20,28},{21,29},{22,30},{23,31}} | collective-permute-start | bytes 1228808 | tf_op jit(solution)/shard_map/ppermute | solution.py:67
  248.0 48.8 %collective-permute-start.38 = (bf16[128,1280]{1,0:T(8,128)(2,1)}, bf16[128,1280]{1,0:T(8,128)(2,1)}, u32[]{:S(2)}, u32[]{:S(2)}) collective-permute-start(bf16[128,1280]{1,0:T(8,128)(2,1)} %get-tuple-element.223), channel_id=1, source_target_pairs={{0,2},{2,0},{4,6},{6,4},{1,3},{3,1},{5,7},{7,5},{8,10},{10,8},{12,... | collective-permute-start | bytes 983048 | tf_op jit(solution)/shard_map/ppermute | solution.py:18
  312.5 33.0 %collective-permute-start.77 = (bf16[160,960]{1,0:T(8,128)(2,1)S(1)}, bf16[160,960]{1,0:T(8,128)(2,1)S(1)}, u32[]{:S(2)}, u32[]{:S(2)}) collective-permute-start(bf16[160,960]{1,0:T(8,128)(2,1)S(1)} %copy-done.127), channel_id=1, source_target_pairs={{0,16},{8,24},{16,0},{24,8},{1,17},{9,25},{17,1},{25,9},{2,18},{10... | collective-permute-start | bytes 921608 | tf_op jit(solution)/shard_map/ppermute | solution.py:122
  342.0 40.5 %collective-permute-start.53 = (f32[512,640]{0,1:T(8,128)S(1)}, f32[512,640]{0,1:T(8,128)S(1)}, u32[]{:S(2)}, u32[]{:S(2)}) collective-permute-start(f32[512,640]{0,1:T(8,128)S(1)} %constant_dynamic-slice_fusion.37), channel_id=1, source_target_pairs={{0,1},{1,0},{2,3},{3,2},{4,5},{5,4},{6,7},{7,6},{8,9},{9,8},{10,11... | collective-permute-start | bytes 3932168 | tf_op jit(solution)/shard_map/ppermute | solution.py:22
  365.7 86.4 %collective-permute-start.79 = (bf16[320,960]{1,0:T(8,128)(2,1)S(1)}, bf16[320,960]{1,0:T(8,128)(2,1)S(1)}, u32[]{:S(2)}, u32[]{:S(2)}) collective-permute-start(bf16[320,960]{1,0:T(8,128)(2,1)S(1)} %get-tuple-element.292), channel_id=1, source_target_pairs={{0,2},{2,0},{4,6},{6,4},{1,3},{3,1},{5,7},{7,5},{8,10},{10,8},{12,... | collective-permute-start | bytes 1843208 | tf_op jit(solution)/shard_map/ppermute | solution.py:18
  367.4 99.8 %collective-permute-start.81 = (bf16[320,960]{1,0:T(8,128)(2,1)S(1)}, bf16[320,960]{1,0:T(8,128)(2,1)S(1)}, u32[]{:S(2)}, u32[]{:S(2)}) collective-permute-start(bf16[320,960]{1,0:T(8,128)(2,1)S(1)} %get-tuple-element.292), channel_id=1, source_target_pairs={{0,4},{2,6},{4,0},{6,2},{1,5},{3,7},{5,1},{7,3},{8,12},{10,14},{12... | collective-permute-start | bytes 1843208 | tf_op jit(solution)/shard_map/ppermute | solution.py:18
  421.2 45.1 %collective-permute-start.80 = (bf16[320,960]{1,0:T(8,128)(2,1)S(1)}, bf16[320,960]{1,0:T(8,128)(2,1)S(1)}, u32[]{:S(2)}, u32[]{:S(2)}) collective-permute-start(bf16[320,960]{1,0:T(8,128)(2,1)S(1)} %get-tuple-element.291), channel_id=1, source_target_pairs={{0,2},{2,0},{4,6},{6,4},{1,3},{3,1},{5,7},{7,5},{8,10},{10,8},{12,... | collective-permute-start | bytes 1843208 | tf_op jit(solution)/shard_map/ppermute | solution.py:18
  466.3 76.1 %collective-permute-start.110 = (bf16[512,2560]{0,1:T(8,128)(2,1)S(1)}, bf16[512,2560]{0,1:T(8,128)(2,1)S(1)}, u32[]{:S(2)}, u32[]{:S(2)}) collective-permute-start(bf16[512,2560]{0,1:T(8,128)(2,1)S(1)} %pad_maximum_fusion.5), channel_id=1, source_target_pairs={{0,1},{1,0},{2,3},{3,2},{4,5},{5,4},{6,7},{7,6},{8,9},{9,8},{10,11... | collective-permute-start | bytes 7864328 | tf_op jit(solution)/shard_map/ppermute | solution.py:22
  470.0 80.5 %collective-permute-start.66 = (bf16[512,2560]{0,1:T(8,128)(2,1)S(1)}, bf16[512,2560]{0,1:T(8,128)(2,1)S(1)}, u32[]{:S(2)}, u32[]{:S(2)}) collective-permute-start(bf16[512,2560]{0,1:T(8,128)(2,1)S(1)} %pad_maximum_fusion.4), channel_id=1, source_target_pairs={{0,1},{1,0},{2,3},{3,2},{4,5},{5,4},{6,7},{7,6},{8,9},{9,8},{10,11... | collective-permute-start | bytes 7864328 | tf_op jit(solution)/shard_map/ppermute | solution.py:22
  528.1 40.0 %collective-permute-start.87 = (bf16[480,640]{1,0:T(8,128)(2,1)S(1)}, bf16[480,640]{1,0:T(8,128)(2,1)S(1)}, u32[]{:S(2)}, u32[]{:S(2)}) collective-permute-start(bf16[480,640]{1,0:T(8,128)(2,1)S(1)} %copy-done.113), channel_id=1, source_target_pairs={{0,4},{2,6},{4,0},{6,2},{1,5},{3,7},{5,1},{7,3},{8,12},{10,14},{12... | collective-permute-start | bytes 1843208 | tf_op jit(solution)/shard_map/ppermute | solution.py:18
  673.7 47.4 %collective-permute-start.164 = (bf16[320,960]{1,0:T(8,128)(2,1)}, bf16[320,960]{1,0:T(8,128)(2,1)}, u32[]{:S(2)}, u32[]{:S(2)}) collective-permute-start(bf16[320,960]{1,0:T(8,128)(2,1)} %copy.176), channel_id=1, source_target_pairs={{0,4},{2,6},{4,0},{6,2},{1,5},{3,7},{5,1},{7,3},{8,12},{10,14},{12... | collective-permute-start | bytes 1843208 | tf_op jit(solution)/shard_map/ppermute | solution.py:18
  677.1 49.8 %collective-permute-start.167 = (bf16[320,960]{1,0:T(8,128)(2,1)}, bf16[320,960]{1,0:T(8,128)(2,1)}, u32[]{:S(2)}, u32[]{:S(2)}) collective-permute-start(bf16[320,960]{1,0:T(8,128)(2,1)} %copy.180), channel_id=1, source_target_pairs={{0,2},{2,0},{4,6},{6,4},{1,3},{3,1},{5,7},{7,5},{8,10},{10,8},{12,... | collective-permute-start | bytes 1843208 | tf_op jit(solution)/shard_map/ppermute | solution.py:18
  690.9 37.7 %collective-permute-start.173 = (bf16[320,960]{1,0:T(8,128)(2,1)}, bf16[320,960]{1,0:T(8,128)(2,1)}, u32[]{:S(2)}, u32[]{:S(2)}) collective-permute-start(bf16[320,960]{1,0:T(8,128)(2,1)} %copy.184), channel_id=1, source_target_pairs={{0,4},{2,6},{4,0},{6,2},{1,5},{3,7},{5,1},{7,3},{8,12},{10,14},{12... | collective-permute-start | bytes 1843208 | tf_op jit(solution)/shard_map/ppermute | solution.py:18
  726.8 65.9 %collective-permute-start.111 = (bf16[512,2560]{0,1:T(8,128)(2,1)}, bf16[512,2560]{0,1:T(8,128)(2,1)S(1)}, u32[]{:S(2)}, u32[]{:S(2)}) collective-permute-start(bf16[512,2560]{0,1:T(8,128)(2,1)} %dynamic-slice_convert_fusion), channel_id=1, source_target_pairs={{0,1},{1,0},{2,3},{3,2},{4,5},{5,4},{6,7},{7,6},{8,9},{9,8},{10,11... | collective-permute-start | bytes 7864328 | tf_op jit(solution)/shard_map/ppermute | solution.py:22
  760.3 39.6 %collective-permute-start.91 = (bf16[512,2560]{0,1:T(8,128)(2,1)S(1)}, bf16[512,2560]{0,1:T(8,128)(2,1)S(1)}, u32[]{:S(2)}, u32[]{:S(2)}) collective-permute-start(bf16[512,2560]{0,1:T(8,128)(2,1)S(1)} %copy-done.83), channel_id=1, source_target_pairs={{0,1},{1,0},{2,3},{3,2},{4,5},{5,4},{6,7},{7,6},{8,9},{9,8},{10,11... | collective-permute-start | bytes 7864328 | tf_op jit(solution)/shard_map/ppermute | solution.py:22
  774.4 92.4 %collective-permute-start.181 = (bf16[480,640]{1,0:T(8,128)(2,1)}, bf16[480,640]{1,0:T(8,128)(2,1)}, u32[]{:S(2)}, u32[]{:S(2)}) collective-permute-start(bf16[480,640]{1,0:T(8,128)(2,1)} %get-tuple-element.224), channel_id=1, source_target_pairs={{0,4},{2,6},{4,0},{6,2},{1,5},{3,7},{5,1},{7,3},{8,12},{10,14},{12... | collective-permute-start | bytes 1843208 | tf_op jit(solution)/shard_map/ppermute | solution.py:18
  788.1 99.0 %collective-permute-start.185 = (bf16[480,640]{1,0:T(8,128)(2,1)}, bf16[480,640]{1,0:T(8,128)(2,1)S(1)}, u32[]{:S(2)}, u32[]{:S(2)}) collective-permute-start(bf16[480,640]{1,0:T(8,128)(2,1)} %get-tuple-element.225), channel_id=1, source_target_pairs={{0,2},{2,0},{4,6},{6,4},{1,3},{3,1},{5,7},{7,5},{8,10},{10,8},{12,... | collective-permute-start | bytes 1843208 | tf_op jit(solution)/shard_map/ppermute | solution.py:18
  789.5 128.4 %collective-permute-start.183 = (bf16[480,640]{1,0:T(8,128)(2,1)}, bf16[480,640]{1,0:T(8,128)(2,1)S(1)}, u32[]{:S(2)}, u32[]{:S(2)}) collective-permute-start(bf16[480,640]{1,0:T(8,128)(2,1)} %fusion.31), channel_id=1, source_target_pairs={{0,2},{2,0},{4,6},{6,4},{1,3},{3,1},{5,7},{7,5},{8,10},{10,8},{12,... | collective-permute-start | bytes 1843208 | tf_op jit(solution)/shard_map/ppermute | solution.py:18
  799.9 34.0 %collective-permute-start.115 = (bf16[128,2560]{0,1:T(8,128)(2,1)S(1)}, bf16[128,2560]{0,1:T(8,128)(2,1)S(1)}, u32[]{:S(2)}, u32[]{:S(2)}) collective-permute-start(bf16[128,2560]{0,1:T(8,128)(2,1)S(1)} %get-tuple-element.207), channel_id=1, source_target_pairs={{24,16},{25,17},{26,18},{27,19},{28,20},{29,21},{30,22},{31,23}} | collective-permute-start | bytes 1966088 | tf_op jit(solution)/shard_map/ppermute | solution.py:73
  850.4 67.4 %collective-permute-start.169 = (bf16[160,960]{1,0:T(8,128)(2,1)S(1)}, bf16[160,960]{1,0:T(8,128)(2,1)S(1)}, u32[]{:S(2)}, u32[]{:S(2)}) collective-permute-start(bf16[160,960]{1,0:T(8,128)(2,1)S(1)} %copy-done.131), channel_id=1, source_target_pairs={{0,8},{8,16},{16,24},{24,0},{1,9},{9,17},{17,25},{25,1},{2,10},{10... | collective-permute-start | bytes 921608 | tf_op jit(solution)/shard_map/ppermute | solution.py:122
  866.8 57.8 %collective-permute-start.170 = (bf16[160,960]{1,0:T(8,128)(2,1)S(1)}, bf16[160,960]{1,0:T(8,128)(2,1)S(1)}, u32[]{:S(2)}, u32[]{:S(2)}) collective-permute-start(bf16[160,960]{1,0:T(8,128)(2,1)S(1)} %copy-done.130), channel_id=1, source_target_pairs={{0,16},{8,24},{16,0},{24,8},{1,17},{9,25},{17,1},{25,9},{2,18},{10... | collective-permute-start | bytes 921608 | tf_op jit(solution)/shard_map/ppermute | solution.py:122
  887.1 39.6 %collective-permute-start.171 = (bf16[160,960]{1,0:T(8,128)(2,1)S(1)}, bf16[160,960]{1,0:T(8,128)(2,1)S(1)}, u32[]{:S(2)}, u32[]{:S(2)}) collective-permute-start(bf16[160,960]{1,0:T(8,128)(2,1)S(1)} %copy-done.129), channel_id=1, source_target_pairs={{0,24},{8,0},{16,8},{24,16},{1,25},{9,1},{17,9},{25,17},{2,26},{10... | collective-permute-start | bytes 921608 | tf_op jit(solution)/shard_map/ppermute | solution.py:122
  887.4 40.5 %collective-permute-start.178 = (bf16[160,960]{1,0:T(8,128)(2,1)S(1)}, bf16[160,960]{1,0:T(8,128)(2,1)S(1)}, u32[]{:S(2)}, u32[]{:S(2)}) collective-permute-start(bf16[160,960]{1,0:T(8,128)(2,1)S(1)} %copy-done.132), channel_id=1, source_target_pairs={{0,8},{8,16},{16,24},{24,0},{1,9},{9,17},{17,25},{25,1},{2,10},{10... | collective-permute-start | bytes 921608 | tf_op jit(solution)/shard_map/ppermute | solution.py:122
  917.9 66.5 %collective-permute-start.114 = (bf16[128,2560]{0,1:T(8,128)(2,1)}, bf16[128,2560]{0,1:T(8,128)(2,1)S(1)}, u32[]{:S(2)}, u32[]{:S(2)}) collective-permute-start(bf16[128,2560]{0,1:T(8,128)(2,1)} %get-tuple-element.204), channel_id=1, source_target_pairs={{0,8},{8,16},{16,24},{1,9},{9,17},{17,25},{2,10},{10,18},{18,26},{... | collective-permute-start | bytes 1966088 | tf_op jit(solution)/shard_map/ppermute | solution.py:67
  924.5 61.7 %collective-permute-start.94 = (bf16[128,2560]{0,1:T(8,128)(2,1)}, bf16[128,2560]{0,1:T(8,128)(2,1)}, u32[]{:S(2)}, u32[]{:S(2)}) collective-permute-start(bf16[128,2560]{0,1:T(8,128)(2,1)} %get-tuple-element.210), channel_id=1, source_target_pairs={{0,8},{8,16},{16,24},{1,9},{9,17},{17,25},{2,10},{10,18},{18,26},{... | collective-permute-start | bytes 1966088 | tf_op jit(solution)/shard_map/ppermute | solution.py:67
  926.7 59.5 %collective-permute-start.117 = (bf16[128,2560]{0,1:T(8,128)(2,1)}, bf16[128,2560]{0,1:T(8,128)(2,1)}, u32[]{:S(2)}, u32[]{:S(2)}) collective-permute-start(bf16[128,2560]{0,1:T(8,128)(2,1)} %add_convert_fusion.9), channel_id=1, source_target_pairs={{24,16},{16,8},{8,0},{25,17},{17,9},{9,1},{26,18},{18,10},{10,2},{... | collective-permute-start | bytes 1966088 | tf_op jit(solution)/shard_map/ppermute | solution.py:73
  928.0 58.2 %collective-permute-start.97 = (bf16[128,2560]{0,1:T(8,128)(2,1)}, bf16[128,2560]{0,1:T(8,128)(2,1)}, u32[]{:S(2)}, u32[]{:S(2)}) collective-permute-start(bf16[128,2560]{0,1:T(8,128)(2,1)} %add_convert_fusion.13), channel_id=1, source_target_pairs={{24,16},{16,8},{8,0},{25,17},{17,9},{9,1},{26,18},{18,10},{10,2},{... | collective-permute-start | bytes 1966088 | tf_op jit(solution)/shard_map/ppermute | solution.py:73
  940.9 35.1 %collective-permute-start.180 = (bf16[160,960]{1,0:T(8,128)(2,1)}, bf16[160,960]{1,0:T(8,128)(2,1)}, u32[]{:S(2)}, u32[]{:S(2)}) collective-permute-start(bf16[160,960]{1,0:T(8,128)(2,1)} %get-tuple-element.267), channel_id=1, source_target_pairs={{0,24},{8,0},{16,8},{24,16},{1,25},{9,1},{17,9},{25,17},{2,26},{10... | collective-permute-start | bytes 921608 | tf_op jit(solution)/shard_map/ppermute | solution.py:122
  1062.6 140.8 %collective-permute-start.161 = (bf16[320,640]{1,0:T(8,128)(2,1)}, bf16[320,640]{1,0:T(8,128)(2,1)}, u32[]{:S(2)}, u32[]{:S(2)}) collective-permute-start(bf16[320,640]{1,0:T(8,128)(2,1)} %get-tuple-element.237), channel_id=1, source_target_pairs={{24,16},{16,8},{25,17},{17,9},{26,18},{18,10},{27,19},{19,11},{28,... | collective-permute-start | bytes 1228808 | tf_op jit(solution)/shard_map/ppermute | solution.py:73
  1064.2 203.3 %collective-permute-start.159 = (bf16[320,640]{1,0:T(8,128)(2,1)}, bf16[320,640]{1,0:T(8,128)(2,1)}, u32[]{:S(2)}, u32[]{:S(2)}) collective-permute-start(bf16[320,640]{1,0:T(8,128)(2,1)} %get-tuple-element.236), channel_id=1, source_target_pairs={{0,8},{8,16},{16,24},{1,9},{9,17},{17,25},{2,10},{10,18},{18,26},{... | collective-permute-start | bytes 1228808 | tf_op jit(solution)/shard_map/ppermute | solution.py:67
  1084.7 120.4 %collective-permute-start.139 = (bf16[128,1280]{1,0:T(8,128)(2,1)}, bf16[128,1280]{1,0:T(8,128)(2,1)}, u32[]{:S(2)}, u32[]{:S(2)}) collective-permute-start(bf16[128,1280]{1,0:T(8,128)(2,1)} %get-tuple-element.306), channel_id=1, source_target_pairs={{0,2},{2,0},{4,6},{6,4},{1,3},{3,1},{5,7},{7,5},{8,10},{10,8},{12,... | collective-permute-start | bytes 983048 | tf_op jit(solution)/shard_map/ppermute | solution.py:18
  1086.0 128.8 %collective-permute-start.141 = (bf16[128,1280]{1,0:T(8,128)(2,1)}, bf16[128,1280]{1,0:T(8,128)(2,1)}, u32[]{:S(2)}, u32[]{:S(2)}) collective-permute-start(bf16[128,1280]{1,0:T(8,128)(2,1)} %get-tuple-element.306), channel_id=1, source_target_pairs={{0,4},{2,6},{4,0},{6,2},{1,5},{3,7},{5,1},{7,3},{8,12},{10,14},{12... | collective-permute-start | bytes 983048 | tf_op jit(solution)/shard_map/ppermute | solution.py:18
  1102.8 88.0 %collective-permute-start.131 = (f32[3,1280]{1,0:T(4,128)S(1)}, f32[3,1280]{1,0:T(4,128)S(1)}, u32[]{:S(2)}, u32[]{:S(2)}) collective-permute-start(f32[3,1280]{1,0:T(4,128)S(1)} %slice.634), channel_id=1, source_target_pairs={{2,0},{4,2},{6,4},{3,1},{5,3},{7,5},{10,8},{12,10},{14,12},{11,9},... | collective-permute-start | bytes 46088 | tf_op jit(solution)/shard_map/ppermute | solution.py:165
  1284.8 47.8 %collective-permute-start.144 = (f32[512,640]{0,1:T(8,128)S(1)}, f32[512,640]{0,1:T(8,128)S(1)}, u32[]{:S(2)}, u32[]{:S(2)}) collective-permute-start(f32[512,640]{0,1:T(8,128)S(1)} %constant_dynamic-slice_fusion.17), channel_id=1, source_target_pairs={{0,1},{1,0},{2,3},{3,2},{4,5},{5,4},{6,7},{7,6},{8,9},{9,8},{10,11... | collective-permute-start | bytes 3932168 | tf_op jit(solution)/shard_map/ppermute | solution.py:22
  1317.2 73.5 %collective-permute-start.153 = (bf16[160,1280]{1,0:T(8,128)(2,1)}, bf16[160,1280]{1,0:T(8,128)(2,1)}, u32[]{:S(2)}, u32[]{:S(2)}) collective-permute-start(bf16[160,1280]{1,0:T(8,128)(2,1)} %get-tuple-element.240), channel_id=1, source_target_pairs={{0,8},{8,16},{16,24},{1,9},{9,17},{17,25},{2,10},{10,18},{18,26},{... | collective-permute-start | bytes 1228808 | tf_op jit(solution)/shard_map/ppermute | solution.py:67
  1323.4 69.7 %collective-permute-start.147 = (bf16[160,1280]{1,0:T(8,128)(2,1)}, bf16[160,1280]{1,0:T(8,128)(2,1)}, u32[]{:S(2)}, u32[]{:S(2)}) collective-permute-start(bf16[160,1280]{1,0:T(8,128)(2,1)} %get-tuple-element.244), channel_id=1, source_target_pairs={{0,8},{8,16},{16,24},{1,9},{9,17},{17,25},{2,10},{10,18},{18,26},{... | collective-permute-start | bytes 1228808 | tf_op jit(solution)/shard_map/ppermute | solution.py:67
  1329.0 61.7 %collective-permute-start.156 = (bf16[160,1280]{1,0:T(8,128)(2,1)}, bf16[160,1280]{1,0:T(8,128)(2,1)}, u32[]{:S(2)}, u32[]{:S(2)}) collective-permute-start(bf16[160,1280]{1,0:T(8,128)(2,1)} %add_convert_fusion.21), channel_id=1, source_target_pairs={{24,16},{16,8},{8,0},{25,17},{17,9},{9,1},{26,18},{18,10},{10,2},{... | collective-permute-start | bytes 1228808 | tf_op jit(solution)/shard_map/ppermute | solution.py:73
  1331.2 61.9 %collective-permute-start.150 = (bf16[160,1280]{1,0:T(8,128)(2,1)}, bf16[160,1280]{1,0:T(8,128)(2,1)}, u32[]{:S(2)}, u32[]{:S(2)}) collective-permute-start(bf16[160,1280]{1,0:T(8,128)(2,1)} %add_convert_fusion.25), channel_id=1, source_target_pairs={{24,16},{16,8},{8,0},{25,17},{17,9},{9,1},{26,18},{18,10},{10,2},{... | collective-permute-start | bytes 1228808 | tf_op jit(solution)/shard_map/ppermute | solution.py:73
  (348 other events, 7035.9 us)

commit v2 on v0

v2 whole, which is shorter than its diff:
```python
import functools

import jax
import jax.numpy as jnp
from jax import lax
from jax.experimental import pallas as pl
from jax.experimental.pallas import tpu as pltpu
from jax.sharding import PartitionSpec as P

epsilon = 1e-06
LOW = jnp.bfloat16
WIDE = jnp.float32
MESH = pl.DeviceIdType.MESH
VMEM = pl.BlockSpec(memory_space=pltpu.VMEM)
ANY = pl.BlockSpec(memory_space=pl.ANY)


class Links:
    def __init__(self, send, recv, local):
        self.send, self.recv, self.local = send, recv, local
        self.sent = self.kept = 0

    def copy(self, src, dst, **where):
        k, self.sent = self.sent, self.sent + 1
        return pltpu.make_async_remote_copy(
            src_ref=src,
            dst_ref=dst,
            send_sem=self.send.at[k],
            recv_sem=self.recv.at[k],
            device_id=where,
            device_id_type=MESH,
        )

    def keep(self, src, dst):
        k, self.kept = self.kept, self.kept + 1
        copy = pltpu.make_async_copy(src, dst, self.local.at[k])
        copy.start()
        return copy


class Place:
    def __init__(self, count_dp):
        self.row, self.dp, self.col = (lax.axis_index(name) for name in ("row", "dp", "col"))
        self.count = count_dp
        first, second = lax.rem(self.row, 2), lax.div(self.row, 2)
        self.near = [self.row, self.row + 1 - 2 * first, self.row + 2 - 4 * second, 3 - self.row]
        self.other = 1 - self.col

    def turn(self, index):
        return lax.rem(index + self.count, self.count)


def greet(place, rows=False, line=False, cores=False):
    barrier = pltpu.get_barrier_semaphore()
    partners = []
    if rows:
        partners += [{"row": place.near[k]} for k in range(1, 4)]
    if line:
        partners += [{"dp": place.turn(place.dp + k)} for k in range(1, place.count)]
    if cores:
        partners += [{"col": place.other}]
    for where in partners:
        pl.semaphore_signal(barrier, inc=1, device_id=where, device_id_type=MESH)
    pl.semaphore_wait(barrier, len(partners))


def run(tasks):
    live = list(tasks)
    while live:
        live = [task for task in live if next(task, None) is not None]


def chain(*tasks):
    for task in tasks:
        yield from task


def when(condition, action):
    pl.when(condition)(lambda: action() and None)


def halves(size):
    first = -(-size // 32) * 16
    return (pl.ds(0, first), pl.ds(first, size - first))


def by_rows(count, body):
    step = 16 if count % 16 == 0 else count

    def lap(i, carry):
        body(pl.ds(pl.multiple_of(i * step, step), step))
        return carry

    lax.fori_loop(0, count // step, lap, 0)


def by_pieces(pieces, height, body):
    def lap(i, carry):
        by_rows(height, lambda rows: body(i, rows))
        return carry

    if pieces == 1:
        by_rows(height, lambda rows: body(0, rows))
    else:
        lax.fori_loop(0, pieces, lap, 0)


def gather_rows(links, place, own, piece):
    row, near, side, _ = place.near
    out = [
        links.copy(own(0), piece(row, 0), row=near),
        links.copy(own(1), piece(row, 1), row=side),
        links.copy(own(1), piece(row, 1), row=near),
        links.copy(own(0), piece(row, 0), row=side),
    ]
    for copy in out:
        copy.start()
    yield 1
    out[0].wait_recv()
    out.append(links.copy(piece(near, 0), piece(near, 0), row=side))
    out[4].start()
    out[1].wait_recv()
    out.append(links.copy(piece(side, 1), piece(side, 1), row=near))
    out[5].start()
    yield 1
    for copy in out[2:]:
        copy.wait_recv()
    for copy in out:
        copy.wait_send()


def exchange_rows(links, place, source, target):
    out = [
        links.copy(source(place.near[k]), target(place.row), row=place.near[k])
        for k in range(1, 4)
    ]
    for copy in out:
        copy.start()
    yield 1
    for copy in out:
        copy.wait_recv()
    for copy in out:
        copy.wait_send()


def exchange_line(links, place, source, target):
    out = []
    for k in range(1, place.count):
        far = place.turn(place.dp + k)
        out.append(links.copy(source(far), target(place.dp), dp=far))
    for copy in out:
        copy.start()
    yield 1
    for copy in out:
        copy.wait_recv()
    for copy in out:
        copy.wait_send()


def gather_line(links, place, own, piece, share=False):
    z, count, turn = place.dp, place.count, place.turn
    ups, downs, shared = [], [], []

    def pass_on(block, valid):
        copy = links.copy(piece(block), piece(block), col=place.other)
        when(valid, copy.start)
        shared.append((copy, valid))

    if share:
        copy = links.copy(own, piece(z), col=place.other)
        copy.start()
        shared.append((copy, z >= 0))
    for step in range(1, count + 1):
        if step > 1:
            yield 1
            below, above = z >= step - 1, z <= count - step
            when(below, ups[-1].wait_recv)
            when(above, downs[-1].wait_recv)
        if step < count:
            low, high = turn(z - step + 1), turn(z + step - 1)
            ups.append(
                links.copy(own if step == 1 else piece(low), piece(low), dp=turn(z + 1))
            )
            downs.append(
                links.copy(own if step == 1 else piece(high), piece(high), dp=turn(z - 1))
            )
            when((z >= step - 1) & (z < count - 1), ups[-1].start)
            when((z <= count - step) & (z > 0), downs[-1].start)
        if step > 1 and share:
            pass_on(turn(z - step + 1), below)
            pass_on(turn(z + step - 1), above)
    yield 1
    for copy, valid in shared:
        when(valid, copy.wait_recv)
    for step in range(1, count):
        when((z >= step - 1) & (z < count - 1), ups[step - 1].wait_send)
        when((z <= count - step) & (z > 0), downs[step - 1].wait_send)
    for copy, valid in shared:
        when(valid, copy.wait_send)


def scatter_rows(links, place, part, buffers, result):
    row, near, side, far = place.near
    heights = [part(row, h).shape[0] for h in range(2)]

    def buffer(i, h):
        return buffers.at[i, pl.ds(0, heights[h])]

    out = [
        links.copy(part(far, 0), buffer(5, 0), row=side),
        links.copy(part(far, 1), buffer(7, 1), row=near),
        links.copy(part(side, 0), buffer(4, 0), row=side),
        links.copy(part(near, 1), buffer(6, 1), row=near),
    ]
    for copy in out:
        copy.start()
    loads = [
        links.keep(part(near, 0), buffer(0, 0)),
        links.keep(part(side, 1), buffer(1, 1)),
        links.keep(part(row, 0), buffer(2, 0)),
        links.keep(part(row, 1), buffer(3, 1)),
    ]
    yield 1
    for h, target in ((0, near), (1, side)):
        loads[h].wait()
        out[h].wait_recv()

        def add(rows, h=h):
            total = buffers[h, rows].astype(WIDE) + buffers[5 + 2 * h, rows].astype(WIDE)
            buffers[h, rows] = total.astype(LOW)

        by_rows(heights[h], add)
        out.append(links.copy(buffer(h, h), buffer(8 + h, h), row=target))
        out[-1].start()
        yield 1
    for h in range(2):
        loads[2 + h].wait()
        out[2 + h].wait_recv()
        out[4 + h].wait_recv()

        def finish(rows, h=h):
            result(
                h,
                rows,
                buffers[2 + h, rows].astype(WIDE)
                + buffers[4 + 2 * h, rows].astype(WIDE)
                + buffers[8 + h, rows].astype(WIDE),
            )

        by_rows(heights[h], finish)
    for copy in out:
        copy.wait_send()


def row_buffers(size, width):
    return pltpu.VMEM((10, halves(size)[0].size, width), LOW)


def scatter_line(links, place, ready, term, ups_in, downs_in, staging, result):
    z, count, turn = place.dp, place.count, place.turn
    pieces, height = ups_in.shape[1:3]
    ups, downs = [None], [None]

    def sends_up(t):
        return (z <= t - 1) & (z < count - 1)

    def sends_down(t):
        return (z >= count - t) & (z > 0)

    def fill(slot, block, arrived):
        def body(i, rows):
            value = term(block, i, rows)
            if arrived is not None:
                value = value + arrived[i, rows].astype(WIDE)
            staging[slot, i, rows] = value.astype(LOW)

        by_pieces(pieces, height, body)

    for t in range(1, count):
        ready(t)
        ready(count - t)
        for which in range(2):
            copies, into = ((ups, ups_in), (downs, downs_in))[which]
            sends = (sends_up, sends_down)[which]
            first = (z == 0, z == count - 1)[which]
            block = (turn(z - t), turn(z + t))[which]
            target = (turn(z + 1), turn(z - 1))[which]
            slot = 2 * which + t % 2
            if t > 2:
                when(sends(t - 2), copies[t - 2].wait_send)
            copy = links.copy(staging.at[slot], into.at[t - 1], dp=target)
            copies.append(copy)

            def begin(copy=copy, slot=slot, block=block):
                fill(slot, block, None)
                copy.start()

            when(sends(t) & first, begin)
            if t > 1:

                def go_on(copy=copy, slot=slot, block=block, before=copies[t - 1], into=into, t=t):
                    before.wait_recv()
                    fill(slot, block, into.at[t - 2])
                    copy.start()

                when(sends(t) & jnp.logical_not(first), go_on)
        yield 1
    ready(0)
    last = count - 1
    from_below, from_above = ups_in.at[last - 1], downs_in.at[last - 1]
    when(z > 0, ups[last].wait_recv)
    when(z < last, downs[last].wait_recv)

    def finish(below, above):
        def body(i, rows):
            value = term(z, i, rows)
            if below:
                value = value + from_below[i, rows].astype(WIDE)
            if above:
                value = value + from_above[i, rows].astype(WIDE)
            result(i, rows, value)

        by_pieces(pieces, height, body)

    when(z == 0, lambda: finish(False, True))
    when((z > 0) & (z < last), lambda: finish(True, True))
    when(z == last, lambda: finish(True, False))
    for t in range(max(1, count - 2), count):
        when(sends_up(t), ups[t].wait_send)
        when(sends_down(t), downs[t].wait_send)


def line_buffers(count, pieces, height, width):
    return [pltpu.VMEM((slots, pieces, height, width), LOW) for slots in (count - 1, count - 1, 4)]


def token_scatter(links, place, partial, ours, theirs, buffers, result):
    out, loads = [], []
    for s in list(range(1, place.count)) + [0]:
        block = place.turn(place.dp - s)
        out.append(
            links.copy(partial.at[place.other, block], theirs.at[block], col=place.other)
        )
        out[-1].start()
        loads.append(links.keep(partial.at[place.col, block], ours.at[block]))
    waited = set()

    def ready(s):
        if s not in waited:
            waited.add(s)
            at = s - 1 if s else place.count - 1
            out[at].wait_recv()
            loads[at].wait()

    def term(block, i, rows):
        return ours[block, rows].astype(WIDE) + theirs[block, rows].astype(WIDE)

    yield 1
    yield from scatter_line(
        links, place, ready, term, *buffers, lambda i, rows, value: result(rows, value)
    )
    for copy in out:
        copy.wait_send()


def call(kernel, name, number, ins, outs, scratch, remote, local):
    return pl.pallas_call(
        kernel,
        in_specs=[VMEM if inside else ANY for _, inside in ins],
        out_specs=[VMEM if inside else ANY for _, _, inside in outs],
        out_shape=[jax.ShapeDtypeStruct(shape, kind) for shape, kind, _ in outs],
        scratch_shapes=list(scratch)
        + [
            pltpu.SemaphoreType.DMA((remote,)),
            pltpu.SemaphoreType.DMA((remote,)),
            pltpu.SemaphoreType.DMA((local,)),
        ],
        compiler_params=pltpu.CompilerParams(
            collective_id=number, has_side_effects=True, vmem_limit_bytes=58 * 1024 * 1024
        ),
        name=name,
    )(*[array for array, _ in ins])


def lanes(index, width):
    return pl.ds(pl.multiple_of(index * width, 128), width)


def strip(index, height, step=16):
    return pl.ds(pl.multiple_of(index * height, step), height)


def gather_inputs(
    count, x, cot, wxy, wout, wgate, wup, wdown, blk, cvec, wvec, x_all, cot_all, wxy_all, wout_all,
    gate_all, up_all, down_all, blk_all, cvec_all, wvec_all, send, recv, local,
):
    place = Place(count)
    links = Links(send, recv, local)
    row, z, col = place.row, place.dp, place.col
    greet(place, rows=True, line=True, cores=True)
    tall, wide = x.shape
    half, quarter = tall // 2, tall // 4
    down_halves = halves(wdown.shape[0])
    kept = []

    def keep(src, dst):
        kept.append(links.keep(src, dst))
        return kept[-1]

    def projections():
        mine = links.keep(wxy.at[row], wxy_all.at[row, z])
        yield from exchange_rows(
            links, place, lambda q: wxy.at[q], lambda q: wxy_all.at[q, z]
        )
        mine.wait()
        yield from gather_line(links, place, wxy_all.at[:, z], lambda b: wxy_all.at[:, b])

    def inputs():
        def at(q, core):
            return x_all.at[strip(core, tall), lanes(q, wide)]

        keep(x, at(row, col))
        shared = [links.copy(x, at(row, col), col=place.other)]
        shared[0].start()
        yield from gather_rows(
            links,
            place,
            lambda h: x.at[pl.ds(half * h, half)],
            lambda q, h: x_all.at[strip(2 * col + h, half), lanes(q, wide)],
        )
        for k in range(1, 4):
            q = place.near[k]
            shared.append(links.copy(at(q, col), at(q, col), col=place.other))
            shared[-1].start()
        yield 1
        for copy in shared:
            copy.wait_recv()
        for copy in shared:
            copy.wait_send()

    def channel_vectors():
        keep(cvec, cvec_all.at[z])
        yield from exchange_line(links, place, lambda b: cvec, lambda b: cvec_all.at[b])

    def width_vectors():
        mine = links.keep(wvec, wvec_all.at[row, z])
        yield from exchange_line(links, place, lambda b: wvec, lambda b: wvec_all.at[row, b])
        mine.wait()
        yield from exchange_rows(
            links, place, lambda q: wvec_all.at[row], lambda q: wvec_all.at[q]
        )

    def gate_blocks():
        mine = links.keep(blk, blk_all.at[z, row])
        yield from exchange_line(links, place, lambda b: blk, lambda b: blk_all.at[b, row])
        mine.wait()
        middle = count // 2
        yield from gather_rows(
            links,
            place,
            lambda h: blk_all.at[pl.ds(middle * h, middle), row],
            lambda q, h: blk_all.at[pl.ds(middle * h, middle), q],
        )

    def hidden_columns(matrix, whole):
        mine = links.keep(matrix.at[z], whole.at[row, z])
        yield from exchange_line(
            links, place, lambda b: matrix.at[b], lambda b: whole.at[row, b]
        )
        mine.wait()
        middle = count // 2
        yield from gather_rows(
            links,
            place,
            lambda h: whole.at[row, pl.ds(middle * h, middle)],
            lambda q, h: whole.at[q, pl.ds(middle * h, middle)],
        )

    def hidden_rows():
        keep(wdown, down_all.at[:, lanes(row, wide)])
        yield from gather_rows(
            links,
            place,
            lambda h: wdown.at[down_halves[h]],
            lambda q, h: down_all.at[down_halves[h], lanes(q, wide)],
        )

    def cotangents():
        def block(b):
            return cot_all.at[strip(col * count + b, quarter)]

        def spot(q):
            return cot_all.at[strip(col * count + z, quarter), lanes(q, wide)]

        mine = links.keep(cot.at[strip(row, quarter)], spot(row))
        yield from exchange_rows(links, place, lambda q: cot.at[strip(q, quarter)], spot)
        mine.wait()
        yield from gather_line(links, place, block(z), block, share=True)

    def output_rows():
        keep(wout, wout_all.at[z])
        yield from gather_line(links, place, wout, lambda b: wout_all.at[b])

    run(
        [
            projections(),
            inputs(),
            channel_vectors(),
            width_vectors(),
            gate_blocks(),
            hidden_columns(wgate, gate_all),
            hidden_columns(wup, up_all),
            cotangents(),
            hidden_rows(),
            output_rows(),
        ]
    )
    for copy in kept:
        copy.wait()


def spread_projected(count, proj, out, send, recv, local):
    place = Place(count)
    links = Links(send, recv, local)
    greet(place, rows=True)
    tall = out.shape[1]
    tokens = tall - 8

    def source(q):
        return proj.at[pl.ds(pl.multiple_of(q * tokens, 8), tall)]

    mine = links.keep(source(place.row), out.at[place.row])
    run([exchange_rows(links, place, source, lambda q: out.at[q])])
    mine.wait()


def combine(earlier, later):
    return (earlier[0] * later[0], later[0] * earlier[1] + later[1])


def scan_rows(decay, value, reverse):
    count = decay.shape[0]
    rows = lax.broadcasted_iota(jnp.int32, decay.shape, 0)
    reach = 1
    while reach < count:
        turn = count - reach if reverse else reach
        inside = rows < count - reach if reverse else rows >= reach
        decay_far = jnp.where(inside, pltpu.roll(decay, turn, 0), 1.0)
        value_far = jnp.where(inside, pltpu.roll(value, turn, 0), 0.0)
        value = decay * value_far + value
        decay = decay * decay_far
        reach *= 2
    return decay, value


def minus_expm1(v):
    series = 1.0 + v / 9.0
    for k in range(8, 1, -1):
        series = 1.0 + (v / k) * series
    return jnp.where(v > -0.5, -v * series, 1.0 - jnp.exp(v))


def each_head(heads, width, body):
    def lap(h, carry):
        body(h, pl.ds(pl.multiple_of(h * width, 128), width))
        return carry

    lax.fori_loop(0, heads, lap, 0)


def carry_over(links, place, ends, table, reverse):
    run([exchange_rows(links, place, lambda q: ends, lambda q: table.at[q])])
    row = place.row
    state = jnp.zeros((1, ends.shape[1]), WIDE)
    for k in range(4):
        q = 3 - k if reverse else k

        def entry(i):
            return table[q, i : i + 1, :]

        reached = q > row if reverse else q < row
        state = jnp.where(reached, entry(0) * state + entry(1), state)
    return state


def recurrence_forward(
    count, taps, proj, side, spots, vectors, blocks, conv_out, in_out, dec_out, state_out,
    entering_out, mixed_all, running, local_state, ends, table, mixed, send, recv, local,
):
    place = Place(count)
    links = Links(send, recv, local)
    greet(place, rows=True)
    tokens, width = side.shape
    heads, block = blocks.shape[0] // 2, blocks.shape[1]
    spot = spots[...]
    ends[...] = jnp.zeros(ends.shape, WIDE)
    entering_out[...] = jnp.zeros(ends.shape, WIDE)

    def one_head(h, at):
        def vector(i):
            return vectors[i : i + 1, at]

        conv = vector(taps) + vector(0) * (proj[8:, at] + vector(taps + 1))
        for k in range(1, taps):
            earlier = proj[8 - k : 8 - k + tokens, at] + vector(taps + 1)
            conv = conv + vector(k) * jnp.where(spot >= k, earlier, 0.0)
        conv_out[:, at] = conv
        low = conv.astype(LOW)
        input_gate = jax.nn.sigmoid(
            jnp.dot(low, blocks[h], preferred_element_type=WIDE) + vector(taps + 3)
        )
        decay_gate = jax.nn.sigmoid(
            jnp.dot(low, blocks[heads + h], preferred_element_type=WIDE) + vector(taps + 4)
        )
        in_out[:, at] = input_gate
        dec_out[:, at] = decay_gate
        log_decay = vector(taps + 5) * decay_gate
        starting = spot == 0
        decay = jnp.where(starting, 0.0, jnp.exp(log_decay))
        multiplier = jnp.where(starting, 1.0, jnp.sqrt(minus_expm1(2.0 * log_decay)))
        reach, state = scan_rows(decay, multiplier * input_gate * conv, False)
        running[:, at] = reach
        local_state[:, at] = state
        ends[0:1, at] = reach[tokens - 1 :, :]
        ends[1:2, at] = state[tokens - 1 :, :]

    each_head(heads, block, one_head)
    own = links.keep(ends, table.at[place.row])
    own.wait()
    entering_out[0:1, :] = carry_over(links, place, ends, table, False)

    def finish(h, at):
        state = local_state[:, at] + running[:, at] * entering_out[0:1, at]
        state_out[:, at] = state
        mixed[:, at] = (state * side[:, at]).astype(LOW)

    each_head(heads, block, finish)
    half = tokens // 2
    mine = links.keep(mixed, mixed_all.at[strip(place.row, tokens)])
    run(
        [
            gather_rows(
                links,
                place,
                lambda h: mixed.at[pl.ds(half * h, half)],
                lambda q, h: mixed_all.at[strip(2 * q + h, half)],
            )
        ]
    )
    mine.wait()


def recurrence_backward(
    count, taps, proj, side, spots, vectors, blocks, conv_in, in_gate, dec_gate, state_in, entering,
    grad_mixed, branch_out, sums_out, blocks_out, reach, local_grad, branch, ends, table, heads_in,
    heads_here, padded, spread, send, recv, local,
):
    place = Place(count)
    links = Links(send, recv, local)
    greet(place, rows=True)
    tokens, width = side.shape
    heads, block = blocks.shape[0] // 2, blocks.shape[1]
    spot = spots[...]
    starting = spot == 0
    ends[...] = jnp.zeros(ends.shape, WIDE)

    def backwards(h, at):
        rate = vectors[taps + 5 : taps + 6, at]
        decay = jnp.where(starting, 0.0, jnp.exp(rate * dec_gate[:, at]))
        padded[0:tokens, :] = decay
        padded[tokens:, :] = jnp.ones((8, block), WIDE)
        far, grad = scan_rows(padded[1 : tokens + 1, :], grad_mixed[:, at] * side[:, at], True)
        reach[:, at] = far
        local_grad[:, at] = grad
        ends[0:1, at] = decay[0:1, :] * far[0:1, :]
        ends[1:2, at] = decay[0:1, :] * grad[0:1, :]

    each_head(heads, block, backwards)
    own = links.keep(ends, table.at[place.row])
    own.wait()
    heads_here[0:1, :] = carry_over(links, place, ends, table, True)

    def one_head(h, at):
        def vector(i):
            return vectors[i : i + 1, at]

        grad_state = local_grad[:, at] + reach[:, at] * heads_here[0:1, at]
        padded[8:, :] = state_in[:, at]
        padded[7:8, :] = entering[0:1, at]
        grad_decay = grad_state * padded[7 : 7 + tokens, :]
        input_gate, decay_gate, conv = in_gate[:, at], dec_gate[:, at], conv_in[:, at]
        rate = vector(taps + 5)
        log_decay = rate * decay_gate
        decay = jnp.exp(log_decay)
        multiplier = jnp.where(starting, 1.0, jnp.sqrt(minus_expm1(2.0 * log_decay)))
        grad_gated = grad_state * conv
        grad_log = jnp.where(
            starting, 0.0, decay * (grad_decay - grad_gated * input_gate * (decay / multiplier))
        )
        grad_in = grad_gated * multiplier * (input_gate * (1.0 - input_gate))
        grad_gate = grad_log * decay_gate
        grad_dec = grad_gate * rate * (1.0 - decay_gate)
        low = conv.astype(LOW)
        low_in, low_dec = grad_in.astype(LOW), grad_dec.astype(LOW)
        across = (((1,), (1,)), ((), ()))
        along = (((0,), (0,)), ((), ()))
        grad_conv = (
            grad_state * multiplier * input_gate
            + lax.dot_general(low_in, blocks[h], across, preferred_element_type=WIDE)
            + lax.dot_general(low_dec, blocks[heads + h], across, preferred_element_type=WIDE)
        )
        blocks_out[h] = lax.dot_general(low, low_in, along, preferred_element_type=WIDE)
        blocks_out[heads + h] = lax.dot_general(low, low_dec, along, preferred_element_type=WIDE)
        spread[0:8, :] = jnp.zeros((8, block), WIDE)
        spread[8:, :] = vector(0) * grad_conv
        shift = vector(taps + 1)

        def total(values):
            return jnp.sum(values, axis=0, keepdims=True)

        sums_out[0:1, at] = total(grad_conv * (proj[8:, at] + shift))
        for k in range(1, taps):
            kept = jnp.where(spot >= k, grad_conv, 0.0)
            sums_out[k : k + 1, at] = total(kept * (proj[8 - k : 8 - k + tokens, at] + shift))
            spread[8 - k : 8 - k + tokens, :] += vector(k) * kept
        branch[:, at] = spread[8:, :]
        heads_in[0, :, at] = spread[0:8, :]
        sums_out[taps : taps + 1, at] = total(grad_conv)
        sums_out[taps + 1 : taps + 2, at] = total(spread[...])
        sums_out[taps + 2 : taps + 3, at] = total(grad_in)
        sums_out[taps + 3 : taps + 4, at] = total(grad_dec)
        sums_out[taps + 4 : taps + 5, at] = total(grad_gate)
        sums_out[taps + 5 :, at] = jnp.zeros((sums_out.shape[0] - taps - 5, block), WIDE)

    each_head(heads, block, one_head)
    row = place.row
    before = lax.rem(row + 3, 4)
    owed = links.copy(heads_in.at[0], heads_in.at[1], row=before)
    owed.start()
    owed.wait_recv()
    owed.wait_send()

    def finish(h, at):
        last = jnp.where(row < 3, heads_in[1, :, at], 0.0)
        branch[tokens - 8 :, at] += last
        branch_out[:, at] = branch[:, at].astype(LOW)

    each_head(heads, block, finish)


def output_and_norm(
    count, partial, x, vectors, middle_out, normed_all, mine, theirs, here, wide, normed, send,
    recv, local,
):
    place = Place(count)
    links = Links(send, recv, local)
    greet(place, rows=True, line=True, cores=True)
    row, z, col = place.row, place.dp, place.col
    tall, narrow = x.shape
    quarter = tall // 4
    other = links.copy(partial.at[strip(place.other, tall, 8)], theirs, col=place.other)
    other.start()
    load = links.keep(partial.at[strip(col, tall, 8)], mine)
    load.wait()
    other.wait_recv()

    def add(rows):
        here[rows] = mine[rows] + theirs[rows] + x[rows].astype(WIDE)

    by_rows(tall, add)

    def source(q):
        return here.at[strip(q, quarter)]

    own = links.keep(source(row), wide.at[:, lanes(row, narrow)])
    run([exchange_rows(links, place, source, lambda q: wide.at[:, lanes(q, narrow)])])
    own.wait()
    other.wait_send()
    shift, gain = vectors[1:2, :], vectors[3:4, :]
    full = wide.shape[1]

    def norm(rows):
        middle = wide[rows] + shift
        middle_out[rows] = middle
        mean = jnp.sum(middle * middle, axis=1, keepdims=True) / full
        normed[rows] = (middle * lax.rsqrt(mean + epsilon) * (1.0 + gain)).astype(LOW)

    by_rows(quarter, norm)

    def block(b):
        return normed_all.at[strip(col * count + b, quarter)]

    keep = links.keep(normed, block(z))
    run([gather_line(links, place, normed, block, share=True)])
    keep.wait()


def norm_rule(rows, grad, value, gain, sums, at):
    full = value.shape[1]
    inverse = lax.rsqrt(jnp.sum(value * value, axis=1, keepdims=True) / full + epsilon)
    scaled = grad * (1.0 + gain)
    inner = jnp.sum(scaled * value, axis=1, keepdims=True)
    sums[at : at + 1, :] += jnp.sum(grad * value * inverse, axis=0, keepdims=True)
    return inverse * scaled - value * (inverse * inverse * inverse) * (inner / full)


def second_norm_back(
    count, grad_partial, cot_all, middle, vectors, down_partial, grad_middle, grad_all, sums, down_out,
    ours, theirs, ups, downs, staging, cot, low, buffers, send, recv, local,
):
    place = Place(count)
    links = Links(send, recv, local)
    greet(place, rows=True, line=True, cores=True)
    row, z, col = place.row, place.dp, place.col
    quarter, full = middle.shape
    narrow = full // 4
    tall = 4 * quarter
    down_halves = halves(down_partial.shape[0])
    sums[...] = jnp.zeros(sums.shape, WIDE)
    gain = vectors[3:4, :]
    load = links.keep(cot_all.at[strip(col * count + z, quarter)], cot)

    def back(rows, grad):
        own = cot[rows].astype(WIDE)
        total = own + norm_rule(rows, grad, middle[rows], gain, sums, 0)
        sums[1:2, :] += jnp.sum(total, axis=0, keepdims=True)
        sums[2:3, :] += jnp.sum(own, axis=0, keepdims=True)
        grad_middle[rows] = total
        low[rows] = total.astype(LOW)

    def tokens():
        load.wait()
        yield from token_scatter(
            links, place, grad_partial, ours, theirs, (ups, downs, staging), back
        )

        def block(q):
            return grad_all.at[strip(4 * col + q, quarter)]

        mine = links.keep(low.at[:, lanes(row, narrow)], block(row))
        yield from exchange_rows(
            links, place, lambda q: low.at[:, lanes(q, narrow)], block
        )
        mine.wait()
        both = grad_all.at[strip(col, tall)]
        share = links.copy(both, both, col=place.other)
        share.start()
        yield 1
        share.wait_recv()
        share.wait_send()

    def keep_down(h, rows, value):
        down_out[pl.ds(pl.multiple_of(down_halves[h].start + rows.start, 16), rows.size)] = value

    run(
        [
            tokens(),
            scatter_rows(
                links,
                place,
                lambda q, h: down_partial.at[down_halves[h], lanes(q, narrow)],
                buffers,
                keep_down,
            ),
        ]
    )


def mixed_and_output(
    count, mixed_partial, out_partial, middle, vectors, gate_partial, mixed_out, layer_out, gate_out,
    mixed_buffers, ours, theirs, ups, downs, staging, low, gate_buffers, send, recv, local,
):
    place = Place(count)
    links = Links(send, recv, local)
    greet(place, rows=True, line=True, cores=True)
    row = place.row
    quarter, full = middle.shape
    narrow = full // 4
    shift = vectors[2:3, :]
    half = mixed_partial.shape[0] // 8
    gate_half = gate_partial.shape[0] // 8

    def keep_mixed(h, rows, value):
        mixed_out[h, rows] = value

    def keep_gate(h, rows, value):
        gate_out[h, rows] = value.astype(LOW)

    def finish(rows, value):
        low[rows] = (middle[rows] + value + shift).astype(LOW)

    def tokens():
        yield from token_scatter(
            links, place, out_partial, ours, theirs, (ups, downs, staging), finish
        )
        mine = links.keep(low.at[:, lanes(row, narrow)], layer_out.at[row])
        yield from exchange_rows(
            links, place, lambda q: low.at[:, lanes(q, narrow)], lambda q: layer_out.at[q]
        )
        mine.wait()

    run(
        [
            scatter_rows(
                links,
                place,
                lambda q, h: mixed_partial.at[strip(2 * q + h, half)],
                mixed_buffers,
                keep_mixed,
            ),
            tokens(),
            scatter_rows(
                links,
                place,
                lambda q, h: gate_partial.at[strip(2 * q + h, gate_half)],
                gate_buffers,
                keep_gate,
            ),
        ]
    )


def spread_gradients(
    count, blocks, up_partial, output_partial, gate_own, all_out, up_out, output_out, gate_out,
    up_buffers, ups, downs, staging, own, send, recv, local,
):
    place = Place(count)
    links = Links(send, recv, local)
    greet(place, rows=True, line=True)
    row, z = place.row, place.dp
    half = up_partial.shape[0] // 8
    mine = links.keep(blocks.at[row], all_out.at[row])
    kept = links.keep(gate_own.at[z], gate_out.at[z])
    load = links.keep(output_partial, own)

    def keep_up(h, rows, value):
        up_out[h, rows] = value.astype(LOW)

    def keep_output(i, rows, value):
        output_out[rows] = value

    def outputs():
        load.wait()
        yield from scatter_line(
            links,
            place,
            lambda s: None,
            lambda b, i, rows: own[b, rows].astype(WIDE),
            ups,
            downs,
            staging,
            keep_output,
        )

    run(
        [
            exchange_rows(links, place, lambda q: blocks.at[q], lambda q: all_out.at[q]),
            outputs(),
            exchange_line(
                links, place, lambda b: gate_own.at[b], lambda b: gate_out.at[b]
            ),
            scatter_rows(
                links,
                place,
                lambda q, h: up_partial.at[strip(2 * q + h, half)],
                up_buffers,
                keep_up,
            ),
        ]
    )
    mine.wait()
    kept.wait()


def first_norm_back(
    count, grad_partial, x_all, grad_middle, vectors, proj_partial, up_own, sums_in, channel_in,
    hidden_in, block_in, grad_out, proj_out, up_out, width_sums, channel_sums, block_out, hidden_sums,
    theirs, ours, added,
    row_buffer, x, result, sums, proj_own, proj_ups, proj_downs, proj_staging, proj_low, width_table,
    width_line, width_part, channel_table, channel_line, hidden_table, block_buffers, block_sum, block_ups, block_downs,
    block_staging, block_low, send, recv, local,
):
    place = Place(count)
    links = Links(send, recv, local)
    greet(place, rows=True, line=True, cores=True)
    row, z, col = place.row, place.dp, place.col
    quarter, full = grad_middle.shape
    narrow = full // 4
    gain = vectors[0:1, :]
    load_x = links.keep(x_all.at[strip(4 * col + row, quarter)], x)
    load_proj = [links.keep(proj_partial.at[:, b], proj_own.at[b]) for b in range(count)]
    kept = links.keep(up_own.at[z], up_out.at[z])

    def tokens():
        share = links.copy(grad_partial.at[place.other], theirs, col=place.other)
        share.start()
        load = links.keep(grad_partial.at[col], ours)
        yield 1
        share.wait_recv()
        load.wait()

        def add(rows):
            for q in range(4):
                total = ours[q, rows].astype(WIDE) + theirs[q, rows].astype(WIDE)
                added[q, rows] = total.astype(LOW)

        by_rows(quarter, add)
        load_x.wait()
        sums[0:3, :] = sums_in[0:3, :]
        sums[3:, :] = jnp.zeros((sums.shape[0] - 3, full), WIDE)
        half = quarter // 2

        def back(h, rows, grad):
            here = pl.ds(pl.multiple_of(rows.start + half * h, 16), rows.size)
            value = x[here].astype(WIDE)
            total = grad_middle[here] + norm_rule(rows, grad, value, gain, sums, 3)
            for q in range(4):
                result[q, here] = total[:, q * narrow : (q + 1) * narrow]

        yield from scatter_rows(
            links,
            place,
            lambda q, h: added.at[q, pl.ds(half * h, half)],
            row_buffer,
            back,
        )
        share.wait_send()
        mine = links.keep(result.at[row], grad_out.at[row])
        yield from exchange_rows(
            links, place, lambda q: result.at[q], lambda q: grad_out.at[q]
        )
        mine.wait()
        for q in range(4):
            width_part[q] = sums[:, q * narrow : (q + 1) * narrow]
        own = links.keep(width_part.at[row], width_table.at[row])
        yield from exchange_rows(
            links, place, lambda q: width_part.at[q], lambda q: width_table.at[q]
        )
        own.wait()
        width_line[z] = width_table[0] + width_table[1] + width_table[2] + width_table[3]
        yield from exchange_line(
            links, place, lambda b: width_line.at[z], lambda b: width_line.at[b]
        )
        total = width_line[0]
        for b in range(1, count):
            total = total + width_line[b]
        width_sums[0] = total
        yield 1
        last = links.copy(width_sums.at[0], width_sums.at[1], col=place.other)
        last.start()
        yield 1
        last.wait_recv()
        last.wait_send()

    def projections():
        for load in load_proj:
            load.wait()

        def keep_proj(i, rows, value):
            proj_low[i, rows] = value.astype(LOW)

        yield from scatter_line(
            links,
            place,
            lambda s: None,
            lambda b, i, rows: proj_own[b, i, rows].astype(WIDE),
            proj_ups,
            proj_downs,
            proj_staging,
            keep_proj,
        )
        mine = links.keep(proj_low.at[row], proj_out.at[row])
        yield from exchange_rows(
            links, place, lambda q: proj_low.at[q], lambda q: proj_out.at[q]
        )
        mine.wait()

    def hidden():
        own = links.keep(hidden_in, hidden_table.at[row])
        yield from exchange_rows(
            links, place, lambda q: hidden_in, lambda q: hidden_table.at[q]
        )
        own.wait()
        hidden_sums[...] = hidden_table[0] + hidden_table[1] + hidden_table[2] + hidden_table[3]

    def channels():
        own = links.keep(channel_in, channel_table.at[row])
        yield from exchange_rows(
            links, place, lambda q: channel_in, lambda q: channel_table.at[q]
        )
        own.wait()
        channel_line[z] = (
            channel_table[0] + channel_table[1] + channel_table[2] + channel_table[3]
        )
        yield from exchange_line(
            links, place, lambda b: channel_line.at[z], lambda b: channel_line.at[b]
        )
        total = channel_line[0]
        for b in range(1, count):
            total = total + channel_line[b]
        channel_sums[...] = total

    def blocks():
        def keep_rows(h, rows, value):
            block_sum[h, rows] = value

        yield from scatter_rows(
            links,
            place,
            lambda q, h: block_in.at[q, h],
            block_buffers,
            keep_rows,
        )
        length = block_sum.shape[1] * 2 // count
        middle = count // 2

        def term(b, i, rows):
            at = pl.multiple_of(lax.rem(b, middle) * length + rows.start, 8)
            return block_sum[lax.div(b, middle), pl.ds(at, rows.size)]

        def keep_line(i, rows, value):
            block_low[rows] = value.astype(LOW)

        yield from scatter_line(
            links, place, lambda s: None, term, block_ups, block_downs, block_staging, keep_line
        )
        mine = links.keep(block_low, block_out.at[row])
        yield from exchange_rows(links, place, lambda q: block_low, lambda q: block_out.at[q])
        mine.wait()

    run(
        [
            tokens(),
            projections(),
            exchange_line(links, place, lambda b: up_own.at[b], lambda b: up_out.at[b]),
            channels(),
            hidden(),
            blocks(),
        ]
    )
    kept.wait()


def times(piece, matrix):
    return jnp.dot(piece, matrix, preferred_element_type=WIDE)


def times_flipped(piece, matrix):
    return lax.dot_general(piece, matrix, (((1,), (1,)), ((), ())), preferred_element_type=WIDE)


def left_product(left, right):
    return lax.dot_general(left, right, (((0,), (0,)), ((), ())), preferred_element_type=WIDE)


def side_by_side(blocks):
    return jnp.concatenate([blocks[i] for i in range(blocks.shape[0])], axis=1)


def columns(matrix, parts):
    width = matrix.shape[1] // parts
    return jnp.stack([matrix[:, i * width : (i + 1) * width] for i in range(parts)])


def padded_rows(rows, height, width):
    return jnp.pad(rows, ((0, height - rows.shape[0]), (0, width - rows.shape[1])))


def round_up(size, step):
    return -(-size // step) * step


def shards(
    inputs,
    positions,
    branch_matrix,
    gelu_matrix,
    output_matrix,
    gate_matrix,
    up_matrix,
    down_matrix,
    input_blocks,
    decay_blocks,
    conv_taps,
    conv_bias,
    branch_bias,
    gelu_bias,
    input_bias,
    decay_bias,
    decay_param,
    output_bias,
    gate_bias,
    up_bias,
    down_bias,
    norm_first,
    norm_second,
    cotangent,
):
    count, rows_count, cores = lax.axis_size("dp"), lax.axis_size("row"), lax.axis_size("col")
    place_dp, place_row = lax.axis_index("dp"), lax.axis_index("row")
    tall, narrow = inputs.shape
    quarter, full, tokens = tall // rows_count, narrow * rows_count, tall * cores
    depth, width = branch_matrix.shape
    part = width // rows_count
    hidden_part = down_matrix.shape[0]
    heads, block_part, block = input_blocks.shape
    taps = conv_taps.shape[0]
    steps = positions.shape[0]
    share = block_part // rows_count
    remote, local = 64 + 24 * count, 40 + 6 * count

    wxy = jnp.concatenate(
        (columns(branch_matrix.astype(LOW), rows_count), columns(gelu_matrix.astype(LOW), rows_count)),
        axis=2,
    )
    blocks_low = jnp.concatenate((input_blocks, decay_blocks), axis=0).astype(LOW)
    blk = lax.dynamic_slice_in_dim(blocks_low, place_row * share, share, 1).reshape(
        2 * heads * share, block
    )
    channel_rows = jnp.concatenate(
        (
            conv_taps,
            jnp.stack((conv_bias, branch_bias, gelu_bias, input_bias, decay_bias, decay_param)),
        ),
        axis=0,
    )
    channel_size = channel_rows.shape[1]
    cvec = padded_rows(
        channel_rows.astype(LOW).astype(WIDE),
        round_up(taps + 6, 8),
        round_up(channel_size, 128),
    )
    wvec = padded_rows(
        jnp.stack((norm_first, output_bias, down_bias, norm_second)).astype(LOW).astype(WIDE),
        8,
        round_up(depth, 128),
    )
    x_all, cot_all, wxy_all, wout_all, gate_all, up_all, down_all, blk_all, cvec_all, wvec_all = call(
        functools.partial(gather_inputs, count),
        "gather_inputs",
        1,
        [
            (array, False)
            for array in (
                inputs,
                cotangent,
                wxy,
                output_matrix.astype(LOW),
                columns(gate_matrix.astype(LOW), count),
                columns(up_matrix.astype(LOW), count),
                down_matrix.astype(LOW),
                blk,
                cvec,
                wvec,
            )
        ],
        [
            ((tokens, full), LOW, False),
            ((cores * count * quarter, full), LOW, False),
            ((rows_count, count, depth, 2 * part), LOW, False),
            ((count,) + output_matrix.shape, LOW, False),
            ((rows_count, count, depth, hidden_part), LOW, False),
            ((rows_count, count, depth, hidden_part), LOW, False),
            ((hidden_part, full), LOW, False),
            ((count, rows_count) + blk.shape, LOW, False),
            ((count,) + cvec.shape, WIDE, False),
            ((rows_count, count) + wvec.shape, WIDE, False),
        ],
        [],
        remote,
        local,
    )
    wxy_all = wxy_all.reshape(full, 2 * part)
    wout_all = wout_all.reshape(width, narrow)
    gate_all = gate_all.reshape(full, hidden_part)
    up_all = up_all.reshape(full, hidden_part)
    blocks = (
        blk_all.reshape(count, rows_count, 2 * heads, share, block)
        .transpose(2, 0, 1, 3, 4)
        .reshape(2 * heads, block, block)
    )
    channel_all = side_by_side(cvec_all[:, : taps + 6, :channel_size])
    gelu_shift, decay_raw = channel_all[taps + 2], channel_all[taps + 5]
    vectors = jnp.concatenate(
        (channel_all[: taps + 5], -8.0 * jax.nn.softplus(decay_raw)[None, :]), axis=0
    )
    width_all = jnp.concatenate(
        [wvec_all[q, b, :, :depth] for q in range(rows_count) for b in range(count)], axis=1
    )

    resid = x_all.astype(WIDE)
    inverse = lax.rsqrt(jnp.mean(resid * resid, axis=1, keepdims=True) + epsilon)
    normed_first = (resid * inverse * (1.0 + width_all[0])).astype(LOW)
    projected = jnp.pad(times(normed_first, wxy_all), ((8, 0), (0, 0)))
    (projected_here,) = call(
        functools.partial(spread_projected, count),
        "spread_projected",
        2,
        [(projected, False)],
        [((rows_count, steps + 8, 2 * part), WIDE, False)],
        [],
        remote,
        local,
    )
    branch = side_by_side(projected_here[:, :, :part])
    gelu_in = side_by_side(projected_here[:, 8:, part:]) + gelu_shift
    side, gelu_pull = jax.vjp(jax.nn.gelu, gelu_in)

    spots = positions[:, None]
    wide_tokens = ((steps, width), WIDE, True)
    tokens_scratch = pltpu.VMEM((steps, width), WIDE)
    eight_rows = pltpu.VMEM((8, width), WIDE)
    table_rows = pltpu.VMEM((rows_count, 8, width), WIDE)
    conv, input_gate, decay_gate, state, entering, mixed_all = call(
        functools.partial(recurrence_forward, count, taps),
        "recurrence_forward",
        3,
        [(array, True) for array in (branch, side, spots, vectors, blocks)],
        [wide_tokens] * 4 + [((8, width), WIDE, True), ((tokens, width), LOW, False)],
        [
            tokens_scratch,
            tokens_scratch,
            eight_rows,
            table_rows,
            pltpu.VMEM((steps, width), LOW),
        ],
        remote,
        local,
    )

    middle, normed_second = call(
        functools.partial(output_and_norm, count),
        "output_and_norm",
        4,
        [(times(mixed_all, wout_all), False), (inputs, True), (width_all, True)],
        [((quarter, full), WIDE, True), ((cores * count * quarter, full), LOW, False)],
        [
            pltpu.VMEM((tall, narrow), WIDE),
            pltpu.VMEM((tall, narrow), WIDE),
            pltpu.VMEM((tall, narrow), WIDE),
            pltpu.VMEM((quarter, full), WIDE),
            pltpu.VMEM((quarter, full), LOW),
        ],
        remote,
        local,
    )

    def feed(gate_value, up_value):
        return jax.nn.gelu(gate_value) * up_value

    hidden_value, feed_pull = jax.vjp(
        feed,
        times(normed_second, gate_all) + gate_bias.astype(LOW).astype(WIDE),
        times(normed_second, up_all) + up_bias.astype(LOW).astype(WIDE),
    )
    hidden = hidden_value.astype(LOW)
    grad_gate, grad_up = feed_pull(times_flipped(cot_all, down_all))
    grad_gate_low, grad_up_low = grad_gate.astype(LOW), grad_up.astype(LOW)
    by_device = (cores, count, quarter, full)
    grad_normed_second = (
        (times_flipped(grad_gate_low, gate_all) + times_flipped(grad_up_low, up_all))
        .astype(LOW)
        .reshape(by_device)
    )
    down_partial = left_product(hidden, cot_all).astype(LOW)
    token_scratch = [
        pltpu.VMEM((count, quarter, full), LOW),
        pltpu.VMEM((count, quarter, full), LOW),
        *line_buffers(count, 1, quarter, full),
    ]
    token_low = pltpu.VMEM((quarter, full), LOW)
    grad_middle, grad_middle_all, width_sums, down_grad = call(
        functools.partial(second_norm_back, count),
        "second_norm_back",
        5,
        [
            (grad_normed_second, False),
            (cot_all, False),
            (middle, True),
            (width_all, True),
            (down_partial, False),
        ],
        [
            ((quarter, full), WIDE, True),
            ((tokens, narrow), LOW, False),
            ((8, full), WIDE, True),
            ((hidden_part, narrow), WIDE, True),
        ],
        token_scratch + [token_low, token_low, row_buffers(hidden_part, narrow)],
        remote,
        local,
    )
    gate_partial = left_product(normed_second, grad_gate_low).astype(LOW)
    up_partial = left_product(normed_second, grad_up_low).astype(LOW)
    forward_partial = times(hidden, down_all).astype(LOW).reshape(by_device)

    mixed_partial = times_flipped(grad_middle_all, wout_all).astype(LOW)
    output_partial = left_product(mixed_all, grad_middle_all).astype(LOW)
    grad_mixed, layer_out, gate_own = call(
        functools.partial(mixed_and_output, count),
        "mixed_and_output",
        6,
        [
            (mixed_partial, False),
            (forward_partial, False),
            (middle, True),
            (width_all, True),
            (gate_partial, False),
        ],
        [
            ((2, steps // 2, width), WIDE, True),
            ((rows_count, quarter, narrow), LOW, False),
            ((2, narrow // 2, hidden_part), LOW, True),
        ],
        [row_buffers(steps, width)]
        + token_scratch
        + [token_low, row_buffers(narrow, hidden_part)],
        remote,
        local,
    )
    grad_mixed = grad_mixed.reshape(steps, width)

    grad_gelu = gelu_pull(grad_mixed * state)[0]
    grad_branch_low, channel_part, block_sums = call(
        functools.partial(recurrence_backward, count, taps),
        "recurrence_backward",
        7,
        [
            (array, True)
            for array in (
                branch,
                side,
                spots,
                vectors,
                blocks,
                conv,
                input_gate,
                decay_gate,
                state,
                entering,
                grad_mixed,
            )
        ],
        [
            ((steps, width), LOW, True),
            ((round_up(taps + 6, 8), width), WIDE, True),
            ((2 * heads, block, block), WIDE, True),
        ],
        [
            tokens_scratch,
            tokens_scratch,
            tokens_scratch,
            eight_rows,
            table_rows,
            pltpu.VMEM((2, 8, width), WIDE),
            eight_rows,
            pltpu.VMEM((steps + 8, block), WIDE),
            pltpu.VMEM((steps + 8, block), WIDE),
        ],
        remote,
        local,
    )
    grad_gelu_low = grad_gelu.astype(LOW)
    projected_grads = jnp.concatenate(
        (columns(grad_branch_low, rows_count), columns(grad_gelu_low, rows_count)), axis=2
    )
    grad_projected, up_own, output_grad, gate_blocks = call(
        functools.partial(spread_gradients, count),
        "spread_gradients",
        8,
        [
            (projected_grads, False),
            (up_partial, False),
            (output_partial.reshape((count,) + output_matrix.shape), False),
            (gate_own.reshape(count, depth, hidden_part), False),
        ],
        [
            ((rows_count, steps, 2 * part), LOW, False),
            ((2, narrow // 2, hidden_part), LOW, True),
            (output_matrix.shape, WIDE, True),
            ((count, depth, hidden_part), LOW, False),
        ],
        [
            row_buffers(narrow, hidden_part),
            *line_buffers(count, 1, *output_matrix.shape),
            pltpu.VMEM((count,) + output_matrix.shape, LOW),
        ],
        remote,
        local,
    )
    grad_projected = grad_projected.reshape(tokens, 2 * part)
    proj_partial = left_product(normed_first, grad_projected).astype(LOW)
    grad_normed_first = times_flipped(grad_projected, wxy_all).astype(LOW)
    channel_part = channel_part.at[taps + 5].set(jnp.sum(grad_gelu, axis=0))
    hidden_part_sums = padded_rows(
        jnp.stack((jnp.sum(grad_gate, axis=0), jnp.sum(grad_up, axis=0))),
        8,
        round_up(hidden_part, 128),
    )
    block_in = (
        block_sums.astype(LOW)
        .reshape(2 * heads, count, rows_count, share, block)
        .transpose(2, 1, 0, 3, 4)
        .reshape(rows_count, 2, count // 2 * 2 * heads * share, block)
    )
    channel_shape, hidden_shape = channel_part.shape, hidden_part_sums.shape
    block_rows = 2 * heads * share
    input_grad, proj_grad, up_blocks, width_sums, channel_sums, block_grads, hidden_sums = call(
        functools.partial(first_norm_back, count),
        "first_norm_back",
        9,
        [
            (grad_normed_first.reshape(cores, rows_count, quarter, full), False),
            (x_all, False),
            (grad_middle, True),
            (width_all, True),
            (proj_partial.reshape(rows_count, count, depth, 2 * part), False),
            (up_own.reshape(count, depth, hidden_part), False),
            (width_sums, True),
            (channel_part, True),
            (hidden_part_sums, True),
            (block_in, False),
        ],
        [
            ((rows_count, quarter, narrow), WIDE, False),
            ((rows_count, depth, 2 * part), LOW, False),
            ((count, depth, hidden_part), LOW, False),
            ((2, 8, narrow), WIDE, True),
            (channel_shape, WIDE, True),
            ((rows_count, block_rows, block), LOW, False),
            (hidden_shape, WIDE, True),
        ],
        [
            pltpu.VMEM((rows_count, quarter, full), LOW),
            pltpu.VMEM((rows_count, quarter, full), LOW),
            pltpu.VMEM((rows_count, quarter, full), LOW),
            row_buffers(quarter, full),
            token_low,
            pltpu.VMEM((rows_count, quarter, narrow), WIDE),
            pltpu.VMEM((8, full), WIDE),
            pltpu.VMEM((count, rows_count, depth, 2 * part), LOW),
            *line_buffers(count, rows_count, depth, 2 * part),
            pltpu.VMEM((rows_count, depth, 2 * part), LOW),
            pltpu.VMEM((rows_count, 8, narrow), WIDE),
            pltpu.VMEM((count, 8, narrow), WIDE),
            pltpu.VMEM((rows_count, 8, narrow), WIDE),
            pltpu.VMEM((rows_count,) + channel_shape, WIDE),
            pltpu.VMEM((count,) + channel_shape, WIDE),
            pltpu.VMEM((rows_count,) + hidden_shape, WIDE),
            row_buffers(2 * block_in.shape[2], block),
            pltpu.VMEM((2, block_in.shape[2], block), WIDE),
            *line_buffers(count, 1, block_rows, block),
            pltpu.VMEM((block_rows, block), LOW),
        ],
        remote,
        local,
    )
    branch_grad = side_by_side(proj_grad[:, :, :part]).astype(WIDE)
    gelu_grad = side_by_side(proj_grad[:, :, part:]).astype(WIDE)
    block_grads = (
        block_grads.reshape(rows_count, 2 * heads, share, block)
        .transpose(1, 0, 2, 3)
        .reshape(2 * heads, block_part, block)
        .astype(WIDE)
    )
    channel_sums = lax.dynamic_slice_in_dim(channel_sums, place_dp * channel_size, channel_size, 1)
    width_sums = lax.dynamic_slice_in_dim(
        width_sums[0] + width_sums[1], place_dp * depth, depth, 1
    )
    decay_raw_here = lax.dynamic_slice_in_dim(decay_raw, place_dp * channel_size, channel_size, 0)
    decay_param_grad = -8.0 * channel_sums[taps + 4] * jax.nn.sigmoid(decay_raw_here)

    return (
        layer_out.reshape(tall, narrow),
        input_grad.reshape(tall, narrow),
        branch_grad,
        gelu_grad,
        output_grad,
        side_by_side(gate_blocks).astype(WIDE),
        side_by_side(up_blocks).astype(WIDE),
        down_grad,
        block_grads[:heads],
        block_grads[heads:],
        channel_sums[:taps],
        channel_sums[taps],
        channel_sums[taps + 1],
        channel_sums[taps + 5],
        channel_sums[taps + 2],
        channel_sums[taps + 3],
        decay_param_grad,
        width_sums[1],
        hidden_sums[0, :hidden_part],
        hidden_sums[1, :hidden_part],
        width_sums[2],
        width_sums[3],
        width_sums[0],
    )


def solution(mesh):
    in_specs = (
        P(("dp", "col"), "row"),
        P(("dp", "row")),
        P(("row", "dp"), "col"),
        P(("row", "dp"), "col"),
        P(("col", "dp"), "row"),
        P(("row", "dp"), "col"),
        P(("row", "dp"), "col"),
        P(("col", "dp"), "row"),
        P("col", "dp", None),
        P("col", "dp", None),
        P(None, ("col", "dp")),
        P(("col", "dp")),
        P(("col", "dp")),
        P(("col", "dp")),
        P(("col", "dp")),
        P(("col", "dp")),
        P(("col", "dp")),
        P(("row", "dp")),
        P(("col", "dp")),
        P(("col", "dp")),
        P(("row", "dp")),
        P(("row", "dp")),
        P(("row", "dp")),
        P(("dp", "col"), "row"),
    )
    out_specs = (
        P(("dp", "col"), "row"),
        P(("dp", "col"), "row"),
        P(("row", "dp"), "col"),
        P(("row", "dp"), "col"),
        P(("col", "dp"), "row"),
        P(("row", "dp"), "col"),
        P(("row", "dp"), "col"),
        P(("col", "dp"), "row"),
        P("col", "dp", None),
        P("col", "dp", None),
        P(None, ("col", "dp")),
        P(("col", "dp")),
        P(("col", "dp")),
        P(("col", "dp")),
        P(("col", "dp")),
        P(("col", "dp")),
        P(("col", "dp")),
        P(("row", "dp")),
        P(("col", "dp")),
        P(("col", "dp")),
        P(("row", "dp")),
        P(("row", "dp")),
        P(("row", "dp")),
    )
    return jax.shard_map(shards, mesh=mesh, in_specs=in_specs, out_specs=out_specs, check_vma=False)
```

time: 2700 us -> 941 us (0.35)
  waiting for transfers between devices: 1950 us -> 0 us
  Pallas kernels: 0 us -> 727 us
  local copies, waits for them, and re-layouts: 284 us -> 51.3 us
  blocking collectives: 153 us -> 0 us
  other arithmetic: 126 us -> 27 us
    reduce_scatter x16 -> x0, waiting for transfers between devices: 1200 us -> none  [the longest x4 501 us: reduce_row(): lax.psum_scatter(term(jnp.int32(0), lax.axis_size('row') * rows_here), 'r...]
    pallas_call x0 -> x9, Pallas kernels: none -> 727 us  [call(): pl.pallas_call(kernel, in_specs=[VMEM if inside else ANY for _, inside in...]
    all_gather x14 -> x0, waiting for transfers between devices: 643 us -> none  [the longest x4 318 us: spread_row(): return lax.all_gather(values, 'row', axis=0, tiled=True)]
    slice x114 -> x7, local copies, waits for them, and re-layouts: 163 us -> 4.95 us  [the longest x1 1.44 us: shards(): hidden_sums[1, :hidden_part]]
    all_gather x7 -> x0, blocking collectives: 79.6 us -> none  [the longest x4 32 us: entering(): everything = jax.tree.map(lambda part: lax.all_gather(part, axis), shard)]
    unnamed x35 -> x0, waiting for transfers between devices: 53 us -> none
    psum x5 -> x0, blocking collectives: 51.6 us -> none  [the longest x4 48.6 us: row_total(): return lax.psum(values, 'row')]
    psum x1 -> x0, waiting for transfers between devices: 51.4 us -> none  [shards(): lax.psum((tap_grad, conv_bias_grad, branch_bias_grad, gelu_bias_grad, inp...]
  transfers between devices with their start and end apart: 35 -> 0, of which waited for: 32 -> 0; matrix products, arithmetic and copies ran while one was open for 12% -> 0% of each run, Pallas kernels for 0% -> 0%
where the time goes in v2:
time: 941 us; the launch traced here: 936 us
  Pallas kernels  727 us (77%)
  matrix products  129 us (14%)
  local copies, waits for them, and re-layouts  51.3 us (5%)
  other arithmetic  27 us (3%)
    pallas_call x9, Pallas kernels, call(): pl.pallas_call(kernel, in_specs=[VMEM if inside else ANY for _, inside in...  727 us
    dot_general x5, matrix products, times(): return jnp.dot(piece, matrix, preferred_element_type=WIDE)  48 us
    dot_general x5, matrix products, times_flipped(): lax.dot_general(piece, matrix, (((1,), (1,)), ((), ())), preferred_elemen...  45.5 us
    dot_general x5, matrix products, left_product(): lax.dot_general(left, right, (((0,), (0,)), ((), ())), preferred_element_...  35.8 us

profile of v2, /device:TPU:0, one launch (start us, length us, event | category | flops | bytes accessed | tf_op | source)
XLA Modules:
  0.0 936.1 jit_solution(9413000924035715859)
XLA Ops:
  1.9 1.3 convert_element_type.113
  7.5 1.9 pad_maximum_fusion
  13.5 200.2 %gather_inputs.1 = (bf16[1024,2560]{1,0:T(8,128)(2,1)}, bf16[1024,2560]{1,0:T(8,128)(2,1)}, bf16[4,4,160,640]{3,2,1,0:T(8,128)(2,1)}, bf16[4,320,640]{2,1,0:T(8,...) custom-call(bf16[512,640]{1,0:T(8,128)(2,1)} %x.11, ...), custom_call_target="tpu_custom_call" | custom-call | tf_op jit(solution)/shard_map/gather_inputs/pallas_call | solution.py:367
  213.8 10.2 %fusion.47 = f32[1024,960]{0,1:T(8,128)} fusion(bf16[1024,2560]{1,0:T(8,128)(2,1)} %get-tuple-element.74.cot_all, bf16[960,2560]{1,0:T(8,128)(2,1)} %get-tuple-element.75), kind=kOutput, calls=%fused_computation.160 | convolution fusion | flops 5033164800 | bytes 14090240 | tf_op jit(solution)/shard_map/dot_general | solution.py:1149
  224.2 3.7 fusion
  228.2 6.3 fusion.10
  234.5 1.7 pad.26.proj
  236.1 36.7 %spread_projected.1 = f32[4,264,640]{2,1,0:T(8,128)} custom-call(f32[1032,640]{1,0:T(8,128)} %pad.26.proj), custom_call_target="tpu_custom_call" | custom-call | tf_op jit(solution)/shard_map/spread_projected/pallas_call | solution.py:367
  272.8 2.5 slice_bitcast_fusion
  275.3 2.3 concatenate.47.proj
  277.6 1.3 slice_bitcast_fusion.4
  278.9 1.6 concatenate.48
  281.5 1.5 multiply_multiply_fusion.5.side
  284.4 1.3 copy.61
  285.7 41.4 %recurrence_forward.1 = (f32[256,1280]{1,0:T(8,128)}, f32[256,1280]{1,0:T(8,128)}, f32[256,1280]{1,0:T(8,128)}, f32[256,1280]{1,0:T(8,128)}, f32[8,1280]{1,0:T(8,128)}, /*index=5*/bf16[1024,1280]{1,0:T(8,128)(2,1)}) custom-call(f32[264,1280]{1,0:T(8,128)} %concatenate.47.proj, f32[256,1280]{1,0:T(8,128)} %multiply_multiply_fusion.5.side, ...), custom_call_target="tpu_custom_call" | custom-call | tf_op jit(solution)/shard_map/recurrence_forward/pallas_call | solution.py:367
  327.1 5.4 fusion.48.partial
  332.6 76.6 %output_and_norm.1 = (f32[128,2560]{1,0:T(8,128)}, bf16[1024,2560]{1,0:T(8,128)(2,1)}) custom-call(f32[1024,640]{1,0:T(8,128)} %fusion.48.partial, bf16[512,640]{1,0:T(8,128)(2,1)} %x.11, f32[8,2560]{1,0:T(8,128)} %copy-done.8), custom_call_target="tpu_custom_call" | custom-call | tf_op jit(solution)/shard_map/output_and_norm/pallas_call | solution.py:367
  409.2 10.3 %fusion.49 = f32[1024,960]{0,1:T(8,128)} fusion(bf16[1024,2560]{1,0:T(8,128)(2,1)} %get-tuple-element.83, bf16[2560,960]{1,0:T(8,128)(2,1)} %bitcast.239), kind=kOutput, calls=%fused_computation.162 | convolution fusion | flops 5033164800 | bytes 14090240 | tf_op jit(solution)/shard_map/dot_general | solution.py:1145
  419.5 15.9 %fusion.38 = (f32[960]{0:T(1024)S(1)}, bf16[1024,960]{0,1:T(8,128)(2,1)}, bf16[1024,960]{0,1:T(8,128)(2,1)}, f32[960]{0:T(1024)S(1)}, bf16[1024,960]{0,1:T(8,128)(2,1)}) fusion(f32[960]{0:T(1024)S(1)} %get-tuple-element.213, f32[1024,960]{0,1:T(8,128)} %fusion.47, f32[1024,960]{0,1:T(8,128)} %fusion.49, f32[960]{0:T(1024)S(1)} %get-tuple-element.214, ...), kind=kOutput, calls=%fused_computation.153 | convolution fusion | flops 5062653952 | bytes 23936000 | tf_op jit(solution)/shard_map/dot_general | solution.py:1145
  435.4 11.6 %fusion.19 = f32[1024,2560]{1,0:T(8,128)} fusion(bf16[2560,960]{1,0:T(8,128)(2,1)} %bitcast.244, bf16[1024,960]{0,1:T(8,128)(2,1)} %get-tuple-element.120), kind=kOutput, calls=%fused_computation.40 | convolution fusion | flops 5033164800 | bytes 17367040 | tf_op jit(solution)/shard_map/dot_general | solution.py:1149
  447.0 10.9 %add_convert_fusion = bf16[1024,2560]{1,0:T(8,128)(2,1)} fusion(f32[1024,2560]{1,0:T(8,128)} %fusion.19, bf16[1024,960]{0,1:T(8,128)(2,1)} %get-tuple-element.125, bf16[2560,960]{1,0:T(8,128)(2,1)S(1)} %bitcast.242), kind=kOutput, calls=%fused_computation.5 | convolution fusion | flops 5038407680 | bytes 22609920 | tf_op jit(solution)/shard_map/dot_general | solution.py:1149
  458.0 8.5 convolution_convert_fusion.4.down_partial
  466.5 72.9 %second_norm_back.1 = (f32[128,2560]{1,0:T(8,128)}, bf16[1024,640]{1,0:T(8,128)(2,1)}, f32[8,2560]{1,0:T(8,128)}, f32[960,640]{1,0:T(8,128)}) custom-call(bf16[2,4,128,2560]{3,2,1,0:T(8,128)(2,1)} %bitcast.214, bf16[1024,2560]{1,0:T(8,128)(2,1)} %get-tuple-element.74.cot_all, f32[128,2560]{1,0:T(8,128)} %get-tuple-element.86.middle, f32[8,2560]{1,0:T(8,128)} %copy-done.8, ...), custom_call_target="tpu_custom_call" | custom-call | tf_op jit(solution)/shard_map/second_norm_back/pallas_call | solution.py:367
  539.4 5.2 convolution_convert_fusion.6.mixed_partial
  544.7 10.1 %convolution_convert_fusion.1 = bf16[1024,2560]{1,0:T(8,128)(2,1)} fusion(bf16[1024,960]{0,1:T(8,128)(2,1)S(1)} %copy-done.38, bf16[960,2560]{1,0:T(8,128)(2,1)} %get-tuple-element.75), kind=kOutput, calls=%fused_computation.7 | convolution fusion | flops 5035786240 | bytes 12124160 | tf_op jit(solution)/shard_map/dot_general | solution.py:1145
  554.8 7.0 convolution_convert_fusion.3
  561.7 7.8 copy.63.gate_partial
  569.6 84.1 %mixed_and_output.1 = (f32[2,128,1280]{2,1,0:T(8,128)}, bf16[4,128,640]{2,1,0:T(8,128)(2,1)}, bf16[2,320,960]{2,1,0:T(8,128)(2,1)}) custom-call(bf16[1024,1280]{1,0:T(8,128)(2,1)} %convolution_convert_fusion.6.mixed_partial, bf16[2,4,128,2560]{3,2,1,0:T(8,128)(2,1)} %bitcast.215, f32[128,2560]{1,0:T(8,128)} %get-tuple-element.86.middle, ...), custom_call_target="tpu_custom_call" | custom-call | tf_op jit(solution)/shard_map/mixed_and_output/pallas_call | solution.py:367
  653.7 2.3 fusion.40
  656.2 30.3 %recurrence_backward.1 = (bf16[256,1280]{1,0:T(8,128)(2,1)}, f32[16,1280]{1,0:T(8,128)}, f32[10,256,256]{2,1,0:T(8,128)}) custom-call(f32[264,1280]{1,0:T(8,128)} %concatenate.47.proj, f32[256,1280]{1,0:T(8,128)} %multiply_multiply_fusion.5.side, s32[256,1]{1,0:T(8,128)} %copy.62.spots, f32[10,1280]{1,0:T(8,128)} %pad_maximum_fusion.2.vectors, ...), custom_call_target="tpu_custom_call" | custom-call | tf_op jit(solution)/shard_map/recurrence_backward/pallas_call | solution.py:367
  686.5 1.6 slice_bitcast_fusion.31
  688.1 1.5 maximum_maximum_fusion.blocks
  689.6 9.3 convolution_convert_fusion.2
  699.0 8.0 copy.65.up_partial
  707.0 4.7 convolution_convert_fusion.7
  711.7 61.4 %spread_gradients.1 = (bf16[4,256,640]{2,1,0:T(8,128)(2,1)}, bf16[2,320,960]{2,1,0:T(8,128)(2,1)}, f32[320,640]{1,0:T(8,128)}, bf16[4,160,960]{2,1,0:T(8,128)(2,1)}) custom-call(bf16[4,256,640]{2,1,0:T(8,128)(2,1)} %maximum_maximum_fusion.blocks, bf16[2560,960]{1,0:T(8,128)(2,1)} %copy.65.up_partial, bf16[4,320,640]{2,1,0:T(8,128)(2,1)} %bitcast.219, ...), custom_call_target="tpu_custom_call" | custom-call | tf_op jit(solution)/shard_map/spread_gradients/pallas_call | solution.py:367
  773.1 7.6 convolution_convert_fusion
  780.7 6.3 convolution_convert_fusion.5
  787.0 1.4 scatter.4.channel_in
  790.4 123.2 %first_norm_back.1 = (f32[4,128,640]{2,1,0:T(8,128)}, bf16[4,160,640]{2,1,0:T(8,128)(2,1)}, bf16[4,160,960]{2,1,0:T(8,128)(2,1)}, f32[2,8,640]{2,1,0:T(8,128)}, ...) custom-call(bf16[2,4,128,2560]{3,2,1,0:T(8,128)(2,1)} %bitcast.213, ...), custom_call_target="tpu_custom_call" | custom-call | tf_op jit(solution)/shard_map/first_norm_back/pallas_call | solution.py:367
  913.6 1.5 slice_bitcast_fusion.40
  917.5 1.4 slice_bitcast_fusion.20
  920.1 1.6 convert_element_type.141
  923.3 1.6 convert_element_type.142
  926.5 1.4 constant_dynamic-slice_fusion
  927.9 1.6 fusion.37
  930.1 1.4 fusion.45
  934.4 1.4 copy.77
  (170 shorter events, 24.7 us)
Async XLA Ops:
  1.8 2.7 copy-start.12
  3.1 2.2 copy-start.4
  7.5 2.6 copy-start.6
  9.4 1.9 copy-start.15
  9.4 1.9 copy-start.16
  9.4 2.6 copy-start.20
  9.4 2.6 copy-start.23
  9.4 2.6 copy-start.24
  9.4 2.6 copy-start.25
  9.4 2.6 copy-start.26
  9.4 2.7 copy-start.27
  9.4 2.7 copy-start.28
  9.4 3.4 copy-start.34
  9.4 3.4 copy-start.35
  9.5 3.4 copy-start.36
  9.5 3.4 copy-start.37
  13.5 200.2 %copy-start.21 = (f32[960]{0:T(1024)S(1)}, f32[960]{0:T(1024)}, u32[]{:S(2)}) copy-start(f32[960]{0:T(1024)} %param.44) | copy-start | bytes 11524
  13.5 200.2 %copy-start.22 = (f32[960]{0:T(1024)S(1)}, f32[960]{0:T(1024)}, u32[]{:S(2)}) copy-start(f32[960]{0:T(1024)} %param.45) | copy-start | bytes 11524
  213.8 10.2 %copy-start.18 = (f32[4,4,8,256]{3,2,1,0:T(8,128)S(1)}, f32[4,4,8,256]{3,2,1,0:T(8,128)}, u32[]{:S(2)}) copy-start(f32[4,4,8,256]{3,2,1,0:T(8,128)} %get-tuple-element.77) | copy-start | bytes 393220
  224.1 3.8 copy-start.8
  224.2 4.0 copy-start
  272.8 4.8 copy-start.1
  278.9 4.0 copy-start.29
  278.9 5.5 copy-start.10
  285.7 41.4 %copy-start.32 = (bf16[4,320,640]{2,1,0:T(8,128)(2,1)S(1)}, bf16[4,320,640]{2,1,0:T(8,128)(2,1)}, u32[]{:S(2)}) copy-start(bf16[4,320,640]{2,1,0:T(8,128)(2,1)} %get-tuple-element.82) | copy-start | bytes 4915204
  409.2 37.8 %slice-start.4 = ((s8[5242880]{0:T(1024)(128)(4,1)}), s8[4194304]{0:T(1024)(128)(4,1)S(1)}, s32[]{:S(2)}) async-start(s8[5242880]{0:T(1024)(128)(4,1)} %bitcast.240), calls=%async_computation.4 | async-start | bytes 8388608
  419.5 27.6 %slice-start.5 = ((s8[5242880]{0:T(1024)(128)(4,1)}), s8[1048576]{0:T(1024)(128)(4,1)S(1)}, s32[]{:S(2)}) async-start(s8[5242880]{0:T(1024)(128)(4,1)} %bitcast.240), calls=%async_computation.5 | async-start | bytes 2097152
  435.4 22.5 %slice-start.2 = ((s8[5242880]{0:T(1024)(128)(4,1)}), s8[4194304]{0:T(1024)(128)(4,1)S(1)}, s32[]{:S(2)}) async-start(s8[5242880]{0:T(1024)(128)(4,1)} %bitcast.211), calls=%async_computation.2 | async-start | bytes 8388608
  447.0 10.9 %slice-start.3 = ((s8[5242880]{0:T(1024)(128)(4,1)}), s8[1048576]{0:T(1024)(128)(4,1)S(1)}, s32[]{:S(2)}) async-start(s8[5242880]{0:T(1024)(128)(4,1)} %bitcast.211), calls=%async_computation.3 | async-start | bytes 2097152
  539.4 5.3 copy-start.38
  539.4 15.3 %slice-start.6 = ((s8[5242880]{0:T(1024)(128)(4,1)}), s8[4194304]{0:T(1024)(128)(4,1)S(1)}, s32[]{:S(2)}) async-start(s8[5242880]{0:T(1024)(128)(4,1)} %bitcast.245), calls=%async_computation.6 | async-start | bytes 8388608
  544.7 10.1 %slice-start.7 = ((s8[5242880]{0:T(1024)(128)(4,1)}), s8[1048576]{0:T(1024)(128)(4,1)S(1)}, s32[]{:S(2)}) async-start(s8[5242880]{0:T(1024)(128)(4,1)} %bitcast.245), calls=%async_computation.7 | async-start | bytes 2097152
  544.7 10.1 %copy-start.40 = (bf16[1024,960]{0,1:T(8,128)(2,1)S(1)}, bf16[1024,960]{0,1:T(8,128)(2,1)}, u32[]{:S(2)}) copy-start(bf16[1024,960]{0,1:T(8,128)(2,1)} %get-tuple-element.120) | copy-start | bytes 5898244
  569.6 84.1 %copy-start.2 = (f32[256,1280]{1,0:T(8,128)S(1)}, f32[256,1280]{1,0:T(8,128)}, u32[]{:S(2)}) copy-start(f32[256,1280]{1,0:T(8,128)} %get-tuple-element.92.state_in) | copy-start | bytes 3932164
  686.5 3.1 copy-start.39
  699.0 8.0 copy-start.31
  711.7 61.4 %copy-start.30 = (bf16[4,4,160,640]{3,2,1,0:T(8,128)(2,1)S(1)}, bf16[4,4,160,640]{3,2,1,0:T(8,128)(2,1)}, u32[]{:S(2)}) copy-start(bf16[4,4,160,640]{3,2,1,0:T(8,128)(2,1)} %get-tuple-element.78) | copy-start | bytes 9830404
  711.7 69.0 %slice-start = ((s8[5242880]{0:T(1024)(128)(4,1)}), s8[1048576]{0:T(1024)(128)(4,1)S(1)}, s32[]{:S(2)}) async-start(s8[5242880]{0:T(1024)(128)(4,1)} %bitcast.206), calls=%async_computation | async-start | bytes 2097152
  773.1 7.6 slice-start.1
  773.1 7.6 copy-start.33
  780.7 8.4 copy-start.3
  920.1 1.8 copy-start.11
  922.0 2.8 copy-start.17
  924.9 4.6 copy-start.19
  924.9 6.7 copy-start.14
  924.9 7.5 copy-start.9
  925.0 8.5 copy-start.13
  931.6 2.8 copy-start.7
  (1 other events, 1.7 us)

commit v3 on v2

--- a/solution.py
+++ b/solution.py
@@ -8,6 +8,8 @@
 from jax.sharding import PartitionSpec as P
 
 epsilon = 1e-06
+ROOT = (2.0 / 3.141592653589793) ** 0.5
+CUBE = 0.044715
 LOW = jnp.bfloat16
 WIDE = jnp.float32
 MESH = pl.DeviceIdType.MESH
@@ -36,6 +38,21 @@
         copy = pltpu.make_async_copy(src, dst, self.local.at[k])
         copy.start()
         return copy
+
+
+class Relay:
+    def __init__(self, links, src, buffer, dst):
+        self.links, self.buffer, self.dst, self.store = links, buffer, dst, None
+        self.load = links.keep(src, buffer)
+
+    def pass_on(self):
+        if self.store is None:
+            self.load.wait()
+            self.store = self.links.keep(self.buffer, self.dst)
+
+    def wait(self):
+        self.pass_on()
+        self.store.wait()
 
 
 class Place:
@@ -199,6 +216,54 @@
         when(valid, copy.wait_send)
 
 
+class LineGather:
+    def __init__(self, links, place, own, piece):
+        self.links, self.place, self.own, self.piece = links, place, own, piece
+        self.ups, self.downs, self.shared = [None], [None], []
+
+    def send(self, step):
+        z, count, turn = self.place.dp, self.place.count, self.place.turn
+        low, high = turn(z - step + 1), turn(z + step - 1)
+        for copies, block, target, valid in (
+            (self.ups, low, turn(z + 1), (z >= step - 1) & (z < count - 1)),
+            (self.downs, high, turn(z - 1), (z <= count - step) & (z > 0)),
+        ):
+            source = self.own if step == 1 else self.piece(block)
+            copy = self.links.copy(source, self.piece(block), dp=target)
+            copies.append((copy, valid))
+            when(valid, copy.start)
+
+    def share(self, blocks, own=None):
+        out = []
+        for block, valid in blocks:
+            source = self.piece(block) if own is None else own
+            copy = self.links.copy(source, self.piece(block), col=self.place.other)
+            when(valid, copy.start)
+            out.append((copy, valid))
+        self.shared.append(out)
+
+    def start(self):
+        self.send(1)
+        self.share([(self.place.dp, self.place.dp >= 0)], self.own)
+
+    def step(self, step):
+        z, count, turn = self.place.dp, self.place.count, self.place.turn
+        below, above = z >= step, z <= count - 1 - step
+        when(below, self.ups[step][0].wait_recv)
+        when(above, self.downs[step][0].wait_recv)
+        if step < count - 1:
+            self.send(step + 1)
+        self.share([(turn(z - step), below), (turn(z + step), above)])
+
+    def ready(self, step):
+        for copy, valid in self.shared[step]:
+            when(valid, copy.wait_recv)
+
+    def close(self):
+        for copy, valid in self.ups[1:] + self.downs[1:] + sum(self.shared, []):
+            when(valid, copy.wait_send)
+
+
 def scatter_rows(links, place, part, buffers, result):
     row, near, side, far = place.near
     heights = [part(row, h).shape[0] for h in range(2)]
@@ -339,10 +404,10 @@
     for s in list(range(1, place.count)) + [0]:
         block = place.turn(place.dp - s)
         out.append(
-            links.copy(partial.at[place.other, block], theirs.at[block], col=place.other)
+            links.copy(partial.at[block, place.other], theirs.at[block], col=place.other)
         )
         out[-1].start()
-        loads.append(links.keep(partial.at[place.col, block], ours.at[block]))
+        loads.append(links.keep(partial.at[block, place.col], ours.at[block]))
     waited = set()
 
     def ready(s):
@@ -390,150 +455,6 @@
     return pl.ds(pl.multiple_of(index * height, step), height)
 
 
-def gather_inputs(
-    count, x, cot, wxy, wout, wgate, wup, wdown, blk, cvec, wvec, x_all, cot_all, wxy_all, wout_all,
-    gate_all, up_all, down_all, blk_all, cvec_all, wvec_all, send, recv, local,
-):
-    place = Place(count)
-    links = Links(send, recv, local)
-    row, z, col = place.row, place.dp, place.col
-    greet(place, rows=True, line=True, cores=True)
-    tall, wide = x.shape
-    half, quarter = tall // 2, tall // 4
-    down_halves = halves(wdown.shape[0])
-    kept = []
-
-    def keep(src, dst):
-        kept.append(links.keep(src, dst))
-        return kept[-1]
-
-    def projections():
-        mine = links.keep(wxy.at[row], wxy_all.at[row, z])
-        yield from exchange_rows(
-            links, place, lambda q: wxy.at[q], lambda q: wxy_all.at[q, z]
-        )
-        mine.wait()
-        yield from gather_line(links, place, wxy_all.at[:, z], lambda b: wxy_all.at[:, b])
-
-    def inputs():
-        def at(q, core):
-            return x_all.at[strip(core, tall), lanes(q, wide)]
-
-        keep(x, at(row, col))
-        shared = [links.copy(x, at(row, col), col=place.other)]
-        shared[0].start()
-        yield from gather_rows(
-            links,
-            place,
-            lambda h: x.at[pl.ds(half * h, half)],
-            lambda q, h: x_all.at[strip(2 * col + h, half), lanes(q, wide)],
-        )
-        for k in range(1, 4):
-            q = place.near[k]
-            shared.append(links.copy(at(q, col), at(q, col), col=place.other))
-            shared[-1].start()
-        yield 1
-        for copy in shared:
-            copy.wait_recv()
-        for copy in shared:
-            copy.wait_send()
-
-    def channel_vectors():
-        keep(cvec, cvec_all.at[z])
-        yield from exchange_line(links, place, lambda b: cvec, lambda b: cvec_all.at[b])
-
-    def width_vectors():
-        mine = links.keep(wvec, wvec_all.at[row, z])
-        yield from exchange_line(links, place, lambda b: wvec, lambda b: wvec_all.at[row, b])
-        mine.wait()
-        yield from exchange_rows(
-            links, place, lambda q: wvec_all.at[row], lambda q: wvec_all.at[q]
-        )
-
-    def gate_blocks():
-        mine = links.keep(blk, blk_all.at[z, row])
-        yield from exchange_line(links, place, lambda b: blk, lambda b: blk_all.at[b, row])
-        mine.wait()
-        middle = count // 2
-        yield from gather_rows(
-            links,
-            place,
-            lambda h: blk_all.at[pl.ds(middle * h, middle), row],
-            lambda q, h: blk_all.at[pl.ds(middle * h, middle), q],
-        )
-
-    def hidden_columns(matrix, whole):
-        mine = links.keep(matrix.at[z], whole.at[row, z])
-        yield from exchange_line(
-            links, place, lambda b: matrix.at[b], lambda b: whole.at[row, b]
-        )
-        mine.wait()
-        middle = count // 2
-        yield from gather_rows(
-            links,
-            place,
-            lambda h: whole.at[row, pl.ds(middle * h, middle)],
-            lambda q, h: whole.at[q, pl.ds(middle * h, middle)],
-        )
-
-    def hidden_rows():
-        keep(wdown, down_all.at[:, lanes(row, wide)])
-        yield from gather_rows(
-            links,
-            place,
-            lambda h: wdown.at[down_halves[h]],
-            lambda q, h: down_all.at[down_halves[h], lanes(q, wide)],
-        )
-
-    def cotangents():
-        def block(b):
-            return cot_all.at[strip(col * count + b, quarter)]
-
-        def spot(q):
-            return cot_all.at[strip(col * count + z, quarter), lanes(q, wide)]
-
-        mine = links.keep(cot.at[strip(row, quarter)], spot(row))
-        yield from exchange_rows(links, place, lambda q: cot.at[strip(q, quarter)], spot)
-        mine.wait()
-        yield from gather_line(links, place, block(z), block, share=True)
-
-    def output_rows():
-        keep(wout, wout_all.at[z])
-        yield from gather_line(links, place, wout, lambda b: wout_all.at[b])
-
-    run(
-        [
-            projections(),
-            inputs(),
-            channel_vectors(),
-            width_vectors(),
-            gate_blocks(),
-            hidden_columns(wgate, gate_all),
-            hidden_columns(wup, up_all),
-            cotangents(),
-            hidden_rows(),
-            output_rows(),
-        ]
-    )
-    for copy in kept:
-        copy.wait()
-
-
-def spread_projected(count, proj, out, send, recv, local):
-    place = Place(count)
-    links = Links(send, recv, local)
-    greet(place, rows=True)
-    tall = out.shape[1]
-    tokens = tall - 8
-
-    def source(q):
-        return proj.at[pl.ds(pl.multiple_of(q * tokens, 8), tall)]
-
-    mine = links.keep(source(place.row), out.at[place.row])
-    run([exchange_rows(links, place, source, lambda q: out.at[q])])
-    mine.wait()
-
-
 def combine(earlier, later):
     return (earlier[0] * later[0], later[0] * earlier[1] + later[1])
 
@@ -583,73 +504,6 @@
     return state
 
 
-def recurrence_forward(
-    count, taps, proj, side, spots, vectors, blocks, conv_out, in_out, dec_out, state_out,
-    entering_out, mixed_all, running, local_state, ends, table, mixed, send, recv, local,
-):
-    place = Place(count)
-    links = Links(send, recv, local)
-    greet(place, rows=True)
-    tokens, width = side.shape
-    heads, block = blocks.shape[0] // 2, blocks.shape[1]
-    spot = spots[...]
-    ends[...] = jnp.zeros(ends.shape, WIDE)
-    entering_out[...] = jnp.zeros(ends.shape, WIDE)
-
-    def one_head(h, at):
-        def vector(i):
-            return vectors[i : i + 1, at]
-
-        conv = vector(taps) + vector(0) * (proj[8:, at] + vector(taps + 1))
-        for k in range(1, taps):
-            earlier = proj[8 - k : 8 - k + tokens, at] + vector(taps + 1)
-            conv = conv + vector(k) * jnp.where(spot >= k, earlier, 0.0)
-        conv_out[:, at] = conv
-        low = conv.astype(LOW)
-        input_gate = jax.nn.sigmoid(
-            jnp.dot(low, blocks[h], preferred_element_type=WIDE) + vector(taps + 3)
-        )
-        decay_gate = jax.nn.sigmoid(
-            jnp.dot(low, blocks[heads + h], preferred_element_type=WIDE) + vector(taps + 4)
-        )
-        in_out[:, at] = input_gate
-        dec_out[:, at] = decay_gate
-        log_decay = vector(taps + 5) * decay_gate
-        starting = spot == 0
-        decay = jnp.where(starting, 0.0, jnp.exp(log_decay))
-        multiplier = jnp.where(starting, 1.0, jnp.sqrt(minus_expm1(2.0 * log_decay)))
-        reach, state = scan_rows(decay, multiplier * input_gate * conv, False)
-        running[:, at] = reach
-        local_state[:, at] = state
-        ends[0:1, at] = reach[tokens - 1 :, :]
-        ends[1:2, at] = state[tokens - 1 :, :]
-
-    each_head(heads, block, one_head)
-    own = links.keep(ends, table.at[place.row])
-    own.wait()
-    entering_out[0:1, :] = carry_over(links, place, ends, table, False)
-
-    def finish(h, at):
-        state = local_state[:, at] + running[:, at] * entering_out[0:1, at]
-        state_out[:, at] = state
-        mixed[:, at] = (state * side[:, at]).astype(LOW)
-
-    each_head(heads, block, finish)
-    half = tokens // 2
-    mine = links.keep(mixed, mixed_all.at[strip(place.row, tokens)])
-    run(
-        [
-            gather_rows(
-                links,
-                place,
-                lambda h: mixed.at[pl.ds(half * h, half)],
-                lambda q, h: mixed_all.at[strip(2 * q + h, half)],
-            )
-        ]
-    )
-    mine.wait()
-
-
 def recurrence_backward(
     count, taps, proj, side, spots, vectors, blocks, conv_in, in_gate, dec_gate, state_in, entering,
     grad_mixed, branch_out, sums_out, blocks_out, reach, local_grad, branch, ends, table, heads_in,
@@ -746,53 +600,6 @@
         branch_out[:, at] = branch[:, at].astype(LOW)
 
     each_head(heads, block, finish)
-
-
-def output_and_norm(
-    count, partial, x, vectors, middle_out, normed_all, mine, theirs, here, wide, normed, send,
-    recv, local,
-):
-    place = Place(count)
-    links = Links(send, recv, local)
-    greet(place, rows=True, line=True, cores=True)
-    row, z, col = place.row, place.dp, place.col
-    tall, narrow = x.shape
-    quarter = tall // 4
-    other = links.copy(partial.at[strip(place.other, tall, 8)], theirs, col=place.other)
-    other.start()
-    load = links.keep(partial.at[strip(col, tall, 8)], mine)
-    load.wait()
-    other.wait_recv()
-
-    def add(rows):
-        here[rows] = mine[rows] + theirs[rows] + x[rows].astype(WIDE)
-
-    by_rows(tall, add)
-
-    def source(q):
-        return here.at[strip(q, quarter)]
-
-    own = links.keep(source(row), wide.at[:, lanes(row, narrow)])
-    run([exchange_rows(links, place, source, lambda q: wide.at[:, lanes(q, narrow)])])
-    own.wait()
-    other.wait_send()
-    shift, gain = vectors[1:2, :], vectors[3:4, :]
-    full = wide.shape[1]
-
-    def norm(rows):
-        middle = wide[rows] + shift
-        middle_out[rows] = middle
-        mean = jnp.sum(middle * middle, axis=1, keepdims=True) / full
-        normed[rows] = (middle * lax.rsqrt(mean + epsilon) * (1.0 + gain)).astype(LOW)
-
-    by_rows(quarter, norm)
-
-    def block(b):
-        return normed_all.at[strip(col * count + b, quarter)]
-
-    keep = links.keep(normed, block(z))
-    run([gather_line(links, place, normed, block, share=True)])
-    keep.wait()
 
 
 def norm_rule(rows, grad, value, gain, sums, at):
@@ -818,7 +625,7 @@
     down_halves = halves(down_partial.shape[0])
     sums[...] = jnp.zeros(sums.shape, WIDE)
     gain = vectors[3:4, :]
-    load = links.keep(cot_all.at[strip(col * count + z, quarter)], cot)
+    load = links.keep(cot_all.at[strip(2 * z + col, quarter)], cot)
 
     def back(rows, grad):
         own = cot[rows].astype(WIDE)
@@ -973,7 +780,7 @@
 
 
 def first_norm_back(
-    count, grad_partial, x_all, grad_middle, vectors, proj_partial, up_own, sums_in, channel_in,
+    count, grad_partial, x_own, grad_middle, vectors, proj_partial, up_own, sums_in, channel_in,
     hidden_in, block_in, grad_out, proj_out, up_out, width_sums, channel_sums, block_out, hidden_sums,
     theirs, ours, added,
     row_buffer, x, result, sums, proj_own, proj_ups, proj_downs, proj_staging, proj_low, width_table,
@@ -987,7 +794,7 @@
     quarter, full = grad_middle.shape
     narrow = full // 4
     gain = vectors[0:1, :]
-    load_x = links.keep(x_all.at[strip(4 * col + row, quarter)], x)
+    load_x = links.keep(x_own, x)
     load_proj = [links.keep(proj_partial.at[:, b], proj_own.at[b]) for b in range(count)]
     kept = links.keep(up_own.at[z], up_out.at[z])
 
@@ -1141,6 +948,477 @@
     kept.wait()
 
 
+def advance(*tasks):
+    for task in tasks:
+        next(task, None)
+
+
+def finish(*tasks):
+    run(tasks)
+
+
+def gelu(v):
+    return 0.5 * v * (1.0 + jnp.tanh(ROOT * (v + CUBE * (v * v * v))))
+
+
+def gelu_slope(v):
+    t = jnp.tanh(ROOT * (v + CUBE * (v * v * v)))
+    return 0.5 * (1.0 + t) + 0.5 * v * (1.0 - t * t) * (ROOT * (1.0 + 3.0 * CUBE * (v * v)))
+
+
+def block_of(blocks, h):
+    width = blocks.shape[-1]
+    return blocks[h].reshape(width, width)
+
+
+def forward(
+    count, taps, x, cot, wxy, wout, wgate, wup, wdown, blk, cvec, wvec, spots,
+    nf_out, x_out, cot_own, wxy_out, wout_out, gate_own, up_own, down_all, blocks_out, vectors_out,
+    width_out, branch_out, gelu_out, side_out, conv_out, in_out, dec_out, state_out, entering_out,
+    mixed_out, middle_out, normed_out,
+    x_all, nf, wxy_all, wout_all, blocks, cvec_all, wvec_all, vectors, width, stage, arrived, branch,
+    gelu_in, side, conv, in_gate, dec_gate, state, running, local_state, ends, table, entering, mixed,
+    mixed_all, partial, theirs, here, wide, middle, normed, gate_here, up_here, down_here, cot_here,
+    send, recv, local,
+):
+    place = Place(count)
+    links = Links(send, recv, local)
+    row, z, col = place.row, place.dp, place.col
+    greet(place, rows=True, line=True, cores=True)
+    tall, narrow = x.shape
+    full = 4 * narrow
+    half, quarter = tall // 2, tall // 4
+    depth, part = wxy.shape[1], wxy.shape[2] // 2
+    tokens, steps = 2 * tall, tall // 2
+    heads, block = blocks.shape[0] // 2, blocks.shape[-1]
+    share = blocks.shape[3]
+    kept = []
+
+    def keep(src, dst):
+        kept.append(links.keep(src, dst))
+        return kept[-1]
+
+    def projections():
+        def at(q, b):
+            return wxy_all.at[q, strip(b, depth, 8)]
+
+        mine = links.keep(wxy.at[row], at(row, z))
+        yield from exchange_rows(links, place, lambda q: wxy.at[q], lambda q: at(q, z))
+        mine.wait()
+
+        def piece(b):
+            return wxy_all.at[:, strip(b, depth, 8)]
+
+        yield from gather_line(links, place, piece(z), piece)
+
+    def inputs():
+        def at(q, core):
+            return x_all.at[strip(core, tall), lanes(q, narrow)]
+
+        mine = links.keep(x, at(row, col))
+        shared = [links.copy(x, at(row, col), col=place.other)]
+        shared[0].start()
+        yield from gather_rows(
+            links,
+            place,
+            lambda h: x.at[pl.ds(half * h, half)],
+            lambda q, h: x_all.at[strip(2 * col + h, half), lanes(q, narrow)],
+        )
+        for k in range(1, 4):
+            q = place.near[k]
+            shared.append(links.copy(at(q, col), at(q, col), col=place.other))
+            shared[-1].start()
+        yield 1
+        mine.wait()
+        for copy in shared:
+            copy.wait_recv()
+        for copy in shared:
+            copy.wait_send()
+
+    def channel_vectors():
+        keep(cvec, cvec_all.at[z])
+        yield from exchange_line(links, place, lambda b: cvec, lambda b: cvec_all.at[b])
+
+    def width_vectors():
+        mine = links.keep(wvec, wvec_all.at[row, z])
+        yield from exchange_line(links, place, lambda b: wvec, lambda b: wvec_all.at[row, b])
+        mine.wait()
+        yield from exchange_rows(
+            links, place, lambda q: wvec_all.at[row], lambda q: wvec_all.at[q]
+        )
+
+    def gate_blocks():
+        split = blocks.shape[2] > 1
+        own = row if split else 0
+        mine = links.keep(blk, blocks.at[:, z, own])
+        yield from exchange_line(links, place, lambda b: blk, lambda b: blocks.at[:, b, own])
+        mine.wait()
+        middle = count // 2
+        if split:
+
+            def at(q, h):
+                return blocks.at[:, pl.ds(middle * h, middle), q]
+
+            yield from gather_rows(links, place, lambda h: at(row, h), at)
+
+    def hidden_rows():
+        parts = halves(wdown.shape[0])
+        mine = Relay(links, wdown, down_here, down_all.at[:, lanes(row, narrow)])
+        kept.append(mine)
+        yield from gather_rows(
+            links,
+            place,
+            lambda h: wdown.at[parts[h]],
+            lambda q, h: down_all.at[parts[h], lanes(q, narrow)],
+        )
+
+    def cotangent_rows():
+        def spot(q):
+            return cot_own.at[:, lanes(q, narrow)]
+
+        mine = Relay(links, cot.at[strip(row, quarter)], cot_here, spot(row))
+        yield from exchange_rows(links, place, lambda q: cot.at[strip(q, quarter)], spot)
+        mine.wait()
+
+    def hidden_columns(matrix, buffer, own):
+        mine = Relay(links, matrix.at[z], buffer, own.at[z])
+        yield from exchange_line(links, place, lambda b: matrix.at[b], lambda b: own.at[b])
+        mine.wait()
+
+    def output_rows():
+        at = wout.shape[0]
+        mine = links.keep(wout, wout_all.at[strip(z, at)])
+        yield from gather_line(links, place, wout, lambda b: wout_all.at[strip(b, at)])
+        mine.wait()
+
+    weights, rows_in = projections(), inputs()
+    vectors_in, widths_in, blocks_in = channel_vectors(), width_vectors(), gate_blocks()
+    cot_in, output_in, down_in = cotangent_rows(), output_rows(), hidden_rows()
+    gate_in = hidden_columns(wgate, gate_here, gate_own)
+    up_in = hidden_columns(wup, up_here, up_own)
+    advance(weights, rows_in, widths_in, vectors_in, blocks_in, cot_in)
+    advance(weights, widths_in, vectors_in, blocks_in)
+    finish(widths_in, vectors_in)
+    for copy in kept:
+        copy.wait()
+    kept.clear()
+
+    for b in range(count):
+        size = vectors.shape[1] // count
+        vectors[:, b * size : (b + 1) * size] = cvec_all[b, :, :size]
+        for q in range(4):
+            at = q * narrow + b * depth
+            width[:, at : at + depth] = wvec_all[q, b, :, :depth]
+    keep(vectors, vectors_out)
+    keep(width, width_out)
+    advance(rows_in)
+    advance(weights)
+    finish(rows_in)
+    advance(down_in)
+    keep(x_all.at[strip(4 * col + row, quarter)], x_out)
+
+    nf[0:16, :] = jnp.zeros((16, full), LOW)
+
+    def first_norm(rows):
+        value = x_all[rows].astype(WIDE)
+        mean = jnp.sum(value * value, axis=1, keepdims=True) / full
+        value = value * lax.rsqrt(mean + epsilon) * (1.0 + width[0:1, :])
+        nf[pl.ds(pl.multiple_of(rows.start + 16, 16), rows.size)] = value.astype(LOW)
+
+    by_rows(tokens, first_norm)
+    keep(nf.at[pl.ds(16, tokens)], nf_out)
+    advance(weights, blocks_in, cot_in)
+    finish(blocks_in)
+    keep(blocks, blocks_out)
+    finish(weights, cot_in)
+    keep(wxy_all, wxy_out)
+
+    advance(output_in)
+    advance(down_in)
+    out = []
+    for k in (3, 2, 1, 0):
+        q = place.near[k]
+
+        def product(k=k, q=q):
+            stage[k] = jnp.dot(
+                nf[pl.ds(pl.multiple_of(q * steps, 16), steps + 16), :],
+                wxy_all[...].astype(LOW).reshape(full, 2 * part),
+                preferred_element_type=WIDE,
+            )
+
+        product()
+        source = stage.at[k, pl.ds(8, steps + 8)]
+        if k:
+            out.append(links.copy(source, arrived.at[row], row=q))
+            out[-1].start()
+        else:
+            mine = links.keep(source, arrived.at[row])
+    advance(output_in, gate_in)
+    mine.wait()
+    for copy in out:
+        copy.wait_recv()
+    finish(down_in)
+    for copy in out:
+        copy.wait_send()
+
+    spot = spots[...]
+    starting = spot == 0
+    for q in range(4):
+        at = slice(q * part, (q + 1) * part)
+        branch[:, at] = arrived[q, :, :part]
+        gelu_in[:, at] = arrived[q, 8:, part:] + vectors[taps + 2 : taps + 3, at]
+    keep(branch, branch_out)
+    keep(gelu_in, gelu_out)
+    ends[...] = jnp.zeros(ends.shape, WIDE)
+    entering[...] = jnp.zeros(ends.shape, WIDE)
+
+    def one_head(h, at):
+        def vector(i):
+            return vectors[i : i + 1, at]
+
+        conv_here = vector(taps) + vector(0) * (branch[8:, at] + vector(taps + 1))
+        for k in range(1, taps):
+            earlier = branch[8 - k : 8 - k + steps, at] + vector(taps + 1)
+            conv_here = conv_here + vector(k) * jnp.where(spot >= k, earlier, 0.0)
+        conv[:, at] = conv_here
+        low = conv_here.astype(LOW)
+        input_gate = jax.nn.sigmoid(
+            jnp.dot(low, block_of(blocks, h), preferred_element_type=WIDE) + vector(taps + 3)
+        )
+        decay_gate = jax.nn.sigmoid(
+            jnp.dot(low, block_of(blocks, heads + h), preferred_element_type=WIDE)
+            + vector(taps + 4)
+        )
+        in_gate[:, at] = input_gate
+        dec_gate[:, at] = decay_gate
+        log_decay = vector(taps + 5) * decay_gate
+        decay = jnp.where(starting, 0.0, jnp.exp(log_decay))
+        multiplier = jnp.where(starting, 1.0, jnp.sqrt(minus_expm1(2.0 * log_decay)))
+        reach, value = scan_rows(decay, multiplier * input_gate * conv_here, False)
+        running[:, at] = reach
+        local_state[:, at] = value
+        ends[0:1, at] = reach[steps - 1 :, :]
+        ends[1:2, at] = value[steps - 1 :, :]
+        side[:, at] = gelu(gelu_in[:, at])
+
+    each_head(heads, block, one_head)
+    for scratch, output in (
+        (conv, conv_out), (in_gate, in_out), (dec_gate, dec_out), (side, side_out),
+    ):
+        keep(scratch, output)
+    own = links.keep(ends, table.at[row])
+    advance(output_in)
+    own.wait()
+    entering[0:1, :] = carry_over(links, place, ends, table, False)
+
+    def mix(h, at):
+        value = local_state[:, at] + running[:, at] * entering[0:1, at]
+        state[:, at] = value
+        mixed[:, at] = (value * side[:, at]).astype(LOW)
+
+    each_head(heads, block, mix)
+    mine = links.keep(mixed, mixed_all.at[strip(row, steps)])
+    mixes = gather_rows(
+        links,
+        place,
+        lambda h: mixed.at[pl.ds(steps // 2 * h, steps // 2)],
+        lambda q, h: mixed_all.at[strip(2 * q + h, steps // 2)],
+    )
+    advance(mixes)
+    keep(state, state_out)
+    keep(entering, entering_out)
+    finish(output_in)
+    keep(wout_all, wout_out)
+    advance(mixes, up_in)
+    finish(mixes)
+    mine.wait()
+    keep(mixed_all, mixed_out)
+
+    def product_rows(first):
+        def body(i, carry):
+            rows = pl.ds(pl.multiple_of(first * tall + i * steps, 16), steps)
+            partial[rows] = jnp.dot(mixed_all[rows], wout_all[...], preferred_element_type=WIDE)
+            return carry
+
+        lax.fori_loop(0, tall // steps, body, 0)
+
+    product_rows(place.other)
+    swap = links.copy(partial.at[strip(place.other, tall)], theirs, col=place.other)
+    swap.start()
+    product_rows(col)
+    swap.wait_recv()
+
+    def add(rows):
+        at = pl.ds(pl.multiple_of(col * tall + rows.start, 16), rows.size)
+        here[rows] = partial[at] + theirs[rows] + x_all[at, lanes(row, narrow)].astype(WIDE)
+
+    by_rows(tall, add)
+
+    def quarter_of(q):
+        return here.at[strip(q, quarter)]
+
+    mine = links.keep(quarter_of(row), wide.at[:, lanes(row, narrow)])
+    middles = exchange_rows(links, place, quarter_of, lambda q: wide.at[:, lanes(q, narrow)])
+    advance(middles)
+    mine.wait()
+    finish(middles)
+    swap.wait_send()
+
+    def second_norm(rows):
+        value = wide[rows] + width[1:2, :]
+        middle[rows] = value
+        mean = jnp.sum(value * value, axis=1, keepdims=True) / full
+        normed[rows] = (value * lax.rsqrt(mean + epsilon) * (1.0 + width[3:4, :])).astype(LOW)
+
+    by_rows(quarter, second_norm)
+    keep(middle, middle_out)
+    keep(normed, normed_out)
+    finish(gate_in, up_in)
+    for copy in kept:
+        copy.wait()
+
+
+def feed_forward(
+    count, normed, cot, wgate, up_own, wdown, biases, normed_all, cot_all, gate_all, up_all, hidden_out,
+    gate_out, up_out, sums, gate_w, up_w, down_w, piece, gate_v, up_v, grad_v, hidden, grad_gate,
+    grad_up, cot_here, normed_here, send, recv, local,
+):
+    place = Place(count)
+    links = Links(send, recv, local)
+    row, z, col = place.row, place.dp, place.col
+    greet(place, rows=True, line=True, cores=True)
+    quarter, full = normed.shape
+    narrow, pair = full // 4, 2 * quarter
+    units = wdown.shape[0]
+    middle = count // 2
+    kept = [
+        links.keep(wgate, gate_w.at[row]),
+        links.keep(up_own, up_w.at[row]),
+    ]
+    load = links.keep(wdown, down_w)
+
+    def tokens(own, buffer, whole):
+        def at(b):
+            return whole.at[strip(2 * b + col, quarter)]
+
+        relay = Relay(links, own, buffer, at(z))
+        return LineGather(links, place, own, at), relay
+
+    def columns_of(own, whole):
+        yield from gather_rows(
+            links,
+            place,
+            lambda h: own.at[pl.ds(middle * h, middle)],
+            lambda q, h: whole.at[q, pl.ds(middle * h, middle)],
+        )
+
+    def neighbours(step, body):
+        if step == 0:
+            body(z)
+            return
+
+        def lap(i, carry):
+            b = z - step + 2 * step * i
+            pl.when((b >= 0) & (b < count))(lambda: body(place.turn(b)))
+            return carry
+
+        lax.fori_loop(0, 2, lap, 0)
+
+    def with_piece(source, body):
+        k, links.kept = links.kept, links.kept + 1
+
+        def inner(b):
+            load = pltpu.make_async_copy(source.at[strip(b, pair)], piece, links.local.at[k])
+            load.start()
+            load.wait()
+            body(strip(b, pair))
+
+        return inner
+
+    def inward(whole, i, values):
+        def body(rows):
+            weight = whole[...].astype(LOW).reshape(full, units)
+            values[rows] = (
+                jnp.dot(piece[...], weight, preferred_element_type=WIDE) + biases[i : i + 1, :]
+            )
+
+        return body
+
+    def backward(rows):
+        grad_v[rows] = lax.dot_general(
+            piece[...], down_w[...], (((1,), (1,)), ((), ())), preferred_element_type=WIDE
+        )
+
+    def outward(rows):
+        def body(inner):
+            at = pl.ds(pl.multiple_of(rows.start + inner.start, 16), inner.size)
+            gate, up, grad = gate_v[at], up_v[at], grad_v[at]
+            t = jnp.tanh(ROOT * (gate + CUBE * (gate * gate * gate)))
+            side = 0.5 * gate * (1.0 + t)
+            slope = 0.5 * (1.0 + t) + 0.5 * gate * (1.0 - t * t) * (
+                ROOT * (1.0 + 3.0 * CUBE * (gate * gate))
+            )
+            hidden[at] = (side * up).astype(LOW)
+            gate, up = grad * up * slope, grad * side
+            grad_gate[at] = gate.astype(LOW)
+            grad_up[at] = up.astype(LOW)
+            sums[0:1, :] += jnp.sum(gate, axis=0, keepdims=True)
+            sums[1:2, :] += jnp.sum(up, axis=0, keepdims=True)
+
+        by_rows(pair, body)
+
+    gates, ups = columns_of(wgate, gate_w), columns_of(up_own, up_w)
+    cots, cot_relay = tokens(cot, cot_here, cot_all)
+    norms, norm_relay = tokens(normed, normed_here, normed_all)
+    cots.start()
+    advance(gates, ups)
+    cot_relay.wait()
+    sums[...] = jnp.zeros(sums.shape, WIDE)
+    load.wait()
+    cots.ready(0)
+    back = with_piece(cot_all, backward)
+    neighbours(0, back)
+    into = with_piece(normed_all, inward(gate_w, 0, gate_v))
+    for step in range(1, count):
+        cots.step(step)
+        if step == 1:
+            norms.start()
+        else:
+            norms.step(step - 1)
+        cots.ready(step)
+        neighbours(step, back)
+    advance(gates, ups)
+    norm_relay.wait()
+    finish(gates)
+    for copy in kept:
+        copy.wait()
+    kept.clear()
+    kept.append(links.keep(gate_w, gate_all))
+    for step in range(count - 1):
+        norms.ready(step)
+        neighbours(step, into)
+    norms.step(count - 1)
+    norms.ready(count - 1)
+    neighbours(count - 1, into)
+    finish(ups)
+    kept.append(links.keep(up_w, up_all))
+    into_up = with_piece(normed_all, inward(up_w, 1, up_v))
+
+    def last(b, carry):
+        into_up(b)
+        outward(strip(b, pair))
+        return carry
+
+    lax.fori_loop(0, count, last, 0)
+    cots.close()
+    norms.close()
+    kept.append(links.keep(hidden, hidden_out))
+    kept.append(links.keep(grad_gate, gate_out))
+    kept.append(links.keep(grad_up, up_out))
+    for copy in kept:
+        copy.wait()
+
+
 def times(piece, matrix):
     return jnp.dot(piece, matrix, preferred_element_type=WIDE)
 
@@ -1164,6 +1442,10 @@
 
 def padded_rows(rows, height, width):
     return jnp.pad(rows, ((0, height - rows.shape[0]), (0, width - rows.shape[1])))
+
+
+def rounded(values):
+    return lax.reduce_precision(values, 8, 7)
 
 
 def round_up(size, step):
@@ -1206,157 +1488,194 @@
     heads, block_part, block = input_blocks.shape
     taps = conv_taps.shape[0]
     steps = positions.shape[0]
-    share = block_part // rows_count
+    splits = rows_count if block_part % (16 * rows_count) == 0 else 1
+    share = block_part // splits
+    back_share = block_part // rows_count
     remote, local = 64 + 24 * count, 40 + 6 * count
 
     wxy = jnp.concatenate(
         (columns(branch_matrix.astype(LOW), rows_count), columns(gelu_matrix.astype(LOW), rows_count)),
         axis=2,
     )
+    if depth % 16:
+        wxy = wxy.astype(WIDE)
     blocks_low = jnp.concatenate((input_blocks, decay_blocks), axis=0).astype(LOW)
-    blk = lax.dynamic_slice_in_dim(blocks_low, place_row * share, share, 1).reshape(
-        2 * heads * share, block
+    blk = lax.dynamic_slice_in_dim(
+        blocks_low, place_row * share if splits > 1 else 0, share, 1
     )
     channel_rows = jnp.concatenate(
         (
             conv_taps,
-            jnp.stack((conv_bias, branch_bias, gelu_bias, input_bias, decay_bias, decay_param)),
+            jnp.stack((conv_bias, branch_bias, gelu_bias, input_bias, decay_bias)),
         ),
         axis=0,
     )
+    decay_raw = rounded(decay_param)
+    channel_rows = jnp.concatenate(
+        (rounded(channel_rows), -8.0 * jax.nn.softplus(decay_raw)[None, :]), axis=0
+    )
     channel_size = channel_rows.shape[1]
     cvec = padded_rows(
-        channel_rows.astype(LOW).astype(WIDE),
+        channel_rows,
         round_up(taps + 6, 8),
         round_up(channel_size, 128),
     )
     wvec = padded_rows(
-        jnp.stack((norm_first, output_bias, down_bias, norm_second)).astype(LOW).astype(WIDE),
+        rounded(jnp.stack((norm_first, output_bias, down_bias, norm_second))),
         8,
         round_up(depth, 128),
     )
-    x_all, cot_all, wxy_all, wout_all, gate_all, up_all, down_all, blk_all, cvec_all, wvec_all = call(
-        functools.partial(gather_inputs, count),
-        "gather_inputs",
-        1,
-        [
-            (array, False)
-            for array in (
-                inputs,
-                cotangent,
-                wxy,
-                output_matrix.astype(LOW),
-                columns(gate_matrix.astype(LOW), count),
-                columns(up_matrix.astype(LOW), count),
-                down_matrix.astype(LOW),
-                blk,
-                cvec,
-                wvec,
-            )
-        ],
-        [
-            ((tokens, full), LOW, False),
-            ((cores * count * quarter, full), LOW, False),
-            ((rows_count, count, depth, 2 * part), LOW, False),
-            ((count,) + output_matrix.shape, LOW, False),
-            ((rows_count, count, depth, hidden_part), LOW, False),
-            ((rows_count, count, depth, hidden_part), LOW, False),
-            ((hidden_part, full), LOW, False),
-            ((count, rows_count) + blk.shape, LOW, False),
-            ((count,) + cvec.shape, WIDE, False),
-            ((rows_count, count) + wvec.shape, WIDE, False),
-        ],
-        [],
-        remote,
-        local,
-    )
-    wxy_all = wxy_all.reshape(full, 2 * part)
-    wout_all = wout_all.reshape(width, narrow)
-    gate_all = gate_all.reshape(full, hidden_part)
-    up_all = up_all.reshape(full, hidden_part)
-    blocks = (
-        blk_all.reshape(count, rows_count, 2 * heads, share, block)
-        .transpose(2, 0, 1, 3, 4)
-        .reshape(2 * heads, block, block)
-    )
-    channel_all = side_by_side(cvec_all[:, : taps + 6, :channel_size])
-    gelu_shift, decay_raw = channel_all[taps + 2], channel_all[taps + 5]
-    vectors = jnp.concatenate(
-        (channel_all[: taps + 5], -8.0 * jax.nn.softplus(decay_raw)[None, :]), axis=0
-    )
-    width_all = jnp.concatenate(
-        [wvec_all[q, b, :, :depth] for q in range(rows_count) for b in range(count)], axis=1
-    )
-
-    resid = x_all.astype(WIDE)
-    inverse = lax.rsqrt(jnp.mean(resid * resid, axis=1, keepdims=True) + epsilon)
-    normed_first = (resid * inverse * (1.0 + width_all[0])).astype(LOW)
-    projected = jnp.pad(times(normed_first, wxy_all), ((8, 0), (0, 0)))
-    (projected_here,) = call(
-        functools.partial(spread_projected, count),
-        "spread_projected",
-        2,
-        [(projected, False)],
-        [((rows_count, steps + 8, 2 * part), WIDE, False)],
-        [],
-        remote,
-        local,
-    )
-    branch = side_by_side(projected_here[:, :, :part])
-    gelu_in = side_by_side(projected_here[:, 8:, part:]) + gelu_shift
-    side, gelu_pull = jax.vjp(jax.nn.gelu, gelu_in)
-
     spots = positions[:, None]
-    wide_tokens = ((steps, width), WIDE, True)
+    heads_all = 2 * heads
+    whole_tokens = ((tokens, full), LOW, False)
+    wide_tokens = ((steps, width), WIDE, False)
+    nf_shape = pltpu.VMEM((16 + tokens, full), LOW)
+    wxy_kind = wxy.dtype
     tokens_scratch = pltpu.VMEM((steps, width), WIDE)
     eight_rows = pltpu.VMEM((8, width), WIDE)
     table_rows = pltpu.VMEM((rows_count, 8, width), WIDE)
-    conv, input_gate, decay_gate, state, entering, mixed_all = call(
-        functools.partial(recurrence_forward, count, taps),
-        "recurrence_forward",
-        3,
-        [(array, True) for array in (branch, side, spots, vectors, blocks)],
-        [wide_tokens] * 4 + [((8, width), WIDE, True), ((tokens, width), LOW, False)],
-        [
+    blocks_shape = (heads_all, count, splits, share, block)
+    hidden_shape = (rows_count, count, depth, hidden_part)
+    here_scratch = pltpu.VMEM((tall, narrow), WIDE)
+    (
+        normed_first, x_own, cot_own, wxy_all, wout_all, gate_own, up_own, down_all, blocks, vectors,
+        width_all, branch, gelu_in, side, conv, input_gate, decay_gate, state, entering, mixed_all,
+        middle, normed_own,
+    ) = call(
+        functools.partial(forward, count, taps),
+        "forward",
+        1,
+        [
+            (inputs, False),
+            (cotangent, False),
+            (wxy, False),
+            (output_matrix.astype(LOW), False),
+            (columns(gate_matrix.astype(LOW), count).astype(wxy_kind), False),
+            (columns(up_matrix.astype(LOW), count).astype(wxy_kind), False),
+            (down_matrix.astype(LOW), False),
+            (blk, False),
+            (cvec, False),
+            (wvec, False),
+            (spots, True),
+        ],
+        [
+            whole_tokens,
+            ((quarter, full), LOW, False),
+            ((quarter, full), LOW, False),
+            ((rows_count, count * depth, 2 * part), wxy_kind, False),
+            ((width, narrow), LOW, False),
+            (hidden_shape[1:], wxy_kind, False),
+            (hidden_shape[1:], wxy_kind, False),
+            ((hidden_part, full), LOW, False),
+            (blocks_shape, LOW, False),
+            ((cvec.shape[0], width), WIDE, False),
+            ((8, full), WIDE, False),
+            ((steps + 8, width), WIDE, False),
+            wide_tokens,
+            wide_tokens,
+            wide_tokens,
+            wide_tokens,
+            wide_tokens,
+            wide_tokens,
+            ((8, width), WIDE, False),
+            ((tokens, width), LOW, False),
+            ((quarter, full), WIDE, False),
+            ((quarter, full), LOW, False),
+        ],
+        [
+            pltpu.VMEM((tokens, full), LOW),
+            nf_shape,
+            pltpu.VMEM((rows_count, count * depth, 2 * part), wxy_kind),
+            pltpu.VMEM((width, narrow), LOW),
+            pltpu.VMEM(blocks_shape, LOW),
+            pltpu.VMEM((count,) + cvec.shape, WIDE),
+            pltpu.VMEM((rows_count, count) + wvec.shape, WIDE),
+            pltpu.VMEM((cvec.shape[0], width), WIDE),
+            pltpu.VMEM((8, full), WIDE),
+            pltpu.VMEM((rows_count, steps + 16, 2 * part), WIDE),
+            pltpu.VMEM((rows_count, steps + 8, 2 * part), WIDE),
+            pltpu.VMEM((steps + 8, width), WIDE),
+            tokens_scratch,
+            tokens_scratch,
+            tokens_scratch,
+            tokens_scratch,
+            tokens_scratch,
+            tokens_scratch,
             tokens_scratch,
             tokens_scratch,
             eight_rows,
             table_rows,
+            eight_rows,
             pltpu.VMEM((steps, width), LOW),
+            pltpu.VMEM((tokens, width), LOW),
+            pltpu.VMEM((tokens, narrow), WIDE),
+            here_scratch,
+            here_scratch,
+            pltpu.VMEM((quarter, full), WIDE),
+            pltpu.VMEM((quarter, full), WIDE),
+            pltpu.VMEM((quarter, full), LOW),
+            pltpu.VMEM((depth, hidden_part), wxy_kind),
+            pltpu.VMEM((depth, hidden_part), wxy_kind),
+            pltpu.VMEM((hidden_part, narrow), LOW),
+            pltpu.VMEM((quarter, narrow), LOW),
         ],
         remote,
         local,
     )
-
-    middle, normed_second = call(
-        functools.partial(output_and_norm, count),
-        "output_and_norm",
-        4,
-        [(times(mixed_all, wout_all), False), (inputs, True), (width_all, True)],
-        [((quarter, full), WIDE, True), ((cores * count * quarter, full), LOW, False)],
-        [
-            pltpu.VMEM((tall, narrow), WIDE),
-            pltpu.VMEM((tall, narrow), WIDE),
-            pltpu.VMEM((tall, narrow), WIDE),
-            pltpu.VMEM((quarter, full), WIDE),
+    wxy_all = wxy_all.reshape(full, 2 * part).astype(LOW)
+    blocks = blocks.reshape(heads_all, block, block)
+    gelu_pull = jax.vjp(jax.nn.gelu, gelu_in)[1]
+
+    hidden_tokens = cores * count * quarter
+    units_rows = ((hidden_tokens, hidden_part), LOW, False)
+    biases = padded_rows(rounded(jnp.stack((gate_bias, up_bias))), 8, hidden_part)
+    weight_scratch = pltpu.VMEM(hidden_shape, wxy_kind)
+    units_wide = pltpu.VMEM((hidden_tokens, hidden_part), WIDE)
+    units_low = pltpu.VMEM((hidden_tokens, hidden_part), LOW)
+    (
+        normed_second, cot_all, gate_all, up_all, hidden, grad_gate_low, grad_up_low, hidden_part_sums,
+    ) = call(
+        functools.partial(feed_forward, count),
+        "feed_forward",
+        2,
+        [
+            (normed_own, False),
+            (cot_own, False),
+            (gate_own, False),
+            (up_own, False),
+            (down_all, False),
+            (biases, True),
+        ],
+        [
+            ((hidden_tokens, full), LOW, False),
+            ((hidden_tokens, full), LOW, False),
+            (hidden_shape, wxy_kind, False),
+            (hidden_shape, wxy_kind, False),
+            units_rows,
+            units_rows,
+            units_rows,
+            ((8, hidden_part), WIDE, True),
+        ],
+        [
+            weight_scratch,
+            weight_scratch,
+            pltpu.VMEM((hidden_part, full), LOW),
+            pltpu.VMEM((cores * quarter, full), LOW),
+            units_wide,
+            units_wide,
+            units_wide,
+            units_low,
+            units_low,
+            units_low,
+            pltpu.VMEM((quarter, full), LOW),
             pltpu.VMEM((quarter, full), LOW),
         ],
         remote,
         local,
     )
-
-    def feed(gate_value, up_value):
-        return jax.nn.gelu(gate_value) * up_value
-
-    hidden_value, feed_pull = jax.vjp(
-        feed,
-        times(normed_second, gate_all) + gate_bias.astype(LOW).astype(WIDE),
-        times(normed_second, up_all) + up_bias.astype(LOW).astype(WIDE),
-    )
-    hidden = hidden_value.astype(LOW)
-    grad_gate, grad_up = feed_pull(times_flipped(cot_all, down_all))
-    grad_gate_low, grad_up_low = grad_gate.astype(LOW), grad_up.astype(LOW)
-    by_device = (cores, count, quarter, full)
+    gate_all = gate_all.reshape(full, hidden_part).astype(LOW)
+    up_all = up_all.reshape(full, hidden_part).astype(LOW)
+    by_device = (count, cores, quarter, full)
     grad_normed_second = (
         (times_flipped(grad_gate_low, gate_all) + times_flipped(grad_up_low, up_all))
         .astype(LOW)
@@ -1492,26 +1811,22 @@
     proj_partial = left_product(normed_first, grad_projected).astype(LOW)
     grad_normed_first = times_flipped(grad_projected, wxy_all).astype(LOW)
     channel_part = channel_part.at[taps + 5].set(jnp.sum(grad_gelu, axis=0))
-    hidden_part_sums = padded_rows(
-        jnp.stack((jnp.sum(grad_gate, axis=0), jnp.sum(grad_up, axis=0))),
-        8,
-        round_up(hidden_part, 128),
-    )
+    hidden_part_sums = padded_rows(hidden_part_sums, 8, round_up(hidden_part, 128))
     block_in = (
         block_sums.astype(LOW)
-        .reshape(2 * heads, count, rows_count, share, block)
+        .reshape(2 * heads, count, rows_count, back_share, block)
         .transpose(2, 1, 0, 3, 4)
-        .reshape(rows_count, 2, count // 2 * 2 * heads * share, block)
-    )
-    channel_shape, hidden_shape = channel_part.shape, hidden_part_sums.shape
-    block_rows = 2 * heads * share
+        .reshape(rows_count, 2, count // 2 * 2 * heads * back_share, block)
+    )
+    channel_shape, sums_shape = channel_part.shape, hidden_part_sums.shape
+    block_rows = 2 * heads * back_share
     input_grad, proj_grad, up_blocks, width_sums, channel_sums, block_grads, hidden_sums = call(
         functools.partial(first_norm_back, count),
         "first_norm_back",
         9,
         [
             (grad_normed_first.reshape(cores, rows_count, quarter, full), False),
-            (x_all, False),
+            (x_own, False),
             (grad_middle, True),
             (width_all, True),
             (proj_partial.reshape(rows_count, count, depth, 2 * part), False),
@@ -1528,7 +1843,7 @@
             ((2, 8, narrow), WIDE, True),
             (channel_shape, WIDE, True),
             ((rows_count, block_rows, block), LOW, False),
-            (hidden_shape, WIDE, True),
+            (sums_shape, WIDE, True),
         ],
         [
             pltpu.VMEM((rows_count, quarter, full), LOW),
@@ -1546,7 +1861,7 @@
             pltpu.VMEM((rows_count, 8, narrow), WIDE),
             pltpu.VMEM((rows_count,) + channel_shape, WIDE),
             pltpu.VMEM((count,) + channel_shape, WIDE),
-            pltpu.VMEM((rows_count,) + hidden_shape, WIDE),
+            pltpu.VMEM((rows_count,) + sums_shape, WIDE),
             row_buffers(2 * block_in.shape[2], block),
             pltpu.VMEM((2, block_in.shape[2], block), WIDE),
             *line_buffers(count, 1, block_rows, block),
@@ -1558,7 +1873,7 @@
     branch_grad = side_by_side(proj_grad[:, :, :part]).astype(WIDE)
     gelu_grad = side_by_side(proj_grad[:, :, part:]).astype(WIDE)
     block_grads = (
-        block_grads.reshape(rows_count, 2 * heads, share, block)
+        block_grads.reshape(rows_count, 2 * heads, back_share, block)
         .transpose(1, 0, 2, 3)
         .reshape(2 * heads, block_part, block)
         .astype(WIDE)
@@ -1567,8 +1882,7 @@
     width_sums = lax.dynamic_slice_in_dim(
         width_sums[0] + width_sums[1], place_dp * depth, depth, 1
     )
-    decay_raw_here = lax.dynamic_slice_in_dim(decay_raw, place_dp * channel_size, channel_size, 0)
-    decay_param_grad = -8.0 * channel_sums[taps + 4] * jax.nn.sigmoid(decay_raw_here)
+    decay_param_grad = -8.0 * channel_sums[taps + 4] * jax.nn.sigmoid(decay_raw)
 
     return (
         layer_out.reshape(tall, narrow),

time: 941 us -> 845 us (0.90)
  matrix products: 129 us -> 78.8 us
  Pallas kernels: 727 us -> 700 us
  local copies, waits for them, and re-layouts: 51.3 us -> 41.3 us
    dot_general x5 -> x1, matrix products: 48 us -> 7.54 us  [times(): return jnp.dot(piece, matrix, preferred_element_type=WIDE)]
    pallas_call x9 -> x7, Pallas kernels: 727 us -> 700 us  [call(): pl.pallas_call(kernel, in_specs=[VMEM if inside else ANY for _, inside in...]
    dot_general x5 -> x4, matrix products: 45.5 us -> 34.8 us  [times_flipped(): lax.dot_general(piece, matrix, (((1,), (1,)), ((), ())), preferred_elemen...]
where the time goes in v3:
time: 845 us; the launch traced here: 841 us
  Pallas kernels  700 us (83%)
  matrix products  78.8 us (9%)
  local copies, waits for them, and re-layouts  41.3 us (5%)
  other arithmetic  19.2 us (2%)
    pallas_call x7, Pallas kernels, call(): pl.pallas_call(kernel, in_specs=[VMEM if inside else ANY for _, inside in...  700 us
    dot_general x5, matrix products, left_product(): lax.dot_general(left, right, (((0,), (0,)), ((), ())), preferred_element_...  36.5 us
    dot_general x4, matrix products, times_flipped(): lax.dot_general(piece, matrix, (((1,), (1,)), ((), ())), preferred_elemen...  34.8 us

profile of v3, /device:TPU:0, one launch (start us, length us, event | category | flops | bytes accessed | tf_op | source)
XLA Modules:
  0.0 840.9 jit_solution(7622732018405262638)
XLA Ops:
  0.7 1.3 convert_element_type.83
  2.4 1.2 maximum_maximum_fusion.1.wxy
  3.5 0.8 convert_element_type.84.wout
  4.9 1.4 copy-done.3
  6.7 1.8 pad_maximum_fusion
  8.6 0.7 copy-done.4
  9.4 1.2 convert_element_type.87.wdown
  12.7 0.8 copy.59.spots
  13.6 193.5 %forward.1 = (bf16[1024,2560]{1,0:T(8,128)(2,1)}, bf16[128,2560]{1,0:T(8,128)(2,1)}, bf16[128,2560]{1,0:T(8,128)(2,1)}, bf16[4,640,640]{2,1,0:T(8,128)(2,1)}, bf...) custom-call(bf16[512,640]{1,0:T(8,128)(2,1)} %x.9, ...), custom_call_target="tpu_custom_call" | custom-call | tf_op jit(solution)/shard_map/forward/pallas_call | solution.py:432
  207.7 134.1 %feed_forward.1 = (bf16[1024,2560]{1,0:T(8,128)(2,1)}, bf16[1024,2560]{1,0:T(8,128)(2,1)}, bf16[4,4,160,960]{3,2,1,0:T(8,128)(2,1)}, bf16[4,4,160,960]{3,2,1,0:T...) custom-call(bf16[128,2560]{1,0:T(8,128)(2,1)} %get-tuple-element.86., ...), custom_call_target="tpu_custom_call" | custom-call | tf_op jit(solution)/shard_map/feed_forward/pallas_call | solution.py:432
  341.9 11.2 %fusion.15 = f32[1024,2560]{1,0:T(8,128)} fusion(bf16[1024,960]{1,0:T(8,128)(2,1)} %get-tuple-element.91, bf16[2560,960]{1,0:T(8,128)(2,1)} %bitcast.178), kind=kOutput, calls=%fused_computation.87 | convolution fusion | flops 5033164800 | bytes 17367040 | tf_op jit(solution)/shard_map/dot_general | solution.py:1427
  353.1 10.4 %add_convert_fusion = bf16[1024,2560]{1,0:T(8,128)(2,1)} fusion(f32[1024,2560]{1,0:T(8,128)} %fusion.15, bf16[1024,960]{1,0:T(8,128)(2,1)S(1)} %copy-done.36, bf16[2560,960]{1,0:T(8,128)(2,1)S(1)} %bitcast.177), kind=kOutput, calls=%fused_computation | convolution fusion | flops 5038407680 | bytes 22609920 | tf_op jit(solution)/shard_map/dot_general | solution.py:1427
  363.5 8.8 %convolution_convert_fusion.4.down_partial = bf16[960,2560]{1,0:T(8,128)(2,1)} fusion(bf16[1024,960]{1,0:T(8,128)(2,1)} %get-tuple-element.98, bf16[1024,2560]{1,0:T(8,128)(2,1)S(1)} %bitcast.142), kind=kOutput, calls=%fused_computation.5 | convolution fusion | flops 5035622400 | bytes 12124160 | tf_op jit(solution)/shard_map/dot_general | solution.py:1431
  372.2 73.4 %second_norm_back.1 = (f32[128,2560]{1,0:T(8,128)}, bf16[1024,640]{1,0:T(8,128)(2,1)}, f32[8,2560]{1,0:T(8,128)}, f32[960,640]{1,0:T(8,128)}) custom-call(bf16[4,2,128,2560]{3,2,1,0:T(8,128)(2,1)} %bitcast.143, bf16[1024,2560]{1,0:T(8,128)(2,1)} %get-tuple-element.95.cot_all, f32[128,2560]{1,0:T(8,128)} %get-tuple-element.96.middle, ...), custom_call_target="tpu_custom_call" | custom-call | tf_op jit(solution)/shard_map/second_norm_back/pallas_call | solution.py:432
  445.6 5.7 convolution_convert_fusion.6.mixed_partial
  451.4 7.5 convolution_convert_fusion.1
  458.9 7.2 convolution_convert_fusion.3
  466.2 7.9 copy.60.gate_partial
  474.1 83.7 %mixed_and_output.1 = (f32[2,128,1280]{2,1,0:T(8,128)}, bf16[4,128,640]{2,1,0:T(8,128)(2,1)}, bf16[2,320,960]{2,1,0:T(8,128)(2,1)}) custom-call(bf16[1024,1280]{1,0:T(8,128)(2,1)} %convolution_convert_fusion.6.mixed_partial, bf16[4,2,128,2560]{3,2,1,0:T(8,128)(2,1)} %bitcast.145, f32[128,2560]{1,0:T(8,128)} %get-tuple-element.96.middle, ...), custom_call_target="tpu_custom_call" | custom-call | tf_op jit(solution)/shard_map/mixed_and_output/pallas_call | solution.py:432
  557.8 2.3 fusion.9
  560.3 30.4 %recurrence_backward.1 = (bf16[256,1280]{1,0:T(8,128)(2,1)}, f32[16,1280]{1,0:T(8,128)}, f32[10,256,256]{2,1,0:T(8,128)}) custom-call(f32[264,1280]{1,0:T(8,128)} %get-tuple-element.103.proj, f32[256,1280]{1,0:T(8,128)} %get-tuple-element.104.side, s32[256,1]{1,0:T(8,128)} %copy.59.spots, f32[16,1280]{1,0:T(8,128)} %get-tuple-element.105.vectors, ...), custom_call_target="tpu_custom_call" | custom-call | tf_op jit(solution)/shard_map/recurrence_backward/pallas_call | solution.py:432
  590.8 1.5 slice_bitcast_fusion.23
  592.2 1.5 maximum_maximum_fusion.blocks
  594.2 9.8 %convolution_convert_fusion.2 = bf16[2560,960]{0,1:T(8,128)(2,1)} fusion(bf16[1024,2560]{1,0:T(8,128)(2,1)} %get-tuple-element.101, bf16[1024,960]{1,0:T(8,128)(2,1)S(1)} %copy-done.37), kind=kOutput, calls=%fused_computation.3 | convolution fusion | flops 5035622400 | bytes 12124160 | tf_op jit(solution)/shard_map/dot_general | solution.py:1431
  604.0 8.0 copy.62.up_partial
  612.1 4.7 convolution_convert_fusion.7
  616.8 61.6 %spread_gradients.1 = (bf16[4,256,640]{2,1,0:T(8,128)(2,1)}, bf16[2,320,960]{2,1,0:T(8,128)(2,1)}, f32[320,640]{1,0:T(8,128)}, bf16[4,160,960]{2,1,0:T(8,128)(2,1)}) custom-call(bf16[4,256,640]{2,1,0:T(8,128)(2,1)} %maximum_maximum_fusion.blocks, bf16[2560,960]{1,0:T(8,128)(2,1)} %copy.62.up_partial, bf16[4,320,640]{2,1,0:T(8,128)(2,1)} %bitcast.151, ...), custom_call_target="tpu_custom_call" | custom-call | tf_op jit(solution)/shard_map/spread_gradients/pallas_call | solution.py:432
  678.4 7.5 convolution_convert_fusion
  686.0 5.9 convolution_convert_fusion.5
  691.9 1.4 scatter.4.channel_in
  694.1 1.2 copy.63
  695.3 123.3 %first_norm_back.1 = (f32[4,128,640]{2,1,0:T(8,128)}, bf16[4,160,640]{2,1,0:T(8,128)(2,1)}, bf16[4,160,960]{2,1,0:T(8,128)(2,1)}, f32[2,8,640]{2,1,0:T(8,128)}, ...) custom-call(bf16[2,4,128,2560]{3,2,1,0:T(8,128)(2,1)} %bitcast.140, ...), custom_call_target="tpu_custom_call" | custom-call | tf_op jit(solution)/shard_map/first_norm_back/pallas_call | solution.py:432
  818.6 1.5 slice_bitcast_fusion.32
  820.4 0.9 convert_element_type.99
  821.5 0.9 convert_element_type.100
  822.6 1.2 concatenate.37
  823.8 1.6 convert_element_type.101
  825.8 1.2 concatenate.38
  827.0 1.6 convert_element_type.102
  828.7 0.7 copy.64
  829.5 0.7 copy.65
  830.2 1.4 constant_dynamic-slice_fusion
  831.6 1.6 fusion.8
  834.4 1.4 fusion.13
  835.9 0.8 copy.71
  836.7 1.1 copy.72
  837.8 0.9 copy.73
  839.2 1.4 copy.74
  (137 shorter events, 8.5 us)
Async XLA Ops:
  0.7 1.4 copy-start.10
  2.1 1.4 copy-start.11
  2.4 2.1 copy-start.2
  4.6 1.7 copy-start.3
  6.7 2.6 copy-start.4
  9.3 1.3 copy-start.15
  9.3 2.0 copy-start.19
  9.3 2.0 copy-start.23
  9.3 2.0 copy-start.24
  9.3 2.1 copy-start.25
  9.3 2.1 copy-start.26
  9.3 2.1 copy-start.27
  9.3 2.1 copy-start.20
  9.4 2.7 copy-start.29
  9.4 2.7 copy-start.30
  9.4 2.7 copy-start.31
  9.4 2.7 copy-start.32
  9.4 3.3 copy-start.28
  13.5 193.5 %copy-start.21 = (f32[960]{0:T(1024)S(1)}, f32[960]{0:T(1024)}, u32[]{:S(2)}) copy-start(f32[960]{0:T(1024)} %param.45) | copy-start | bytes 11524
  13.6 193.5 %copy-start.22 = (f32[960]{0:T(1024)S(1)}, f32[960]{0:T(1024)}, u32[]{:S(2)}) copy-start(f32[960]{0:T(1024)} %param.44) | copy-start | bytes 11524
  341.9 11.2 %copy-start.33 = (bf16[4,4,160,960]{3,2,1,0:T(8,128)(2,1)S(1)}, bf16[4,4,160,960]{3,2,1,0:T(8,128)(2,1)}, u32[]{:S(2)}) copy-start(bf16[4,4,160,960]{3,2,1,0:T(8,128)(2,1)} %get-tuple-element.94) | copy-start | bytes 14745604
  341.9 11.2 %copy-start.36 = (bf16[1024,960]{1,0:T(8,128)(2,1)S(1)}, bf16[1024,960]{1,0:T(8,128)(2,1)}, u32[]{:S(2)}) copy-start(bf16[1024,960]{1,0:T(8,128)(2,1)} %get-tuple-element.93) | copy-start | bytes 5898244
  341.9 21.6 %slice-start = ((s8[5242880]{0:T(1024)(128)(4,1)}), s8[4194304]{0:T(1024)(128)(4,1)S(1)}, s32[]{:S(2)}) async-start(s8[5242880]{0:T(1024)(128)(4,1)} %bitcast.141), calls=%async_computation | async-start | bytes 8388608
  353.1 10.4 %slice-start.1 = ((s8[5242880]{0:T(1024)(128)(4,1)}), s8[1048576]{0:T(1024)(128)(4,1)S(1)}, s32[]{:S(2)}) async-start(s8[5242880]{0:T(1024)(128)(4,1)} %bitcast.141), calls=%async_computation.1 | async-start | bytes 2097152
  363.5 87.9 %slice-start.2 = ((s8[4915200]{0:T(1024)(128)(4,1)}), s8[720896]{0:T(1024)(128)(4,1)S(1)}, s32[]{:S(2)}) async-start(s8[4915200]{0:T(1024)(128)(4,1)} %bitcast.148), calls=%async_computation.2 | async-start | bytes 1441792
  372.2 79.1 %slice-start.3 = ((s8[4915200]{0:T(1024)(128)(4,1)}), s8[4194304]{0:T(1024)(128)(4,1)S(1)}, s32[]{:S(2)}) async-start(s8[4915200]{0:T(1024)(128)(4,1)} %bitcast.148), calls=%async_computation.3 | async-start | bytes 8388608
  445.6 5.7 copy-start.39
  445.6 13.3 %slice-start.6 = ((s8[5242880]{0:T(1024)(128)(4,1)}), s8[4194304]{0:T(1024)(128)(4,1)S(1)}, s32[]{:S(2)}) async-start(s8[5242880]{0:T(1024)(128)(4,1)} %bitcast.175), calls=%async_computation.6 | async-start | bytes 8388608
  451.4 7.6 slice-start.7
  451.4 7.6 copy-start.38
  474.1 83.7 %copy-start = (f32[256,1280]{1,0:T(8,128)S(1)}, f32[256,1280]{1,0:T(8,128)}, u32[]{:S(2)}) copy-start(f32[256,1280]{1,0:T(8,128)} %get-tuple-element.110.state_in) | copy-start | bytes 3932164
  474.1 83.7 %copy-start.9 = (f32[256,1280]{1,0:T(8,128)S(1)}, f32[256,1280]{1,0:T(8,128)}, u32[]{:S(2)}) copy-start(f32[256,1280]{1,0:T(8,128)} %get-tuple-element.114) | copy-start | bytes 3932164
  592.2 2.0 copy-start.37
  604.0 8.0 copy-start.35
  616.8 61.6 %copy-start.34 = (bf16[4,640,640]{2,1,0:T(8,128)(2,1)S(1)}, bf16[4,640,640]{2,1,0:T(8,128)(2,1)}, u32[]{:S(2)}) copy-start(bf16[4,640,640]{2,1,0:T(8,128)(2,1)} %get-tuple-element.118) | copy-start | bytes 9830404
  616.8 69.2 %slice-start.4 = ((s8[5242880]{0:T(1024)(128)(4,1)}), s8[1048576]{0:T(1024)(128)(4,1)S(1)}, s32[]{:S(2)}) async-start(s8[5242880]{0:T(1024)(128)(4,1)} %bitcast.173), calls=%async_computation.4 | async-start | bytes 2097152
  678.4 7.5 slice-start.5
  678.4 7.5 copy-start.40
  686.0 7.3 copy-start.18
  686.0 7.9 copy-start.1
  820.4 2.1 copy-start.7
  823.8 1.8 copy-start.8
  827.0 1.6 copy-start.16
  828.6 5.2 copy-start.17
  828.7 7.2 copy-start.13
  828.7 8.0 copy-start.6
  835.9 1.9 copy-start.12
  836.7 2.5 copy-start.5
  (1 other events, 1.3 us)

commit v4 on v3

--- a/solution.py
+++ b/solution.py
@@ -15,6 +15,18 @@
 MESH = pl.DeviceIdType.MESH
 VMEM = pl.BlockSpec(memory_space=pltpu.VMEM)
 ANY = pl.BlockSpec(memory_space=pl.ANY)
+
+
+def times(piece, matrix):
+    return jnp.dot(piece, matrix, preferred_element_type=WIDE)
+
+
+def times_flipped(piece, matrix):
+    return lax.dot_general(piece, matrix, (((1,), (1,)), ((), ())), preferred_element_type=WIDE)
+
+
+def left_product(left, right):
+    return lax.dot_general(left, right, (((0,), (0,)), ((), ())), preferred_element_type=WIDE)
 
 
 class Links:
@@ -85,6 +97,15 @@
     live = list(tasks)
     while live:
         live = [task for task in live if next(task, None) is not None]
+
+
+def advance(*tasks):
+    for task in tasks:
+        next(task, None)
+
+
+def finish(*tasks):
+    run(tasks)
 
 
 def chain(*tasks):
@@ -264,8 +285,10 @@
             when(valid, copy.wait_send)
 
 
-def scatter_rows(links, place, part, buffers, result):
+def scatter_rows(links, place, part, buffers, result, prepare=None, gentle=False):
     row, near, side, far = place.near
+    if prepare is not None:
+        prepare(far)
     heights = [part(row, h).shape[0] for h in range(2)]
 
     def buffer(i, h):
@@ -277,8 +300,14 @@
         links.copy(part(side, 0), buffer(4, 0), row=side),
         links.copy(part(near, 1), buffer(6, 1), row=near),
     ]
-    for copy in out:
+    for i, copy in enumerate(out):
+        if i == 2 and gentle:
+            yield 1
+        if i > 1 and prepare is not None:
+            prepare(near if i == 3 else side)
         copy.start()
+    if prepare is not None:
+        prepare(row)
     loads = [
         links.keep(part(near, 0), buffer(0, 0)),
         links.keep(part(side, 1), buffer(1, 1)),
@@ -395,14 +424,35 @@
         when(sends_down(t), downs[t].wait_send)
 
 
+def scatter_line_in_parts(links, place, ready, term, ups_in, downs_in, staging, result):
+    def part(i):
+        return scatter_line(
+            links,
+            place,
+            ready,
+            lambda b, _, rows: term(b, i, rows),
+            ups_in.at[:, pl.ds(i, 1)],
+            downs_in.at[:, pl.ds(i, 1)],
+            staging.at[:, pl.ds(i, 1)],
+            lambda _, rows, value: result(i, rows, value),
+        )
+
+    live = [part(i) for i in range(ups_in.shape[1])]
+    while live:
+        live = [task for task in live if next(task, None) is not None]
+        yield 1
+
+
 def line_buffers(count, pieces, height, width):
     return [pltpu.VMEM((slots, pieces, height, width), LOW) for slots in (count - 1, count - 1, 4)]
 
 
-def token_scatter(links, place, partial, ours, theirs, buffers, result):
+def token_scatter(links, place, partial, ours, theirs, buffers, result, prepare=None):
     out, loads = [], []
     for s in list(range(1, place.count)) + [0]:
         block = place.turn(place.dp - s)
+        if prepare is not None:
+            prepare(block)
         out.append(
             links.copy(partial.at[block, place.other], theirs.at[block], col=place.other)
         )
@@ -417,12 +467,18 @@
             out[at].wait_recv()
             loads[at].wait()
 
+    height = buffers[0].shape[2]
+
+    def at(i, rows):
+        return pl.ds(pl.multiple_of(rows.start + i * height, 16), rows.size)
+
     def term(block, i, rows):
-        return ours[block, rows].astype(WIDE) + theirs[block, rows].astype(WIDE)
+        here = at(i, rows)
+        return ours[block, here].astype(WIDE) + theirs[block, here].astype(WIDE)
 
     yield 1
-    yield from scatter_line(
-        links, place, ready, term, *buffers, lambda i, rows, value: result(rows, value)
+    yield from scatter_line_in_parts(
+        links, place, ready, term, *buffers, lambda i, rows, value: result(at(i, rows), value)
     )
     for copy in out:
         copy.wait_send()
@@ -507,11 +563,12 @@
 def recurrence_backward(
     count, taps, proj, side, spots, vectors, blocks, conv_in, in_gate, dec_gate, state_in, entering,
     grad_mixed, branch_out, sums_out, blocks_out, reach, local_grad, branch, ends, table, heads_in,
-    heads_here, padded, spread, send, recv, local,
+    heads_here, padded, spread, send, recv, local, links=None, between=lambda: None,
 ):
     place = Place(count)
-    links = Links(send, recv, local)
-    greet(place, rows=True)
+    if links is None:
+        links = Links(send, recv, local)
+        greet(place, rows=True)
     tokens, width = side.shape
     heads, block = blocks.shape[0] // 2, blocks.shape[1]
     spot = spots[...]
@@ -533,6 +590,7 @@
     own = links.keep(ends, table.at[place.row])
     own.wait()
     heads_here[0:1, :] = carry_over(links, place, ends, table, True)
+    between()
 
     def one_head(h, at):
         def vector(i):
@@ -593,6 +651,7 @@
     owed.start()
     owed.wait_recv()
     owed.wait_send()
+    between()
 
     def finish(h, at):
         last = jnp.where(row < 3, heads_in[1, :, at], 0.0)
@@ -600,6 +659,65 @@
         branch_out[:, at] = branch[:, at].astype(LOW)
 
     each_head(heads, block, finish)
+
+
+def recurrence_back_inside(
+    count, taps, proj, side, gelu_in, spots, vectors, blocks, conv_in, in_gate, dec_gate, state_in,
+    entering, grad_mixed, output_partial, up_own, sums_out, blocks_out, all_out, output_out, up_out, branch_low, gelu_low, stage, reach, local_grad, branch, ends, table, heads_in,
+    heads_here, padded, spread, ups, downs, staging, own, up_here, send, recv, local,
+):
+    place = Place(count)
+    links = Links(send, recv, local)
+    greet(place, rows=True, line=True)
+    row, z = place.row, place.dp
+    part = stage.shape[2] // 2
+    kept = Relay(links, up_own.at[z], up_here, up_out.at[z])
+    load = links.keep(output_partial, own)
+
+    output_half = ups.shape[2]
+
+    def output_rows(i, rows):
+        return pl.ds(pl.multiple_of(rows.start + i * output_half, 16), rows.size)
+
+    def keep_output(i, rows, value):
+        output_out[output_rows(i, rows)] = value
+
+    output_sum = scatter_line_in_parts(
+        links,
+        place,
+        lambda s: None,
+        lambda b, i, rows: own[b, output_rows(i, rows)].astype(WIDE),
+        ups,
+        downs,
+        staging,
+        keep_output,
+    )
+    up_line = exchange_line(links, place, lambda b: up_own.at[b], lambda b: up_out.at[b])
+    load.wait()
+    advance(output_sum, up_line)
+    kept.pass_on()
+
+    def gelu_back(h, at):
+        grad = grad_mixed[:, at] * state_in[:, at] * gelu_slope(gelu_in[:, at])
+        gelu_low[:, at] = grad.astype(LOW)
+        spread[0:1, :] = jnp.sum(grad, axis=0, keepdims=True)
+        sums_out[taps + 5 : taps + 6, at] = spread[0:1, :]
+
+    recurrence_backward(
+        count, taps, proj, side, spots, vectors, blocks, conv_in, in_gate, dec_gate, state_in, entering,
+        grad_mixed, branch_low, sums_out, blocks_out, reach, local_grad, branch, ends, table, heads_in,
+        heads_here, padded, spread, None, None, None, links, lambda: advance(output_sum),
+    )
+    each_head(blocks.shape[0] // 2, blocks.shape[1], gelu_back)
+    for q in range(4):
+        at = slice(q * part, (q + 1) * part)
+        stage[q, :, :part] = branch_low[:, at]
+        stage[q, :, part:] = gelu_low[:, at]
+    mine = links.keep(stage.at[row], all_out.at[row])
+    spread_out = exchange_rows(links, place, lambda q: stage.at[q], lambda q: all_out.at[q])
+    run([spread_out, output_sum, up_line])
+    mine.wait()
+    kept.wait()
 
 
 def norm_rule(rows, grad, value, gain, sums, at):
@@ -611,18 +729,76 @@
     return inverse * scaled - value * (inverse * inverse * inverse) * (inner / full)
 
 
-def second_norm_back(
-    count, grad_partial, cot_all, middle, vectors, down_partial, grad_middle, grad_all, sums, down_out,
-    ours, theirs, ups, downs, staging, cot, low, buffers, send, recv, local,
+def second_norm_back_inside(
+    count, grad_gate, grad_up, gate_all, up_all, normed, cot_all, middle, vectors, grad_middle, grad_all,
+    sums, gate_out, ours, theirs, ups, downs, staging, cot, low, buffers, gate_v, up_v, gate_w, up_w,
+    tile, partial, gate_partial, send, recv, local,
 ):
     place = Place(count)
     links = Links(send, recv, local)
     greet(place, rows=True, line=True, cores=True)
+    loads = [links.keep(grad_gate, gate_v), links.keep(grad_up, up_v)]
+    pieces = [
+        (links.keep(gate_all.at[q], gate_w.at[q]), links.keep(up_all.at[q], up_w.at[q]))
+        for q in range(4)
+    ]
+    quarter, full = middle.shape
+    narrow, units = full // 4, gate_v.shape[1]
+    for load in loads:
+        load.wait()
+    first = [True]
+
+    def tokens(block):
+        rows = strip(block, 2 * quarter)
+
+        def lap(q, carry):
+            total = sum(
+                times_flipped(values[rows, :], weight[q].astype(LOW).reshape(narrow, units))
+                for values, weight in ((gate_v, gate_w), (up_v, up_w))
+            ).astype(LOW)
+            for core in range(2):
+                partial[block, core, :, lanes(q, narrow)] = total[
+                    core * quarter : (core + 1) * quarter
+                ]
+            return carry
+
+        if first:
+            first.clear()
+            for q in range(4):
+                for load in pieces[q]:
+                    load.wait()
+                lap(q, 0)
+        else:
+            lax.fori_loop(0, 4, lap, 0)
+
+    k, links.kept = links.kept, links.kept + 1
+
+    def gate(q):
+        load = pltpu.make_async_copy(normed.at[:, lanes(q, narrow)], tile, links.local.at[k])
+        load.start()
+        load.wait()
+        gate_partial[strip(q, narrow)] = left_product(tile[...], gate_v[...]).astype(LOW)
+
+    second_norm_back(
+        count, partial, cot_all, middle, vectors, gate_partial, grad_middle, grad_all, sums, gate_out,
+        ours, theirs, ups, downs, staging, cot, low, buffers, None, None, None, links, tokens, gate,
+    )
+
+
+def second_norm_back(
+    count, grad_partial, cot_all, middle, vectors, gate_partial, grad_middle, grad_all, sums, gate_out,
+    ours, theirs, ups, downs, staging, cot, low, buffers, send, recv, local, links=None,
+    prepare_tokens=None, prepare_gate=None,
+):
+    place = Place(count)
+    if links is None:
+        links = Links(send, recv, local)
+        greet(place, rows=True, line=True, cores=True)
     row, z, col = place.row, place.dp, place.col
     quarter, full = middle.shape
     narrow = full // 4
     tall = 4 * quarter
-    down_halves = halves(down_partial.shape[0])
+    half = gate_partial.shape[0] // 8
     sums[...] = jnp.zeros(sums.shape, WIDE)
     gain = vectors[3:4, :]
     load = links.keep(cot_all.at[strip(2 * z + col, quarter)], cot)
@@ -638,7 +814,7 @@
     def tokens():
         load.wait()
         yield from token_scatter(
-            links, place, grad_partial, ours, theirs, (ups, downs, staging), back
+            links, place, grad_partial, ours, theirs, (ups, downs, staging), back, prepare_tokens
         )
 
         def block(q):
@@ -656,42 +832,107 @@
         share.wait_recv()
         share.wait_send()
 
-    def keep_down(h, rows, value):
-        down_out[pl.ds(pl.multiple_of(down_halves[h].start + rows.start, 16), rows.size)] = value
-
-    run(
-        [
-            tokens(),
-            scatter_rows(
-                links,
-                place,
-                lambda q, h: down_partial.at[down_halves[h], lanes(q, narrow)],
-                buffers,
-                keep_down,
-            ),
-        ]
-    )
-
-
-def mixed_and_output(
-    count, mixed_partial, out_partial, middle, vectors, gate_partial, mixed_out, layer_out, gate_out,
-    mixed_buffers, ours, theirs, ups, downs, staging, low, gate_buffers, send, recv, local,
+    def keep_gate(h, rows, value):
+        gate_out[h, rows] = value.astype(LOW)
+
+    tokens_back = tokens()
+    gate_back = scatter_rows(
+        links,
+        place,
+        lambda q, h: gate_partial.at[strip(2 * q + h, half)],
+        buffers,
+        keep_gate,
+        prepare_gate,
+    )
+    advance(tokens_back)
+    advance(tokens_back)
+    run([gate_back, tokens_back])
+
+
+def mixed_and_output_inside(
+    count, grad_all, wout, mixed_all, normed, cot_all, grad_up, hidden, out_partial, middle, vectors, gate_own,
+    mixed_out, layer_out, up_out, gate_out, output_out, down_out, mixed_buffers, ours, theirs, ups, downs,
+    staging, low, up_buffers, gate_here, grad_v, wout_v, mixed_v, tile, up_v, hidden_v, mixed_partial,
+    up_partial, output_v, down_v, send, recv, local,
 ):
     place = Place(count)
     links = Links(send, recv, local)
     greet(place, rows=True, line=True, cores=True)
+    loads = [
+        links.keep(source, target)
+        for source, target in (
+            (grad_all, grad_v), (wout, wout_v), (grad_up, up_v), (mixed_all, mixed_v),
+            (hidden, hidden_v),
+        )
+    ]
+    steps = mixed_partial.shape[0] // 4
+    narrow = grad_v.shape[1]
+    for load in loads[:2]:
+        load.wait()
+
+    def mixed(q):
+        rows = strip(q, steps)
+        mixed_partial[rows] = times_flipped(grad_v[rows, :], wout_v[...]).astype(LOW)
+
+    k, links.kept = links.kept, links.kept + 1
+
+    def fetch(source, q):
+        load = pltpu.make_async_copy(source.at[:, lanes(q, narrow)], tile, links.local.at[k])
+        load.start()
+        load.wait()
+
+    def up(q):
+        fetch(normed, q)
+        up_partial[strip(q, narrow)] = left_product(tile[...], up_v[...]).astype(LOW)
+
+    def ready():
+        for load in loads[2:]:
+            load.wait()
+
+    def others():
+        output_v[...] = left_product(mixed_v[...], grad_v[...]).astype(LOW)
+        stores = [links.keep(output_v, output_out)]
+
+        def lap(q, carry):
+            fetch(cot_all, q)
+            down_v[:, lanes(q, narrow)] = left_product(hidden_v[...], tile[...]).astype(LOW)
+            return carry
+
+        lax.fori_loop(0, 4, lap, 0)
+        stores.append(links.keep(down_v, down_out))
+        yield 1
+        for store in stores:
+            store.wait()
+
+    mixed_and_output(
+        count, mixed_partial, out_partial, middle, vectors, up_partial, gate_own, mixed_out, layer_out,
+        up_out, gate_out, mixed_buffers, ours, theirs, ups, downs, staging, low, up_buffers, gate_here, None,
+        None, None, links, ready, mixed, up, others(),
+    )
+
+
+def mixed_and_output(
+    count, mixed_partial, out_partial, middle, vectors, up_partial, gate_own, mixed_out, layer_out, up_out,
+    gate_out, mixed_buffers, ours, theirs, ups, downs, staging, low, up_buffers, gate_here, send, recv,
+    local, links=None, ready=None, prepare_mixed=None, prepare_up=None, others=None,
+):
+    place = Place(count)
+    if links is None:
+        links = Links(send, recv, local)
+        greet(place, rows=True, line=True, cores=True)
     row = place.row
     quarter, full = middle.shape
     narrow = full // 4
     shift = vectors[2:3, :]
     half = mixed_partial.shape[0] // 8
-    gate_half = gate_partial.shape[0] // 8
+    up_half = up_partial.shape[0] // 8
+    kept = Relay(links, gate_own.at[place.dp], gate_here, gate_out.at[place.dp])
 
     def keep_mixed(h, rows, value):
         mixed_out[h, rows] = value
 
-    def keep_gate(h, rows, value):
-        gate_out[h, rows] = value.astype(LOW)
+    def keep_up(h, rows, value):
+        up_out[h, rows] = value.astype(LOW)
 
     def finish(rows, value):
         low[rows] = (middle[rows] + value + shift).astype(LOW)
@@ -706,53 +947,62 @@
         )
         mine.wait()
 
-    run(
-        [
-            scatter_rows(
-                links,
-                place,
-                lambda q, h: mixed_partial.at[strip(2 * q + h, half)],
-                mixed_buffers,
-                keep_mixed,
-            ),
-            tokens(),
-            scatter_rows(
-                links,
-                place,
-                lambda q, h: gate_partial.at[strip(2 * q + h, gate_half)],
-                gate_buffers,
-                keep_gate,
-            ),
-        ]
-    )
+    outs = tokens()
+    mixes = scatter_rows(
+        links,
+        place,
+        lambda q, h: mixed_partial.at[strip(2 * q + h, half)],
+        mixed_buffers,
+        keep_mixed,
+        prepare_mixed,
+    )
+    sums_up = scatter_rows(
+        links,
+        place,
+        lambda q, h: up_partial.at[strip(2 * q + h, up_half)],
+        up_buffers,
+        keep_up,
+        prepare_up,
+    )
+    gates = exchange_line(links, place, lambda b: gate_own.at[b], lambda b: gate_out.at[b])
+    advance(outs, mixes, outs)
+    kept.pass_on()
+    if ready is not None:
+        ready()
+    advance(sums_up, mixes, outs, gates)
+    if others is not None:
+        advance(others)
+    advance(mixes)
+    run([outs, sums_up, mixes, gates] + ([others] if others is not None else []))
+    kept.wait()
 
 
 def spread_gradients(
-    count, blocks, up_partial, output_partial, gate_own, all_out, up_out, output_out, gate_out,
-    up_buffers, ups, downs, staging, own, send, recv, local,
+    count, blocks, output_partial, up_own, all_out, output_out, up_out, ups, downs, staging, own, send, recv, local,
 ):
     place = Place(count)
     links = Links(send, recv, local)
     greet(place, rows=True, line=True)
     row, z = place.row, place.dp
-    half = up_partial.shape[0] // 8
     mine = links.keep(blocks.at[row], all_out.at[row])
-    kept = links.keep(gate_own.at[z], gate_out.at[z])
+    kept = links.keep(up_own.at[z], up_out.at[z])
     load = links.keep(output_partial, own)
 
-    def keep_up(h, rows, value):
-        up_out[h, rows] = value.astype(LOW)
+    output_half = ups.shape[2]
+
+    def output_rows(i, rows):
+        return pl.ds(pl.multiple_of(rows.start + i * output_half, 16), rows.size)
 
     def keep_output(i, rows, value):
-        output_out[rows] = value
+        output_out[output_rows(i, rows)] = value
 
     def outputs():
         load.wait()
-        yield from scatter_line(
+        yield from scatter_line_in_parts(
             links,
             place,
             lambda s: None,
-            lambda b, i, rows: own[b, rows].astype(WIDE),
+            lambda b, i, rows: own[b, output_rows(i, rows)].astype(WIDE),
             ups,
             downs,
             staging,
@@ -763,16 +1013,7 @@
         [
             exchange_rows(links, place, lambda q: blocks.at[q], lambda q: all_out.at[q]),
             outputs(),
-            exchange_line(
-                links, place, lambda b: gate_own.at[b], lambda b: gate_out.at[b]
-            ),
-            scatter_rows(
-                links,
-                place,
-                lambda q, h: up_partial.at[strip(2 * q + h, half)],
-                up_buffers,
-                keep_up,
-            ),
+            exchange_line(links, place, lambda b: up_own.at[b], lambda b: up_out.at[b]),
         ]
     )
     mine.wait()
@@ -780,27 +1021,45 @@
 
 
 def first_norm_back(
-    count, grad_partial, x_own, grad_middle, vectors, proj_partial, up_own, sums_in, channel_in,
-    hidden_in, block_in, grad_out, proj_out, up_out, width_sums, channel_sums, block_out, hidden_sums,
+    count, grad_partial, x_own, grad_middle, vectors, proj_partial, down_partial, sums_in,
+    channel_in, hidden_in, block_in, grad_out, proj_out, down_out, width_sums, channel_sums, block_out, hidden_sums,
     theirs, ours, added,
     row_buffer, x, result, sums, proj_own, proj_ups, proj_downs, proj_staging, proj_low, width_table,
     width_line, width_part, channel_table, channel_line, hidden_table, block_buffers, block_sum, block_ups, block_downs,
-    block_staging, block_low, send, recv, local,
+    block_staging, block_low, down_buffers, send, recv, local, links=None, prepare_tokens=None, prepare_proj=None,
 ):
     place = Place(count)
-    links = Links(send, recv, local)
-    greet(place, rows=True, line=True, cores=True)
+    if links is None:
+        links = Links(send, recv, local)
+        greet(place, rows=True, line=True, cores=True)
     row, z, col = place.row, place.dp, place.col
     quarter, full = grad_middle.shape
     narrow = full // 4
     gain = vectors[0:1, :]
     load_x = links.keep(x_own, x)
-    load_proj = [links.keep(proj_partial.at[:, b], proj_own.at[b]) for b in range(count)]
-    kept = links.keep(up_own.at[z], up_out.at[z])
+    if prepare_proj is None:
+        load_proj = [links.keep(proj_partial.at[:, b], proj_own.at[b]) for b in range(count)]
+
+    parts = halves(down_partial.shape[0])
+
+    def keep_down(h, rows, value):
+        down_out[pl.ds(pl.multiple_of(parts[h].start + rows.start, 16), rows.size)] = value
+
+    down_sum = scatter_rows(
+        links,
+        place,
+        lambda q, h: down_partial.at[parts[h], lanes(q, narrow)],
+        down_buffers,
+        keep_down,
+    )
 
     def tokens():
+        if prepare_tokens is not None:
+            prepare_tokens(place.other)
         share = links.copy(grad_partial.at[place.other], theirs, col=place.other)
         share.start()
+        if prepare_tokens is not None:
+            prepare_tokens(col)
         load = links.keep(grad_partial.at[col], ours)
         yield 1
         share.wait_recv()
@@ -860,13 +1119,16 @@
         last.wait_send()
 
     def projections():
-        for load in load_proj:
-            load.wait()
+        if prepare_proj is None:
+            for load in load_proj:
+                load.wait()
+        else:
+            prepare_proj()
 
         def keep_proj(i, rows, value):
             proj_low[i, rows] = value.astype(LOW)
 
-        yield from scatter_line(
+        yield from scatter_line_in_parts(
             links,
             place,
             lambda s: None,
@@ -928,33 +1190,63 @@
         def keep_line(i, rows, value):
             block_low[rows] = value.astype(LOW)
 
-        yield from scatter_line(
+        yield from scatter_line_in_parts(
             links, place, lambda s: None, term, block_ups, block_downs, block_staging, keep_line
         )
         mine = links.keep(block_low, block_out.at[row])
         yield from exchange_rows(links, place, lambda q: block_low, lambda q: block_out.at[q])
         mine.wait()
 
-    run(
-        [
-            tokens(),
-            projections(),
-            exchange_line(links, place, lambda b: up_own.at[b], lambda b: up_out.at[b]),
-            channels(),
-            hidden(),
-            blocks(),
-        ]
-    )
-    kept.wait()
-
-
-def advance(*tasks):
-    for task in tasks:
-        next(task, None)
-
-
-def finish(*tasks):
-    run(tasks)
+    proj_sum, token_sum = projections(), tokens()
+    small = [channels(), hidden(), blocks()]
+    advance(down_sum, proj_sum, token_sum, *small)
+    advance(token_sum)
+    run([proj_sum, token_sum, down_sum] + small)
+
+
+def first_norm_back_inside(
+    count, grad_proj, wxy, nf, x_own, grad_middle, vectors, down_partial, *refs
+):
+    rest, (grad_v, wxy_v, nf_v, partial, send, recv, local) = refs[:-7], refs[-7:]
+    proj_own = rest[18]
+    place = Place(count)
+    links = Links(send, recv, local)
+    greet(place, rows=True, line=True, cores=True)
+    loads = [
+        links.keep(source, target)
+        for source, target in ((grad_proj, grad_v), (nf, nf_v), (wxy, wxy_v))
+    ]
+    quarter, full = grad_middle.shape
+    narrow, tall = full // 4, 4 * quarter
+    depth = proj_own.shape[2]
+
+    def tokens(core):
+        def lap(q, carry):
+            total = times_flipped(
+                grad_v[strip(core, tall), :], wxy_v[strip(q, narrow), :]
+            ).astype(LOW)
+            for r in range(4):
+                partial[core, r, :, lanes(q, narrow)] = total[r * quarter : (r + 1) * quarter]
+            return carry
+
+        lax.fori_loop(0, 4, lap, 0)
+
+    def proj():
+        for load in loads:
+            load.wait()
+
+        def lap(q, carry):
+            total = left_product(nf_v[:, lanes(q, narrow)], grad_v[...]).astype(LOW)
+            for b in range(count):
+                proj_own[b, q] = total[b * depth : (b + 1) * depth]
+            return carry
+
+        lax.fori_loop(0, 4, lap, 0)
+
+    first_norm_back(
+        count, partial, x_own, grad_middle, vectors, None, down_partial, *rest, None, None, None, links,
+        tokens, proj,
+    )
 
 
 def gelu(v):
@@ -1417,18 +1709,6 @@
     kept.append(links.keep(grad_up, up_out))
     for copy in kept:
         copy.wait()
-
-
-def times(piece, matrix):
-    return jnp.dot(piece, matrix, preferred_element_type=WIDE)
-
-
-def times_flipped(piece, matrix):
-    return lax.dot_general(piece, matrix, (((1,), (1,)), ((), ())), preferred_element_type=WIDE)
-
-
-def left_product(left, right):
-    return lax.dot_general(left, right, (((0,), (0,)), ((), ())), preferred_element_type=WIDE)
 
 
 def side_by_side(blocks):
@@ -1673,144 +1953,270 @@
         remote,
         local,
     )
-    gate_all = gate_all.reshape(full, hidden_part).astype(LOW)
-    up_all = up_all.reshape(full, hidden_part).astype(LOW)
     by_device = (count, cores, quarter, full)
-    grad_normed_second = (
-        (times_flipped(grad_gate_low, gate_all) + times_flipped(grad_up_low, up_all))
-        .astype(LOW)
-        .reshape(by_device)
-    )
-    down_partial = left_product(hidden, cot_all).astype(LOW)
     token_scratch = [
         pltpu.VMEM((count, quarter, full), LOW),
         pltpu.VMEM((count, quarter, full), LOW),
-        *line_buffers(count, 1, quarter, full),
+        *line_buffers(count, 2, quarter // 2, full),
     ]
     token_low = pltpu.VMEM((quarter, full), LOW)
-    grad_middle, grad_middle_all, width_sums, down_grad = call(
-        functools.partial(second_norm_back, count),
-        "second_norm_back",
-        5,
-        [
-            (grad_normed_second, False),
-            (cot_all, False),
-            (middle, True),
-            (width_all, True),
-            (down_partial, False),
-        ],
-        [
-            ((quarter, full), WIDE, True),
-            ((tokens, narrow), LOW, False),
-            ((8, full), WIDE, True),
-            ((hidden_part, narrow), WIDE, True),
-        ],
-        token_scratch + [token_low, token_low, row_buffers(hidden_part, narrow)],
-        remote,
-        local,
-    )
-    gate_partial = left_product(normed_second, grad_gate_low).astype(LOW)
-    up_partial = left_product(normed_second, grad_up_low).astype(LOW)
+    back_outs = [
+        ((quarter, full), WIDE, True),
+        ((tokens, narrow), LOW, False),
+        ((8, full), WIDE, True),
+        ((2, narrow // 2, hidden_part), LOW, True),
+    ]
+    back_scratch = token_scratch + [token_low, token_low, row_buffers(narrow, hidden_part)]
+    inside = count <= 4
+    if inside:
+        grad_middle, grad_middle_all, width_sums, gate_own = call(
+            functools.partial(second_norm_back_inside, count),
+            "second_norm_back",
+            5,
+            [
+                (grad_gate_low, False),
+                (grad_up_low, False),
+                (gate_all, False),
+                (up_all, False),
+                (normed_second, False),
+                (cot_all, False),
+                (middle, True),
+                (width_all, True),
+            ],
+            back_outs,
+            back_scratch
+            + [
+                units_low,
+                units_low,
+                weight_scratch,
+                weight_scratch,
+                pltpu.VMEM((hidden_tokens, narrow), LOW),
+                pltpu.VMEM(by_device, LOW),
+                pltpu.VMEM((full, hidden_part), LOW),
+            ],
+            remote,
+            local,
+        )
+    else:
+        gate_all = gate_all.reshape(full, hidden_part).astype(LOW)
+        up_all = up_all.reshape(full, hidden_part).astype(LOW)
+        grad_normed_second = (
+            (times_flipped(grad_gate_low, gate_all) + times_flipped(grad_up_low, up_all))
+            .astype(LOW)
+            .reshape(by_device)
+        )
+        grad_middle, grad_middle_all, width_sums, gate_own = call(
+            functools.partial(second_norm_back, count),
+            "second_norm_back",
+            5,
+            [
+                (grad_normed_second, False),
+                (cot_all, False),
+                (middle, True),
+                (width_all, True),
+                (left_product(normed_second, grad_gate_low).astype(LOW), False),
+            ],
+            back_outs,
+            back_scratch,
+            remote,
+            local,
+        )
     forward_partial = times(hidden, down_all).astype(LOW).reshape(by_device)
 
-    mixed_partial = times_flipped(grad_middle_all, wout_all).astype(LOW)
-    output_partial = left_product(mixed_all, grad_middle_all).astype(LOW)
-    grad_mixed, layer_out, gate_own = call(
-        functools.partial(mixed_and_output, count),
-        "mixed_and_output",
-        6,
-        [
-            (mixed_partial, False),
-            (forward_partial, False),
-            (middle, True),
-            (width_all, True),
-            (gate_partial, False),
-        ],
-        [
-            ((2, steps // 2, width), WIDE, True),
-            ((rows_count, quarter, narrow), LOW, False),
-            ((2, narrow // 2, hidden_part), LOW, True),
-        ],
+    mixed_outs = [
+        ((2, steps // 2, width), WIDE, True),
+        ((rows_count, quarter, narrow), LOW, False),
+        ((2, narrow // 2, hidden_part), LOW, True),
+        ((count, depth, hidden_part), LOW, False),
+    ]
+    mixed_scratch = (
         [row_buffers(steps, width)]
         + token_scratch
-        + [token_low, row_buffers(narrow, hidden_part)],
-        remote,
-        local,
-    )
+        + [token_low, row_buffers(narrow, hidden_part), pltpu.VMEM((depth, hidden_part), LOW)]
+    )
+    gate_own = gate_own.reshape(count, depth, hidden_part)
+    if inside:
+        grad_mixed, layer_out, up_own, gate_blocks, output_partial, down_partial = call(
+            functools.partial(mixed_and_output_inside, count),
+            "mixed_and_output",
+            6,
+            [
+                (grad_middle_all, False),
+                (wout_all, False),
+                (mixed_all, False),
+                (normed_second, False),
+                (cot_all, False),
+                (grad_up_low, False),
+                (hidden, False),
+                (forward_partial, False),
+                (middle, True),
+                (width_all, True),
+                (gate_own, False),
+            ],
+            mixed_outs + [((width, narrow), LOW, False), ((hidden_part, full), LOW, False)],
+            mixed_scratch
+            + [
+                pltpu.VMEM((tokens, narrow), LOW),
+                pltpu.VMEM((width, narrow), LOW),
+                pltpu.VMEM((tokens, width), LOW),
+                pltpu.VMEM((hidden_tokens, narrow), LOW),
+                units_low,
+                units_low,
+                pltpu.VMEM((tokens, width), LOW),
+                pltpu.VMEM((full, hidden_part), LOW),
+                pltpu.VMEM((width, narrow), LOW),
+                pltpu.VMEM((hidden_part, full), LOW),
+            ],
+            remote,
+            local,
+        )
+    else:
+        down_partial = left_product(hidden, cot_all).astype(LOW)
+        output_partial = left_product(mixed_all, grad_middle_all).astype(LOW)
+        grad_mixed, layer_out, up_own, gate_blocks = call(
+            functools.partial(mixed_and_output, count),
+            "mixed_and_output",
+            6,
+            [
+                (times_flipped(grad_middle_all, wout_all).astype(LOW), False),
+                (forward_partial, False),
+                (middle, True),
+                (width_all, True),
+                (left_product(normed_second, grad_up_low).astype(LOW), False),
+                (gate_own, False),
+            ],
+            mixed_outs,
+            mixed_scratch,
+            remote,
+            local,
+        )
+    up_own = up_own.reshape(count, depth, hidden_part)
     grad_mixed = grad_mixed.reshape(steps, width)
 
-    grad_gelu = gelu_pull(grad_mixed * state)[0]
-    grad_branch_low, channel_part, block_sums = call(
-        functools.partial(recurrence_backward, count, taps),
-        "recurrence_backward",
-        7,
-        [
-            (array, True)
-            for array in (
-                branch,
-                side,
-                spots,
-                vectors,
-                blocks,
-                conv,
-                input_gate,
-                decay_gate,
-                state,
-                entering,
-                grad_mixed,
-            )
-        ],
-        [
-            ((steps, width), LOW, True),
-            ((round_up(taps + 6, 8), width), WIDE, True),
-            ((2 * heads, block, block), WIDE, True),
-        ],
-        [
-            tokens_scratch,
-            tokens_scratch,
-            tokens_scratch,
-            eight_rows,
-            table_rows,
-            pltpu.VMEM((2, 8, width), WIDE),
-            eight_rows,
-            pltpu.VMEM((steps + 8, block), WIDE),
-            pltpu.VMEM((steps + 8, block), WIDE),
-        ],
-        remote,
-        local,
-    )
-    grad_gelu_low = grad_gelu.astype(LOW)
-    projected_grads = jnp.concatenate(
-        (columns(grad_branch_low, rows_count), columns(grad_gelu_low, rows_count)), axis=2
-    )
-    grad_projected, up_own, output_grad, gate_blocks = call(
-        functools.partial(spread_gradients, count),
-        "spread_gradients",
-        8,
-        [
-            (projected_grads, False),
-            (up_partial, False),
-            (output_partial.reshape((count,) + output_matrix.shape), False),
-            (gate_own.reshape(count, depth, hidden_part), False),
-        ],
-        [
-            ((rows_count, steps, 2 * part), LOW, False),
-            ((2, narrow // 2, hidden_part), LOW, True),
-            (output_matrix.shape, WIDE, True),
-            ((count, depth, hidden_part), LOW, False),
-        ],
-        [
-            row_buffers(narrow, hidden_part),
-            *line_buffers(count, 1, *output_matrix.shape),
-            pltpu.VMEM((count,) + output_matrix.shape, LOW),
-        ],
-        remote,
-        local,
-    )
-    grad_projected = grad_projected.reshape(tokens, 2 * part)
-    proj_partial = left_product(normed_first, grad_projected).astype(LOW)
-    grad_normed_first = times_flipped(grad_projected, wxy_all).astype(LOW)
-    channel_part = channel_part.at[taps + 5].set(jnp.sum(grad_gelu, axis=0))
+    sums_rows = round_up(taps + 6, 8)
+    output_parts = 2 if output_matrix.shape[0] % 32 == 0 else 1
+    if inside:
+        channel_part, block_sums, grad_projected, output_grad, up_blocks = call(
+            functools.partial(recurrence_back_inside, count, taps),
+            "recurrence_backward",
+            7,
+            [
+                (array, True)
+                for array in (
+                    branch,
+                    side,
+                    gelu_in,
+                    spots,
+                    vectors,
+                    blocks,
+                    conv,
+                    input_gate,
+                    decay_gate,
+                    state,
+                    entering,
+                    grad_mixed,
+                )
+            ]
+            + [
+                (output_partial.reshape((count,) + output_matrix.shape), False),
+                (up_own, False),
+            ],
+            [
+                ((sums_rows, width), WIDE, True),
+                ((2 * heads, block, block), WIDE, True),
+                ((rows_count, steps, 2 * part), LOW, False),
+                (output_matrix.shape, WIDE, True),
+                ((count, depth, hidden_part), LOW, False),
+            ],
+            [
+                pltpu.VMEM((steps, width), LOW),
+                pltpu.VMEM((steps, width), LOW),
+                pltpu.VMEM((rows_count, steps, 2 * part), LOW),
+                tokens_scratch,
+                tokens_scratch,
+                tokens_scratch,
+                eight_rows,
+                table_rows,
+                pltpu.VMEM((2, 8, width), WIDE),
+                eight_rows,
+                pltpu.VMEM((steps + 8, block), WIDE),
+                pltpu.VMEM((steps + 8, block), WIDE),
+                *line_buffers(count, output_parts, output_matrix.shape[0] // output_parts, narrow),
+                pltpu.VMEM((count,) + output_matrix.shape, LOW),
+                pltpu.VMEM((depth, hidden_part), LOW),
+            ],
+            remote,
+            local,
+        )
+        grad_projected = grad_projected.reshape(tokens, 2 * part)
+    else:
+        grad_gelu = gelu_pull(grad_mixed * state)[0]
+        grad_branch_low, channel_part, block_sums = call(
+            functools.partial(recurrence_backward, count, taps),
+            "recurrence_backward",
+            7,
+            [
+                (array, True)
+                for array in (
+                    branch,
+                    side,
+                    spots,
+                    vectors,
+                    blocks,
+                    conv,
+                    input_gate,
+                    decay_gate,
+                    state,
+                    entering,
+                    grad_mixed,
+                )
+            ],
+            [
+                ((steps, width), LOW, True),
+                ((round_up(taps + 6, 8), width), WIDE, True),
+                ((2 * heads, block, block), WIDE, True),
+            ],
+            [
+                tokens_scratch,
+                tokens_scratch,
+                tokens_scratch,
+                eight_rows,
+                table_rows,
+                pltpu.VMEM((2, 8, width), WIDE),
+                eight_rows,
+                pltpu.VMEM((steps + 8, block), WIDE),
+                pltpu.VMEM((steps + 8, block), WIDE),
+            ],
+            remote,
+            local,
+        )
+        grad_gelu_low = grad_gelu.astype(LOW)
+        projected_grads = jnp.concatenate(
+            (columns(grad_branch_low, rows_count), columns(grad_gelu_low, rows_count)), axis=2
+        )
+        grad_projected, output_grad, up_blocks = call(
+            functools.partial(spread_gradients, count),
+            "spread_gradients",
+            8,
+            [
+                (projected_grads, False),
+                (output_partial.reshape((count,) + output_matrix.shape), False),
+                (up_own, False),
+            ],
+            [
+                ((rows_count, steps, 2 * part), LOW, False),
+                (output_matrix.shape, WIDE, True),
+                ((count, depth, hidden_part), LOW, False),
+            ],
+            [
+                *line_buffers(count, output_parts, output_matrix.shape[0] // output_parts, narrow),
+                pltpu.VMEM((count,) + output_matrix.shape, LOW),
+            ],
+            remote,
+            local,
+        )
+        grad_projected = grad_projected.reshape(tokens, 2 * part)
+        channel_part = channel_part.at[taps + 5].set(jnp.sum(grad_gelu, axis=0))
     hidden_part_sums = padded_rows(hidden_part_sums, 8, round_up(hidden_part, 128))
     block_in = (
         block_sums.astype(LOW)
@@ -1820,53 +2226,86 @@
     )
     channel_shape, sums_shape = channel_part.shape, hidden_part_sums.shape
     block_rows = 2 * heads * back_share
-    input_grad, proj_grad, up_blocks, width_sums, channel_sums, block_grads, hidden_sums = call(
-        functools.partial(first_norm_back, count),
-        "first_norm_back",
-        9,
-        [
-            (grad_normed_first.reshape(cores, rows_count, quarter, full), False),
+    first_outs = [
+        ((rows_count, quarter, narrow), WIDE, False),
+        ((rows_count, depth, 2 * part), LOW, False),
+        ((hidden_part, narrow), WIDE, True),
+        ((2, 8, narrow), WIDE, True),
+        (channel_shape, WIDE, True),
+        ((rows_count, block_rows, block), LOW, False),
+        (sums_shape, WIDE, True),
+    ]
+    first_scratch = [
+        pltpu.VMEM((rows_count, quarter, full), LOW),
+        pltpu.VMEM((rows_count, quarter, full), LOW),
+        pltpu.VMEM((rows_count, quarter, full), LOW),
+        row_buffers(quarter, full),
+        token_low,
+        pltpu.VMEM((rows_count, quarter, narrow), WIDE),
+        pltpu.VMEM((8, full), WIDE),
+        pltpu.VMEM((count, rows_count, depth, 2 * part), LOW),
+        *line_buffers(count, rows_count, depth, 2 * part),
+        pltpu.VMEM((rows_count, depth, 2 * part), LOW),
+        pltpu.VMEM((rows_count, 8, narrow), WIDE),
+        pltpu.VMEM((count, 8, narrow), WIDE),
+        pltpu.VMEM((rows_count, 8, narrow), WIDE),
+        pltpu.VMEM((rows_count,) + channel_shape, WIDE),
+        pltpu.VMEM((count,) + channel_shape, WIDE),
+        pltpu.VMEM((rows_count,) + sums_shape, WIDE),
+        row_buffers(2 * block_in.shape[2], block),
+        pltpu.VMEM((2, block_in.shape[2], block), WIDE),
+        *line_buffers(count, 1, block_rows, block),
+        pltpu.VMEM((block_rows, block), LOW),
+        row_buffers(hidden_part, narrow),
+    ]
+    sums_in = [
+        (width_sums, True),
+        (channel_part, True),
+        (hidden_part_sums, True),
+        (block_in, False),
+    ]
+    if inside:
+        first_kernel, first_ins = first_norm_back_inside, [
+            (grad_projected, False),
+            (wxy_all, False),
+            (normed_first, False),
             (x_own, False),
             (grad_middle, True),
             (width_all, True),
-            (proj_partial.reshape(rows_count, count, depth, 2 * part), False),
-            (up_own.reshape(count, depth, hidden_part), False),
-            (width_sums, True),
-            (channel_part, True),
-            (hidden_part_sums, True),
-            (block_in, False),
-        ],
-        [
-            ((rows_count, quarter, narrow), WIDE, False),
-            ((rows_count, depth, 2 * part), LOW, False),
-            ((count, depth, hidden_part), LOW, False),
-            ((2, 8, narrow), WIDE, True),
-            (channel_shape, WIDE, True),
-            ((rows_count, block_rows, block), LOW, False),
-            (sums_shape, WIDE, True),
-        ],
-        [
-            pltpu.VMEM((rows_count, quarter, full), LOW),
-            pltpu.VMEM((rows_count, quarter, full), LOW),
-            pltpu.VMEM((rows_count, quarter, full), LOW),
-            row_buffers(quarter, full),
-            token_low,
-            pltpu.VMEM((rows_count, quarter, narrow), WIDE),
-            pltpu.VMEM((8, full), WIDE),
-            pltpu.VMEM((count, rows_count, depth, 2 * part), LOW),
-            *line_buffers(count, rows_count, depth, 2 * part),
-            pltpu.VMEM((rows_count, depth, 2 * part), LOW),
-            pltpu.VMEM((rows_count, 8, narrow), WIDE),
-            pltpu.VMEM((count, 8, narrow), WIDE),
-            pltpu.VMEM((rows_count, 8, narrow), WIDE),
-            pltpu.VMEM((rows_count,) + channel_shape, WIDE),
-            pltpu.VMEM((count,) + channel_shape, WIDE),
-            pltpu.VMEM((rows_count,) + sums_shape, WIDE),
-            row_buffers(2 * block_in.shape[2], block),
-            pltpu.VMEM((2, block_in.shape[2], block), WIDE),
-            *line_buffers(count, 1, block_rows, block),
-            pltpu.VMEM((block_rows, block), LOW),
-        ],
+            (down_partial, False),
+        ]
+        first_scratch += [
+            pltpu.VMEM((tokens, 2 * part), LOW),
+            pltpu.VMEM((full, 2 * part), LOW),
+            pltpu.VMEM((tokens, full), LOW),
+            pltpu.VMEM((cores, rows_count, quarter, full), LOW),
+        ]
+    else:
+        first_kernel, first_ins = first_norm_back, [
+            (
+                times_flipped(grad_projected, wxy_all)
+                .astype(LOW)
+                .reshape(cores, rows_count, quarter, full),
+                False,
+            ),
+            (x_own, False),
+            (grad_middle, True),
+            (width_all, True),
+            (
+                left_product(normed_first, grad_projected)
+                .astype(LOW)
+                .reshape(rows_count, count, depth, 2 * part),
+                False,
+            ),
+            (down_partial, False),
+        ]
+    input_grad, proj_grad, down_grad, width_sums, channel_sums, block_grads, hidden_sums = call(
+        functools.partial(first_kernel, count),
+        "first_norm_back",
+        9,
+        first_ins + sums_in,
+        first_outs,
+        first_scratch,
         remote,
         local,
     )

time: 845 us -> 771 us (0.912)
  matrix products: 78.8 us -> 8.96 us
  local copies, waits for them, and re-layouts: 41.3 us -> 22.2 us
  Pallas kernels: 700 us -> 717 us
    dot_general x9 -> x0, matrix products: 71.2 us -> none  [the longest x5 36.5 us: left_product(): lax.dot_general(left, right, (((0,), (0,)), ((), ())), preferred_element_...]
    pallas_call x7 -> x6, Pallas kernels: 700 us -> 717 us  [call(): pl.pallas_call(kernel, in_specs=[VMEM if inside else ANY for _, inside in...]
    convert_element_type x2 -> x0, local copies, waits for them, and re-layouts: 15.9 us -> none  [the longest x1 8.02 us: shards(): up_partial = left_product(normed_second, grad_up_low).astype(LOW)]
where the time goes in v4:
time: 771 us; the launch traced here: 766 us
  Pallas kernels  717 us (93%)
  local copies, waits for them, and re-layouts  22.2 us (3%)
  other arithmetic  17.1 us (2%)
  matrix products  8.96 us (1%)
    pallas_call x6, Pallas kernels, call(): pl.pallas_call(kernel, in_specs=[VMEM if inside else ANY for _, inside in...  717 us

profile of v4, /device:TPU:0, one launch (start us, length us, event | category | flops | bytes accessed | tf_op | source)
XLA Modules:
  0.0 766.3 jit_solution(2385442756652983686)
XLA Ops:
  0.7 1.3 convert_element_type.56
  2.1 0.3 slice_bitcast_fusion.19
  2.4 1.2 maximum_maximum_fusion.wxy
  3.5 0.8 convert_element_type.57.wout
  4.6 0.3 slice_bitcast_fusion.7
  4.9 1.4 copy-done.1
  6.4 0.3 slice_bitcast_fusion.3
  6.7 1.8 pad_maximum_fusion
  8.6 0.7 copy-done.2
  9.3 1.2 convert_element_type.60.wdown
  10.6 0.7 fusion.blk
  11.5 0.6 select_maximum_fusion.cvec
  12.1 0.6 pad.17.wvec
  12.7 0.8 copy.50.spots
  13.6 193.4 %forward.1 = (bf16[1024,2560]{1,0:T(8,128)(2,1)}, bf16[128,2560]{1,0:T(8,128)(2,1)}, bf16[128,2560]{1,0:T(8,128)(2,1)}, bf16[4,640,640]{2,1,0:T(8,128)(2,1)}, bf...) custom-call(bf16[512,640]{1,0:T(8,128)(2,1)} %x.9, ...), custom_call_target="tpu_custom_call" | custom-call | tf_op jit(solution)/shard_map/forward/pallas_call | solution.py:488
  207.0 0.6 pad.18.biases
  207.7 134.3 %feed_forward.1 = (bf16[1024,2560]{1,0:T(8,128)(2,1)}, bf16[1024,2560]{1,0:T(8,128)(2,1)}, bf16[4,4,160,960]{3,2,1,0:T(8,128)(2,1)}, bf16[4,4,160,960]{3,2,1,0:T...) custom-call(bf16[128,2560]{1,0:T(8,128)(2,1)} %get-tuple-element.75., ...), custom_call_target="tpu_custom_call" | custom-call | tf_op jit(solution)/shard_map/feed_forward/pallas_call | solution.py:488
  342.0 92.2 %second_norm_back.1 = (f32[128,2560]{1,0:T(8,128)}, bf16[1024,640]{1,0:T(8,128)(2,1)}, f32[8,2560]{1,0:T(8,128)}, bf16[2,320,960]{2,1,0:T(8,128)(2,1)}) custom-call(bf16[1024,960]{1,0:T(8,128)(2,1)} %get-tuple-element.80.grad_gate, bf16[1024,960]{1,0:T(8,128)(2,1)} %get-tuple-element.81.grad_up, bf16[4,4,160,960]{3,2,1,0:T(8,128)(2,1)} %get-tuple-element.82.gate_all, ...), custom_call_target="tpu_custom_call" | custom-call | tf_op jit(solution)/shard_map/second_norm_back/pallas_call | solution.py:488
  434.2 9.0 %convolution_convert_fusion = bf16[1024,2560]{1,0:T(8,128)(2,1)} fusion(bf16[1024,960]{1,0:T(8,128)(2,1)} %get-tuple-element.91.hidden, bf16[960,2560]{1,0:T(8,128)(2,1)S(1)} %bitcast.103), kind=kOutput, calls=%fused_computation | convolution fusion | flops 5035786240 | bytes 12124160 | tf_op jit(solution)/shard_map/dot_general | solution.py:21
  443.2 102.1 %mixed_and_output.1 = (f32[2,128,1280]{2,1,0:T(8,128)}, bf16[4,128,640]{2,1,0:T(8,128)(2,1)}, bf16[2,320,960]{2,1,0:T(8,128)(2,1)}, bf16[4,160,960]{2,1,0:T(8,12...) custom-call(bf16[1024,640]{1,0:T(8,128)(2,1)} %get-tuple-element.88.grad_all, ...), custom_call_target="tpu_custom_call" | custom-call | tf_op jit(solution)/shard_map/mixed_and_output/pallas_call | solution.py:488
  545.3 66.5 %recurrence_backward.1 = (f32[16,1280]{1,0:T(8,128)}, f32[10,256,256]{2,1,0:T(8,128)}, bf16[4,256,640]{2,1,0:T(8,128)(2,1)}, f32[320,640]{1,0:T(8,128)}, bf16[4,160,960]{2,1,0:T(8,128)(2,1)}) custom-call(f32[264,1280]{1,0:T(8,128)} %get-tuple-element.94.proj, f32[256,1280]{1,0:T(8,128)} %get-tuple-element.95.side, f32[256,1280]{1,0:T(8,128)} %get-tuple-element.96.gelu_in, ...), custom_call_target="tpu_custom_call" | custom-call | tf_op jit(solution)/shard_map/recurrence_backward/pallas_call | solution.py:488
  611.8 0.6 pad.19.refs_2_
  612.4 1.9 convert_element_type.62
  614.3 1.2 copy.52
  615.5 128.0 %first_norm_back.1 = (f32[4,128,640]{2,1,0:T(8,128)}, bf16[4,160,640]{2,1,0:T(8,128)(2,1)}, f32[960,640]{1,0:T(8,128)}, f32[2,8,640]{2,1,0:T(8,128)}, f32[16,128...) custom-call(bf16[1024,640]{1,0:T(8,128)(2,1)} %bitcast.111, bf16[2560,640]{1,0:T(8,128)(2,1)} %bitcast.104, ...), custom_call_target="tpu_custom_call" | custom-call | tf_op jit(solution)/shard_map/first_norm_back/pallas_call | solution.py:488
  743.5 1.5 slice_bitcast_fusion.24
  745.0 0.2 concatenate.29
  745.3 0.9 convert_element_type.63
  746.2 0.2 concatenate.30
  746.4 0.9 convert_element_type.64
  747.4 0.4 copy-done.5
  747.9 1.2 concatenate.31
  749.1 1.6 convert_element_type.65
  750.7 0.2 copy-done.6
  751.1 1.2 concatenate.32
  752.3 1.6 convert_element_type.66
  754.0 0.7 copy.53
  754.8 0.7 copy.54
  755.5 1.4 constant_dynamic-slice_fusion
  756.9 1.6 fusion.2
  758.5 0.6 divide_multiply_fusion
  759.2 0.6 fusion.6
  759.7 1.4 fusion.5
  761.2 0.8 copy.59
  762.0 1.1 copy.60
  763.1 0.9 copy.61
  764.0 0.6 copy-done.3
  764.5 1.4 copy.62
  (82 shorter events, 1.2 us)
Async XLA Ops:
  0.7 1.4 copy-start.7
  2.1 1.4 copy-start.8
  2.4 2.1 copy-start
  4.6 1.7 copy-start.1
  6.7 2.6 copy-start.2
  9.3 1.3 copy-start.11
  9.3 1.3 copy-start.12
  10.5 0.8 copy-start.16
  10.5 0.9 copy-start.20
  10.5 0.9 copy-start.21
  10.5 0.9 copy-start.22
  10.5 0.9 copy-start.23
  10.5 0.9 copy-start.24
  10.5 0.9 copy-start.17
  10.5 1.6 copy-start.26
  10.5 1.6 copy-start.27
  10.5 1.6 copy-start.28
  10.5 1.6 copy-start.29
  10.5 2.2 copy-start.25
  13.5 193.4 %copy-start.18 = (f32[960]{0:T(1024)S(1)}, f32[960]{0:T(1024)}, u32[]{:S(2)}) copy-start(f32[960]{0:T(1024)} %param.43) | copy-start | bytes 11524
  13.5 193.5 %copy-start.19 = (f32[960]{0:T(1024)S(1)}, f32[960]{0:T(1024)}, u32[]{:S(2)}) copy-start(f32[960]{0:T(1024)} %param.42) | copy-start | bytes 11524
  207.7 226.5 %slice-start = ((s8[4915200]{0:T(1024)(128)(4,1)}), s8[4194304]{0:T(1024)(128)(4,1)S(1)}, s32[]{:S(2)}) async-start(s8[4915200]{0:T(1024)(128)(4,1)} %bitcast.102), calls=%async_computation | async-start | bytes 8388608
  342.0 92.3 %slice-start.1 = ((s8[4915200]{0:T(1024)(128)(4,1)}), s8[720896]{0:T(1024)(128)(4,1)S(1)}, s32[]{:S(2)}) async-start(s8[4915200]{0:T(1024)(128)(4,1)} %bitcast.102), calls=%async_computation.1 | async-start | bytes 1441792
  545.2 66.5 %copy-start.15 = (f32[8,960]{1,0:T(8,128)S(1)}, f32[8,960]{1,0:T(8,128)}, u32[]{:S(2)}) copy-start(f32[8,960]{1,0:T(8,128)} %get-tuple-element.115) | copy-start | bytes 92164
  746.2 1.6 copy-start.5
  749.1 1.8 copy-start.6
  752.3 1.6 copy-start.13
  754.0 5.1 copy-start.14
  754.0 7.2 copy-start.10
  754.0 8.0 %copy-start.4 = (f32[4,128,640]{2,1,0:T(8,128)S(1)}, f32[4,128,640]{2,1,0:T(8,128)}, u32[]{:S(2)}) copy-start(f32[4,128,640]{2,1,0:T(8,128)} %get-tuple-element.117) | copy-start | bytes 3932164
  761.2 1.9 copy-start.9
  762.0 2.5 copy-start.3

commit v5 on v4

--- a/solution.py
+++ b/solution.py
@@ -730,9 +730,10 @@
 
 
 def second_norm_back_inside(
-    count, grad_gate, grad_up, gate_all, up_all, normed, cot_all, middle, vectors, grad_middle, grad_all,
-    sums, gate_out, ours, theirs, ups, downs, staging, cot, low, buffers, gate_v, up_v, gate_w, up_w,
-    tile, partial, gate_partial, send, recv, local,
+    count, grad_gate, grad_up, gate_all, up_all, normed, hidden, down_all, cot_all, middle, vectors,
+    grad_middle, grad_all, sums, gate_out, forward_out, ours, theirs, ups, downs, staging, cot, low, buffers,
+    gate_v, up_v, gate_w, up_w, tile, partial, gate_partial, hidden_v, down_tile, forward_tile, send, recv,
+    local,
 ):
     place = Place(count)
     links = Links(send, recv, local)
@@ -779,16 +780,36 @@
         load.wait()
         gate_partial[strip(q, narrow)] = left_product(tile[...], gate_v[...]).astype(LOW)
 
+    k_down, links.kept = links.kept, links.kept + 1
+    load_hidden = links.keep(hidden, hidden_v)
+
+    def forward_sum():
+        load_hidden.wait()
+        store = None
+        for q in range(4):
+            load = pltpu.make_async_copy(
+                down_all.at[:, lanes(q, narrow)], down_tile, links.local.at[k_down]
+            )
+            load.start()
+            load.wait()
+            if store is not None:
+                store.wait()
+            forward_tile[...] = times(hidden_v[...], down_tile[...]).astype(LOW)
+            store = links.keep(forward_tile, forward_out.at[:, lanes(q, narrow)])
+            yield 1
+        store.wait()
+
     second_norm_back(
         count, partial, cot_all, middle, vectors, gate_partial, grad_middle, grad_all, sums, gate_out,
         ours, theirs, ups, downs, staging, cot, low, buffers, None, None, None, links, tokens, gate,
+        [forward_sum()],
     )
 
 
 def second_norm_back(
     count, grad_partial, cot_all, middle, vectors, gate_partial, grad_middle, grad_all, sums, gate_out,
     ours, theirs, ups, downs, staging, cot, low, buffers, send, recv, local, links=None,
-    prepare_tokens=None, prepare_gate=None,
+    prepare_tokens=None, prepare_gate=None, others=(),
 ):
     place = Place(count)
     if links is None:
@@ -846,7 +867,7 @@
     )
     advance(tokens_back)
     advance(tokens_back)
-    run([gate_back, tokens_back])
+    run([gate_back, tokens_back, *others])
 
 
 def mixed_and_output_inside(
@@ -965,11 +986,11 @@
         prepare_up,
     )
     gates = exchange_line(links, place, lambda b: gate_own.at[b], lambda b: gate_out.at[b])
-    advance(outs, mixes, outs)
+    advance(gates, outs, mixes, outs)
     kept.pass_on()
     if ready is not None:
         ready()
-    advance(sums_up, mixes, outs, gates)
+    advance(sums_up, mixes, outs)
     if others is not None:
         advance(others)
     advance(mixes)
@@ -1025,8 +1046,8 @@
     channel_in, hidden_in, block_in, grad_out, proj_out, down_out, width_sums, channel_sums, block_out, hidden_sums,
     theirs, ours, added,
     row_buffer, x, result, sums, proj_own, proj_ups, proj_downs, proj_staging, proj_low, width_table,
-    width_line, width_part, channel_table, channel_line, hidden_table, block_buffers, block_sum, block_ups, block_downs,
-    block_staging, block_low, down_buffers, send, recv, local, links=None, prepare_tokens=None, prepare_proj=None,
+    width_line, width_part, channel_table, channel_line, hidden_table, block_table, block_part, block_line, block_low,
+    down_buffers, send, recv, local, links=None, prepare_tokens=None, prepare_proj=None,
 ):
     place = Place(count)
     if links is None:
@@ -1081,7 +1102,7 @@
             value = x[here].astype(WIDE)
             total = grad_middle[here] + norm_rule(rows, grad, value, gain, sums, 3)
             for q in range(4):
-                result[q, here] = total[:, q * narrow : (q + 1) * narrow]
+                result[q, here] = total[:, q * narrow : (q + 1) * narrow].astype(LOW)
 
         yield from scatter_rows(
             links,
@@ -1092,16 +1113,18 @@
         )
         share.wait_send()
         mine = links.keep(result.at[row], grad_out.at[row])
-        yield from exchange_rows(
-            links, place, lambda q: result.at[q], lambda q: grad_out.at[q]
-        )
-        mine.wait()
         for q in range(4):
             width_part[q] = sums[:, q * narrow : (q + 1) * narrow]
         own = links.keep(width_part.at[row], width_table.at[row])
-        yield from exchange_rows(
+        vectors_out = exchange_rows(
             links, place, lambda q: width_part.at[q], lambda q: width_table.at[q]
         )
+        results_out = exchange_rows(
+            links, place, lambda q: result.at[q], lambda q: grad_out.at[q]
+        )
+        advance(vectors_out, results_out)
+        yield 1
+        finish(vectors_out)
         own.wait()
         width_line[z] = width_table[0] + width_table[1] + width_table[2] + width_table[3]
         yield from exchange_line(
@@ -1117,6 +1140,8 @@
         yield 1
         last.wait_recv()
         last.wait_send()
+        finish(results_out)
+        mine.wait()
 
     def projections():
         if prepare_proj is None:
@@ -1170,32 +1195,23 @@
         channel_sums[...] = total
 
     def blocks():
-        def keep_rows(h, rows, value):
-            block_sum[h, rows] = value
-
-        yield from scatter_rows(
-            links,
-            place,
-            lambda q, h: block_in.at[q, h],
-            block_buffers,
-            keep_rows,
-        )
-        length = block_sum.shape[1] * 2 // count
-        middle = count // 2
-
-        def term(b, i, rows):
-            at = pl.multiple_of(lax.rem(b, middle) * length + rows.start, 8)
-            return block_sum[lax.div(b, middle), pl.ds(at, rows.size)]
-
-        def keep_line(i, rows, value):
-            block_low[rows] = value.astype(LOW)
-
-        yield from scatter_line_in_parts(
-            links, place, lambda s: None, term, block_ups, block_downs, block_staging, keep_line
-        )
-        mine = links.keep(block_low, block_out.at[row])
+        own = links.keep(block_in.at[row], block_table.at[row])
+        yield from exchange_rows(
+            links, place, lambda q: block_in.at[q], lambda q: block_table.at[q]
+        )
+        own.wait()
+
+        for b in range(count):
+            block_part[b] = sum(block_table[q, b].astype(WIDE) for q in range(4)).astype(LOW)
+        own = links.keep(block_part.at[z], block_line.at[z])
+        yield from exchange_line(
+            links, place, lambda b: block_part.at[b], lambda b: block_line.at[b]
+        )
+        own.wait()
+        block_low[...] = sum(block_line[b].astype(WIDE) for b in range(count)).astype(LOW)
+        own = links.keep(block_low, block_out.at[row])
         yield from exchange_rows(links, place, lambda q: block_low, lambda q: block_out.at[q])
-        mine.wait()
+        own.wait()
 
     proj_sum, token_sum = projections(), tokens()
     small = [channels(), hidden(), blocks()]
@@ -1265,7 +1281,7 @@
 
 def forward(
     count, taps, x, cot, wxy, wout, wgate, wup, wdown, blk, cvec, wvec, spots,
-    nf_out, x_out, cot_own, wxy_out, wout_out, gate_own, up_own, down_all, blocks_out, vectors_out,
+    nf_out, x_out, cot_all, wxy_out, wout_out, gate_all, up_own, down_all, blocks_out, vectors_out,
     width_out, branch_out, gelu_out, side_out, conv_out, in_out, dec_out, state_out, entering_out,
     mixed_out, middle_out, normed_out,
     x_all, nf, wxy_all, wout_all, blocks, cvec_all, wvec_all, vectors, width, stage, arrived, branch,
@@ -1366,7 +1382,7 @@
 
     def cotangent_rows():
         def spot(q):
-            return cot_own.at[:, lanes(q, narrow)]
+            return cot_all.at[strip(2 * z + col, quarter), lanes(q, narrow)]
 
         mine = Relay(links, cot.at[strip(row, quarter)], cot_here, spot(row))
         yield from exchange_rows(links, place, lambda q: cot.at[strip(q, quarter)], spot)
@@ -1376,6 +1392,18 @@
         mine = Relay(links, matrix.at[z], buffer, own.at[z])
         yield from exchange_line(links, place, lambda b: matrix.at[b], lambda b: own.at[b])
         mine.wait()
+
+    def all_hidden_columns(matrix, buffer, whole):
+        yield from hidden_columns(matrix, buffer, whole.at[row])
+        middle = count // 2
+
+        def at(q, h):
+            return whole.at[q, pl.ds(middle * h, middle)]
+
+        yield from gather_rows(links, place, lambda h: at(row, h), at)
+
+    def cot_block(b):
+        return cot_all.at[strip(2 * b + col, quarter)]
 
     def output_rows():
         at = wout.shape[0]
@@ -1386,7 +1414,8 @@
     weights, rows_in = projections(), inputs()
     vectors_in, widths_in, blocks_in = channel_vectors(), width_vectors(), gate_blocks()
     cot_in, output_in, down_in = cotangent_rows(), output_rows(), hidden_rows()
-    gate_in = hidden_columns(wgate, gate_here, gate_own)
+    gate_in = all_hidden_columns(wgate, gate_here, gate_all)
+    cots = LineGather(links, place, cot_block(z), cot_block)
     up_in = hidden_columns(wup, up_here, up_own)
     advance(weights, rows_in, widths_in, vectors_in, blocks_in, cot_in)
     advance(weights, widths_in, vectors_in, blocks_in)
@@ -1452,6 +1481,7 @@
     finish(down_in)
     for copy in out:
         copy.wait_send()
+    cots.start()
 
     spot = spots[...]
     starting = spot == 0
@@ -1524,6 +1554,8 @@
     advance(mixes, up_in)
     finish(mixes)
     mine.wait()
+    cots.step(1)
+    advance(gate_in)
     keep(mixed_all, mixed_out)
 
     def product_rows(first):
@@ -1565,15 +1597,21 @@
     by_rows(quarter, second_norm)
     keep(middle, middle_out)
     keep(normed, normed_out)
+    advance(gate_in)
+    for step in range(2, count):
+        cots.step(step)
     finish(gate_in, up_in)
+    for step in range(count):
+        cots.ready(step)
+    cots.close()
     for copy in kept:
         copy.wait()
 
 
 def feed_forward(
-    count, normed, cot, wgate, up_own, wdown, biases, normed_all, cot_all, gate_all, up_all, hidden_out,
-    gate_out, up_out, sums, gate_w, up_w, down_w, piece, gate_v, up_v, grad_v, hidden, grad_gate,
-    grad_up, cot_here, normed_here, send, recv, local,
+    count, normed, cot_all, gate_all, up_own, wdown, biases, normed_all, up_all, hidden_out, gate_out,
+    up_out, sums, gate_w, up_w, down_w, piece, gate_v, up_v, grad_v, hidden, grad_gate, grad_up, normed_here,
+    send, recv, local,
 ):
     place = Place(count)
     links = Links(send, recv, local)
@@ -1583,11 +1621,8 @@
     narrow, pair = full // 4, 2 * quarter
     units = wdown.shape[0]
     middle = count // 2
-    kept = [
-        links.keep(wgate, gate_w.at[row]),
-        links.keep(up_own, up_w.at[row]),
-    ]
     load = links.keep(wdown, down_w)
+    kept = [links.keep(gate_all, gate_w), links.keep(up_own, up_w.at[row])]
 
     def tokens(own, buffer, whole):
         def at(b):
@@ -1659,39 +1694,36 @@
 
         by_rows(pair, body)
 
-    gates, ups = columns_of(wgate, gate_w), columns_of(up_own, up_w)
-    cots, cot_relay = tokens(cot, cot_here, cot_all)
+    ups = columns_of(up_own, up_w)
     norms, norm_relay = tokens(normed, normed_here, normed_all)
-    cots.start()
-    advance(gates, ups)
-    cot_relay.wait()
+    norms.start()
+    advance(ups)
+    norm_relay.wait()
     sums[...] = jnp.zeros(sums.shape, WIDE)
     load.wait()
-    cots.ready(0)
     back = with_piece(cot_all, backward)
-    neighbours(0, back)
     into = with_piece(normed_all, inward(gate_w, 0, gate_v))
-    for step in range(1, count):
-        cots.step(step)
-        if step == 1:
-            norms.start()
-        else:
-            norms.step(step - 1)
-        cots.ready(step)
-        neighbours(step, back)
-    advance(gates, ups)
-    norm_relay.wait()
-    finish(gates)
+
+    def backs(first, last):
+        def lap(b, carry):
+            back(b)
+            return carry
+
+        lax.fori_loop(first, last, lap, 0)
+
+    backs(0, middle)
+    norms.step(1)
+    backs(middle, count)
     for copy in kept:
         copy.wait()
     kept.clear()
-    kept.append(links.keep(gate_w, gate_all))
-    for step in range(count - 1):
+    for step in range(count):
+        if step > 1:
+            norms.step(step)
+        if step == 2:
+            advance(ups)
         norms.ready(step)
         neighbours(step, into)
-    norms.step(count - 1)
-    norms.ready(count - 1)
-    neighbours(count - 1, into)
     finish(ups)
     kept.append(links.keep(up_w, up_all))
     into_up = with_piece(normed_all, inward(up_w, 1, up_v))
@@ -1702,7 +1734,6 @@
         return carry
 
     lax.fori_loop(0, count, last, 0)
-    cots.close()
     norms.close()
     kept.append(links.keep(hidden, hidden_out))
     kept.append(links.keep(grad_gate, gate_out))
@@ -1818,7 +1849,7 @@
     hidden_shape = (rows_count, count, depth, hidden_part)
     here_scratch = pltpu.VMEM((tall, narrow), WIDE)
     (
-        normed_first, x_own, cot_own, wxy_all, wout_all, gate_own, up_own, down_all, blocks, vectors,
+        normed_first, x_own, cot_all, wxy_all, wout_all, gate_all, up_own, down_all, blocks, vectors,
         width_all, branch, gelu_in, side, conv, input_gate, decay_gate, state, entering, mixed_all,
         middle, normed_own,
     ) = call(
@@ -1841,10 +1872,10 @@
         [
             whole_tokens,
             ((quarter, full), LOW, False),
-            ((quarter, full), LOW, False),
+            ((cores * count * quarter, full), LOW, False),
             ((rows_count, count * depth, 2 * part), wxy_kind, False),
             ((width, narrow), LOW, False),
-            (hidden_shape[1:], wxy_kind, False),
+            (hidden_shape, wxy_kind, False),
             (hidden_shape[1:], wxy_kind, False),
             ((hidden_part, full), LOW, False),
             (blocks_shape, LOW, False),
@@ -1913,23 +1944,21 @@
     units_wide = pltpu.VMEM((hidden_tokens, hidden_part), WIDE)
     units_low = pltpu.VMEM((hidden_tokens, hidden_part), LOW)
     (
-        normed_second, cot_all, gate_all, up_all, hidden, grad_gate_low, grad_up_low, hidden_part_sums,
+        normed_second, up_all, hidden, grad_gate_low, grad_up_low, hidden_part_sums,
     ) = call(
         functools.partial(feed_forward, count),
         "feed_forward",
         2,
         [
             (normed_own, False),
-            (cot_own, False),
-            (gate_own, False),
+            (cot_all, False),
+            (gate_all, False),
             (up_own, False),
             (down_all, False),
             (biases, True),
         ],
         [
             ((hidden_tokens, full), LOW, False),
-            ((hidden_tokens, full), LOW, False),
-            (hidden_shape, wxy_kind, False),
             (hidden_shape, wxy_kind, False),
             units_rows,
             units_rows,
@@ -1948,7 +1977,6 @@
             units_low,
             units_low,
             pltpu.VMEM((quarter, full), LOW),
-            pltpu.VMEM((quarter, full), LOW),
         ],
         remote,
         local,
@@ -1969,7 +1997,7 @@
     back_scratch = token_scratch + [token_low, token_low, row_buffers(narrow, hidden_part)]
     inside = count <= 4
     if inside:
-        grad_middle, grad_middle_all, width_sums, gate_own = call(
+        grad_middle, grad_middle_all, width_sums, gate_own, forward_partial = call(
             functools.partial(second_norm_back_inside, count),
             "second_norm_back",
             5,
@@ -1979,11 +2007,13 @@
                 (gate_all, False),
                 (up_all, False),
                 (normed_second, False),
+                (hidden, False),
+                (down_all, False),
                 (cot_all, False),
                 (middle, True),
                 (width_all, True),
             ],
-            back_outs,
+            back_outs + [((hidden_tokens, full), LOW, False)],
             back_scratch
             + [
                 units_low,
@@ -1993,11 +2023,15 @@
                 pltpu.VMEM((hidden_tokens, narrow), LOW),
                 pltpu.VMEM(by_device, LOW),
                 pltpu.VMEM((full, hidden_part), LOW),
+                units_low,
+                pltpu.VMEM((hidden_part, narrow), LOW),
+                pltpu.VMEM((hidden_tokens, narrow), LOW),
             ],
             remote,
             local,
         )
     else:
+        forward_partial = times(hidden, down_all).astype(LOW)
         gate_all = gate_all.reshape(full, hidden_part).astype(LOW)
         up_all = up_all.reshape(full, hidden_part).astype(LOW)
         grad_normed_second = (
@@ -2021,7 +2055,7 @@
             remote,
             local,
         )
-    forward_partial = times(hidden, down_all).astype(LOW).reshape(by_device)
+    forward_partial = forward_partial.reshape(by_device)
 
     mixed_outs = [
         ((2, steps // 2, width), WIDE, True),
@@ -2222,12 +2256,12 @@
         block_sums.astype(LOW)
         .reshape(2 * heads, count, rows_count, back_share, block)
         .transpose(2, 1, 0, 3, 4)
-        .reshape(rows_count, 2, count // 2 * 2 * heads * back_share, block)
+        .reshape(rows_count, count, 2 * heads * back_share, block)
     )
     channel_shape, sums_shape = channel_part.shape, hidden_part_sums.shape
     block_rows = 2 * heads * back_share
     first_outs = [
-        ((rows_count, quarter, narrow), WIDE, False),
+        ((rows_count, quarter, narrow), LOW, False),
         ((rows_count, depth, 2 * part), LOW, False),
         ((hidden_part, narrow), WIDE, True),
         ((2, 8, narrow), WIDE, True),
@@ -2241,7 +2275,7 @@
         pltpu.VMEM((rows_count, quarter, full), LOW),
         row_buffers(quarter, full),
         token_low,
-        pltpu.VMEM((rows_count, quarter, narrow), WIDE),
+        pltpu.VMEM((rows_count, quarter, narrow), LOW),
         pltpu.VMEM((8, full), WIDE),
         pltpu.VMEM((count, rows_count, depth, 2 * part), LOW),
         *line_buffers(count, rows_count, depth, 2 * part),
@@ -2252,9 +2286,9 @@
         pltpu.VMEM((rows_count,) + channel_shape, WIDE),
         pltpu.VMEM((count,) + channel_shape, WIDE),
         pltpu.VMEM((rows_count,) + sums_shape, WIDE),
-        row_buffers(2 * block_in.shape[2], block),
-        pltpu.VMEM((2, block_in.shape[2], block), WIDE),
-        *line_buffers(count, 1, block_rows, block),
+        pltpu.VMEM(block_in.shape, LOW),
+        pltpu.VMEM(block_in.shape[1:], LOW),
+        pltpu.VMEM(block_in.shape[1:], LOW),
         pltpu.VMEM((block_rows, block), LOW),
         row_buffers(hidden_part, narrow),
     ]
@@ -2309,8 +2343,8 @@
         remote,
         local,
     )
-    branch_grad = side_by_side(proj_grad[:, :, :part]).astype(WIDE)
-    gelu_grad = side_by_side(proj_grad[:, :, part:]).astype(WIDE)
+    branch_grad = side_by_side(proj_grad[:, :, :part].astype(WIDE))
+    gelu_grad = side_by_side(proj_grad[:, :, part:].astype(WIDE))
     block_grads = (
         block_grads.reshape(rows_count, 2 * heads, back_share, block)
         .transpose(1, 0, 2, 3)
@@ -2325,12 +2359,12 @@
 
     return (
         layer_out.reshape(tall, narrow),
-        input_grad.reshape(tall, narrow),
+        input_grad.reshape(tall, narrow).astype(WIDE),
         branch_grad,
         gelu_grad,
         output_grad,
-        side_by_side(gate_blocks).astype(WIDE),
-        side_by_side(up_blocks).astype(WIDE),
+        side_by_side(gate_blocks.astype(WIDE)),
+        side_by_side(up_blocks.astype(WIDE)),
         down_grad,
         block_grads[:heads],
         block_grads[heads:],

time: 771 us -> 729 us (0.946)
  Pallas kernels: 717 us -> 682 us
  matrix products: 8.96 us -> 0 us
    pallas_call x6, Pallas kernels: 717 us -> 682 us  [call(): pl.pallas_call(kernel, in_specs=[VMEM if inside else ANY for _, inside in...]
    dot_general x1 -> x0, matrix products: 8.96 us -> none  [times(): return jnp.dot(piece, matrix, preferred_element_type=WIDE)]
where the time goes in v5:
time: 729 us; the launch traced here: 723 us
  Pallas kernels  682 us (94%)
  local copies, waits for them, and re-layouts  24 us (3%)
  other arithmetic  15.4 us (2%)
    pallas_call x6, Pallas kernels, call(): pl.pallas_call(kernel, in_specs=[VMEM if inside else ANY for _, inside in...  682 us

profile of v5, /device:TPU:0, one launch (start us, length us, event | category | flops | bytes accessed | tf_op | source)
XLA Modules:
  0.0 723.0 jit_solution(1214336422234697292)
XLA Ops:
  0.7 1.3 convert_element_type.58
  2.1 0.3 slice_bitcast_fusion.27
  2.4 1.2 maximum_maximum_fusion.wxy
  3.5 0.6 copy-done
  4.1 0.1 convert_element_type.62
  4.2 0.3 slice_bitcast_fusion.11
  4.6 1.4 copy-done.1
  5.9 0.1 convert_element_type.61
  6.0 0.3 slice_bitcast_fusion.15
  6.4 1.8 pad_maximum_fusion
  8.3 0.7 fusion.blk
  9.0 0.8 copy.50.spots
  9.8 1.2 convert_element_type.63.wdown
  11.0 0.8 convert_element_type.60.wout
  12.0 0.6 select_maximum_fusion.cvec
  12.7 0.6 pad.17.wvec
  13.3 231.0 %forward.1 = (bf16[1024,2560]{1,0:T(8,128)(2,1)}, bf16[128,2560]{1,0:T(8,128)(2,1)}, bf16[1024,2560]{1,0:T(8,128)(2,1)}, bf16[4,640,640]{2,1,0:T(8,128)(2,1)}, b...) custom-call(bf16[512,640]{1,0:T(8,128)(2,1)} %x.9, ...), custom_call_target="tpu_custom_call" | custom-call | tf_op jit(solution)/shard_map/forward/pallas_call | solution.py:488
  244.3 0.6 pad.18.biases
  245.0 81.8 %feed_forward.1 = (bf16[1024,2560]{1,0:T(8,128)(2,1)}, bf16[4,4,160,960]{3,2,1,0:T(8,128)(2,1)}, bf16[1024,960]{1,0:T(8,128)(2,1)}, bf16[1024,960]{1,0:T(8,128)(...) custom-call(bf16[128,2560]{1,0:T(8,128)(2,1)} %get-tuple-element.74.normed, ...), custom_call_target="tpu_custom_call" | custom-call | tf_op jit(solution)/shard_map/feed_forward/pallas_call | solution.py:488
  326.7 92.6 %second_norm_back.1 = (f32[128,2560]{1,0:T(8,128)}, bf16[1024,640]{1,0:T(8,128)(2,1)}, f32[8,2560]{1,0:T(8,128)}, bf16[2,320,960]{2,1,0:T(8,128)(2,1)}, bf16[1024,2560]{1,0:T(8,128)(2,1)}) custom-call(bf16[1024,960]{1,0:T(8,128)(2,1)} %get-tuple-element.79.grad_gate, bf16[1024,960]{1,0:T(8,128)(2,1)} %get-tuple-element.80.grad_up, ...), custom_call_target="tpu_custom_call" | custom-call | tf_op jit(solution)/shard_map/second_norm_back/pallas_call | solution.py:488
  419.3 101.8 %mixed_and_output.1 = (f32[2,128,1280]{2,1,0:T(8,128)}, bf16[4,128,640]{2,1,0:T(8,128)(2,1)}, bf16[2,320,960]{2,1,0:T(8,128)(2,1)}, bf16[4,160,960]{2,1,0:T(8,12...) custom-call(bf16[1024,640]{1,0:T(8,128)(2,1)} %get-tuple-element.86.grad_all, ...), custom_call_target="tpu_custom_call" | custom-call | tf_op jit(solution)/shard_map/mixed_and_output/pallas_call | solution.py:488
  521.2 59.9 %recurrence_backward.1 = (f32[16,1280]{1,0:T(8,128)}, f32[10,256,256]{2,1,0:T(8,128)}, bf16[4,256,640]{2,1,0:T(8,128)(2,1)}, f32[320,640]{1,0:T(8,128)}, bf16[4,160,960]{2,1,0:T(8,128)(2,1)}) custom-call(f32[264,1280]{1,0:T(8,128)} %get-tuple-element.92.proj, f32[256,1280]{1,0:T(8,128)} %get-tuple-element.93.side, f32[256,1280]{1,0:T(8,128)} %get-tuple-element.94.gelu_in, ...), custom_call_target="tpu_custom_call" | custom-call | tf_op jit(solution)/shard_map/recurrence_backward/pallas_call | solution.py:488
  581.1 1.9 convert_element_type.64
  583.0 1.2 copy.52
  584.2 0.6 pad.19.refs_2_
  584.9 115.0 %first_norm_back.1 = (bf16[4,128,640]{2,1,0:T(8,128)(2,1)}, bf16[4,160,640]{2,1,0:T(8,128)(2,1)}, f32[960,640]{1,0:T(8,128)}, f32[2,8,640]{2,1,0:T(8,128)}, f32[...) custom-call(bf16[1024,640]{1,0:T(8,128)(2,1)} %bitcast.108, bf16[2560,640]{1,0:T(8,128)(2,1)} %bitcast.102, ...), custom_call_target="tpu_custom_call" | custom-call | tf_op jit(solution)/shard_map/first_norm_back/pallas_call | solution.py:488
  699.9 0.8 fusion.4
  700.7 0.6 fusion.6
  701.3 0.3 convert_element_type.70
  701.6 0.2 slice_bitcast_fusion
  701.8 2.5 concatenate.32
  704.3 1.6 convert_element_type.69
  705.9 0.2 slice_bitcast_fusion.4
  706.1 2.5 concatenate.31
  708.6 0.3 slice_convert_fusion
  709.0 1.1 concatenate.30
  710.1 1.1 concatenate.29
  711.4 0.7 copy.53
  712.1 0.7 copy.54
  712.9 1.2 bitcast_convert_fusion
  714.1 1.6 fusion.2
  715.6 0.6 divide_multiply_fusion
  716.2 1.4 constant_dynamic-slice_fusion
  717.6 1.4 fusion.5
  719.0 0.8 copy.58
  719.9 0.9 copy.59
  720.8 0.5 copy-done.3
  721.3 1.4 copy.60
  (74 shorter events, 0.7 us)
Async XLA Ops:
  0.7 1.4 copy-start.6
  2.1 2.0 copy-start
  4.2 1.7 copy-start.1
  6.4 1.9 copy-start.11
  6.4 1.9 copy-start.12
  6.4 3.4 copy-start.2
  8.3 0.7 copy-start.24
  9.8 1.2 copy-start.7
  9.8 2.0 copy-start.19
  9.8 2.1 copy-start.20
  9.8 2.1 copy-start.21
  9.8 2.1 copy-start.22
  9.8 2.1 copy-start.23
  9.8 2.1 copy-start.16
  9.8 2.1 copy-start.15
  11.0 1.6 copy-start.25
  11.0 1.6 copy-start.26
  11.0 1.6 copy-start.27
  11.0 1.6 copy-start.28
  13.3 231.0 %copy-start.17 = (f32[960]{0:T(1024)S(1)}, f32[960]{0:T(1024)}, u32[]{:S(2)}) copy-start(f32[960]{0:T(1024)} %param.43) | copy-start | bytes 11524
  13.3 231.0 %copy-start.18 = (f32[960]{0:T(1024)S(1)}, f32[960]{0:T(1024)}, u32[]{:S(2)}) copy-start(f32[960]{0:T(1024)} %param.42) | copy-start | bytes 11524
  583.0 1.2 copy-start.14
  584.9 116.4 %copy-start.4 = (bf16[4,160,960]{2,1,0:T(8,128)(2,1)S(1)}, bf16[4,160,960]{2,1,0:T(8,128)(2,1)}, u32[]{:S(2)}) copy-start(bf16[4,160,960]{2,1,0:T(8,128)(2,1)} %get-tuple-element.119) | copy-start | bytes 3686404
  706.1 2.5 copy-start.5
  710.1 1.1 copy-start.13
  711.3 1.6 copy-start.10
  712.1 6.9 copy-start.9
  712.9 7.0 copy-start.8
  719.0 2.2 copy-start.3

commit v6 on v5

--- a/solution.py
+++ b/solution.py
@@ -662,17 +662,26 @@
 
 
 def recurrence_back_inside(
-    count, taps, proj, side, gelu_in, spots, vectors, blocks, conv_in, in_gate, dec_gate, state_in,
-    entering, grad_mixed, output_partial, up_own, sums_out, blocks_out, all_out, output_out, up_out, branch_low, gelu_low, stage, reach, local_grad, branch, ends, table, heads_in,
-    heads_here, padded, spread, ups, downs, staging, own, up_here, send, recv, local,
+    count, taps, proj_hbm, side_hbm, gelu_hbm, spots, vectors, blocks_hbm, conv_hbm, in_hbm, dec_hbm,
+    state_hbm, entering, mixed_hbm, output_partial, up_own, sums_out, blocks_out, all_out, output_out, up_out, branch_low, gelu_low, stage, reach, local_grad, branch, ends, table, heads_in,
+    heads_here, padded, spread, ups, downs, staging, own, up_here, proj, side, gelu_in, blocks, conv_in,
+    in_gate, dec_gate, state_in, grad_mixed, send, recv, local,
 ):
     place = Place(count)
     links = Links(send, recv, local)
+    load = links.keep(output_partial, own)
+    arrays = [
+        links.keep(source, target)
+        for source, target in (
+            (dec_hbm, dec_gate), (mixed_hbm, grad_mixed), (side_hbm, side), (state_hbm, state_in),
+            (blocks_hbm, blocks), (conv_hbm, conv_in), (in_hbm, in_gate), (proj_hbm, proj),
+            (gelu_hbm, gelu_in),
+        )
+    ]
     greet(place, rows=True, line=True)
     row, z = place.row, place.dp
     part = stage.shape[2] // 2
     kept = Relay(links, up_own.at[z], up_here, up_out.at[z])
-    load = links.keep(output_partial, own)
 
     output_half = ups.shape[2]
 
@@ -696,6 +705,8 @@
     load.wait()
     advance(output_sum, up_line)
     kept.pass_on()
+    for array in arrays:
+        array.wait()
 
     def gelu_back(h, at):
         grad = grad_mixed[:, at] * state_in[:, at] * gelu_slope(gelu_in[:, at])
@@ -737,12 +748,12 @@
 ):
     place = Place(count)
     links = Links(send, recv, local)
-    greet(place, rows=True, line=True, cores=True)
     loads = [links.keep(grad_gate, gate_v), links.keep(grad_up, up_v)]
     pieces = [
         (links.keep(gate_all.at[q], gate_w.at[q]), links.keep(up_all.at[q], up_w.at[q]))
         for q in range(4)
     ]
+    greet(place, rows=True, line=True, cores=True)
     quarter, full = middle.shape
     narrow, units = full // 4, gate_v.shape[1]
     for load in loads:
@@ -878,7 +889,6 @@
 ):
     place = Place(count)
     links = Links(send, recv, local)
-    greet(place, rows=True, line=True, cores=True)
     loads = [
         links.keep(source, target)
         for source, target in (
@@ -886,6 +896,7 @@
             (hidden, hidden_v),
         )
     ]
+    greet(place, rows=True, line=True, cores=True)
     steps = mixed_partial.shape[0] // 4
     narrow = grad_v.shape[1]
     for load in loads[:2]:
@@ -1227,11 +1238,11 @@
     proj_own = rest[18]
     place = Place(count)
     links = Links(send, recv, local)
-    greet(place, rows=True, line=True, cores=True)
     loads = [
         links.keep(source, target)
         for source, target in ((grad_proj, grad_v), (nf, nf_v), (wxy, wxy_v))
     ]
+    greet(place, rows=True, line=True, cores=True)
     quarter, full = grad_middle.shape
     narrow, tall = full // 4, 4 * quarter
     depth = proj_own.shape[2]
@@ -1616,13 +1627,13 @@
     place = Place(count)
     links = Links(send, recv, local)
     row, z, col = place.row, place.dp, place.col
-    greet(place, rows=True, line=True, cores=True)
     quarter, full = normed.shape
     narrow, pair = full // 4, 2 * quarter
     units = wdown.shape[0]
     middle = count // 2
     load = links.keep(wdown, down_w)
     kept = [links.keep(gate_all, gate_w), links.keep(up_own, up_w.at[row])]
+    greet(place, rows=True, line=True, cores=True)
 
     def tokens(own, buffer, whole):
         def at(b):
@@ -2135,21 +2146,18 @@
             "recurrence_backward",
             7,
             [
-                (array, True)
-                for array in (
-                    branch,
-                    side,
-                    gelu_in,
-                    spots,
-                    vectors,
-                    blocks,
-                    conv,
-                    input_gate,
-                    decay_gate,
-                    state,
-                    entering,
-                    grad_mixed,
-                )
+                (branch, False),
+                (side, False),
+                (gelu_in, False),
+                (spots, True),
+                (vectors, True),
+                (blocks, False),
+                (conv, False),
+                (input_gate, False),
+                (decay_gate, False),
+                (state, False),
+                (entering, True),
+                (grad_mixed, False),
             ]
             + [
                 (output_partial.reshape((count,) + output_matrix.shape), False),
@@ -2178,6 +2186,15 @@
                 *line_buffers(count, output_parts, output_matrix.shape[0] // output_parts, narrow),
                 pltpu.VMEM((count,) + output_matrix.shape, LOW),
                 pltpu.VMEM((depth, hidden_part), LOW),
+                pltpu.VMEM((steps + 8, width), WIDE),
+                tokens_scratch,
+                tokens_scratch,
+                pltpu.VMEM((2 * heads, block, block), LOW),
+                tokens_scratch,
+                tokens_scratch,
+                tokens_scratch,
+                tokens_scratch,
+                tokens_scratch,
             ],
             remote,
             local,

time: 729 us -> 719 us (0.986)
  Pallas kernels: 682 us -> 671 us
    pallas_call x6, Pallas kernels: 682 us -> 671 us  [call(): pl.pallas_call(kernel, in_specs=[VMEM if inside else ANY for _, inside in...]
where the time goes in v6:
time: 719 us; the launch traced here: 712 us
  Pallas kernels  671 us (93%)
  local copies, waits for them, and re-layouts  24 us (3%)
  other arithmetic  15.4 us (2%)
    pallas_call x6, Pallas kernels, call(): pl.pallas_call(kernel, in_specs=[VMEM if inside else ANY for _, inside in...  671 us

profile of v6, /device:TPU:0, one launch (start us, length us, event | category | flops | bytes accessed | tf_op | source)
XLA Modules:
  0.0 712.3 jit_solution(9176219274219123111)
XLA Ops:
  0.7 1.3 convert_element_type.58
  2.1 0.3 slice_bitcast_fusion.27
  2.4 1.2 maximum_maximum_fusion.wxy
  3.5 0.6 copy-done
  4.1 0.1 convert_element_type.62
  4.2 0.3 slice_bitcast_fusion.11
  4.6 1.4 copy-done.1
  5.9 0.1 convert_element_type.61
  6.0 0.3 slice_bitcast_fusion.15
  6.4 1.8 pad_maximum_fusion
  8.3 0.7 fusion.blk
  9.0 0.8 copy.50.spots
  9.8 1.2 convert_element_type.63.wdown
  11.0 0.8 convert_element_type.60.wout
  12.0 0.6 select_maximum_fusion.cvec
  12.7 0.6 pad.17.wvec
  13.3 231.0 %forward.1 = (bf16[1024,2560]{1,0:T(8,128)(2,1)}, bf16[128,2560]{1,0:T(8,128)(2,1)}, bf16[1024,2560]{1,0:T(8,128)(2,1)}, bf16[4,640,640]{2,1,0:T(8,128)(2,1)}, b...) custom-call(bf16[512,640]{1,0:T(8,128)(2,1)} %x.9, ...), custom_call_target="tpu_custom_call" | custom-call | tf_op jit(solution)/shard_map/forward/pallas_call | solution.py:488
  244.3 0.6 pad.18.biases
  245.0 81.8 %feed_forward.1 = (bf16[1024,2560]{1,0:T(8,128)(2,1)}, bf16[4,4,160,960]{3,2,1,0:T(8,128)(2,1)}, bf16[1024,960]{1,0:T(8,128)(2,1)}, bf16[1024,960]{1,0:T(8,128)(...) custom-call(bf16[128,2560]{1,0:T(8,128)(2,1)} %get-tuple-element.74.normed, ...), custom_call_target="tpu_custom_call" | custom-call | tf_op jit(solution)/shard_map/feed_forward/pallas_call | solution.py:488
  326.7 89.0 %second_norm_back.1 = (f32[128,2560]{1,0:T(8,128)}, bf16[1024,640]{1,0:T(8,128)(2,1)}, f32[8,2560]{1,0:T(8,128)}, bf16[2,320,960]{2,1,0:T(8,128)(2,1)}, bf16[1024,2560]{1,0:T(8,128)(2,1)}) custom-call(bf16[1024,960]{1,0:T(8,128)(2,1)} %get-tuple-element.79.grad_gate, bf16[1024,960]{1,0:T(8,128)(2,1)} %get-tuple-element.80.grad_up, ...), custom_call_target="tpu_custom_call" | custom-call | tf_op jit(solution)/shard_map/second_norm_back/pallas_call | solution.py:488
  415.7 99.7 %mixed_and_output.1 = (f32[2,128,1280]{2,1,0:T(8,128)}, bf16[4,128,640]{2,1,0:T(8,128)(2,1)}, bf16[2,320,960]{2,1,0:T(8,128)(2,1)}, bf16[4,160,960]{2,1,0:T(8,12...) custom-call(bf16[1024,640]{1,0:T(8,128)(2,1)} %get-tuple-element.86.grad_all, ...), custom_call_target="tpu_custom_call" | custom-call | tf_op jit(solution)/shard_map/mixed_and_output/pallas_call | solution.py:488
  515.4 54.6 %recurrence_backward.1 = (f32[16,1280]{1,0:T(8,128)}, f32[10,256,256]{2,1,0:T(8,128)}, bf16[4,256,640]{2,1,0:T(8,128)(2,1)}, f32[320,640]{1,0:T(8,128)}, bf16[4,160,960]{2,1,0:T(8,128)(2,1)}) custom-call(f32[264,1280]{1,0:T(8,128)} %get-tuple-element.92.proj_hbm, f32[256,1280]{1,0:T(8,128)} %get-tuple-element.93.side_hbm, ...), custom_call_target="tpu_custom_call" | custom-call | tf_op jit(solution)/shard_map/recurrence_backward/pallas_call | solution.py:488
  570.0 1.9 convert_element_type.64
  571.9 1.2 copy.52
  573.1 0.6 pad.19.refs_2_
  573.8 115.4 %first_norm_back.1 = (bf16[4,128,640]{2,1,0:T(8,128)(2,1)}, bf16[4,160,640]{2,1,0:T(8,128)(2,1)}, f32[960,640]{1,0:T(8,128)}, f32[2,8,640]{2,1,0:T(8,128)}, f32[...) custom-call(bf16[1024,640]{1,0:T(8,128)(2,1)} %bitcast.108, bf16[2560,640]{1,0:T(8,128)(2,1)} %bitcast.102, ...), custom_call_target="tpu_custom_call" | custom-call | tf_op jit(solution)/shard_map/first_norm_back/pallas_call | solution.py:488
  689.2 0.8 fusion.4
  690.0 0.6 fusion.6
  690.6 0.3 convert_element_type.70
  690.9 0.2 slice_bitcast_fusion
  691.1 2.5 concatenate.32
  693.6 1.6 convert_element_type.69
  695.2 0.2 slice_bitcast_fusion.4
  695.4 2.5 concatenate.31
  697.9 0.3 slice_convert_fusion
  698.3 1.1 concatenate.30
  699.4 1.1 concatenate.29
  700.7 0.7 copy.53
  701.4 0.7 copy.54
  702.2 1.2 bitcast_convert_fusion
  703.4 1.6 fusion.2
  704.9 0.6 divide_multiply_fusion
  705.5 1.4 constant_dynamic-slice_fusion
  706.9 1.4 fusion.5
  708.3 0.8 copy.58
  709.2 0.9 copy.59
  710.1 0.5 copy-done.3
  710.6 1.4 copy.60
  (74 shorter events, 0.7 us)
Async XLA Ops:
  0.7 1.4 copy-start.6
  2.1 2.0 copy-start
  4.2 1.7 copy-start.1
  6.4 1.9 copy-start.11
  6.4 1.9 copy-start.12
  6.4 3.4 copy-start.2
  8.3 0.7 copy-start.24
  9.8 1.2 copy-start.7
  9.8 2.0 copy-start.19
  9.8 2.1 copy-start.20
  9.8 2.1 copy-start.21
  9.8 2.1 copy-start.22
  9.8 2.1 copy-start.23
  9.8 2.1 copy-start.16
  9.8 2.1 copy-start.15
  11.0 1.6 copy-start.25
  11.0 1.6 copy-start.26
  11.0 1.6 copy-start.27
  11.0 1.6 copy-start.28
  13.3 231.0 %copy-start.17 = (f32[960]{0:T(1024)S(1)}, f32[960]{0:T(1024)}, u32[]{:S(2)}) copy-start(f32[960]{0:T(1024)} %param.43) | copy-start | bytes 11524
  13.3 231.0 %copy-start.18 = (f32[960]{0:T(1024)S(1)}, f32[960]{0:T(1024)}, u32[]{:S(2)}) copy-start(f32[960]{0:T(1024)} %param.42) | copy-start | bytes 11524
  571.9 1.2 copy-start.14
  573.8 116.8 %copy-start.4 = (bf16[4,160,960]{2,1,0:T(8,128)(2,1)S(1)}, bf16[4,160,960]{2,1,0:T(8,128)(2,1)}, u32[]{:S(2)}) copy-start(bf16[4,160,960]{2,1,0:T(8,128)(2,1)} %get-tuple-element.119) | copy-start | bytes 3686404
  695.4 2.5 copy-start.5
  699.4 1.1 copy-start.13
  700.6 1.6 copy-start.10
  701.4 6.9 copy-start.9
  702.2 7.0 copy-start.8
  708.3 2.2 copy-start.3

commit v7 on v6

--- a/solution.py
+++ b/solution.py
@@ -1486,13 +1486,13 @@
         else:
             mine = links.keep(source, arrived.at[row])
     advance(output_in, gate_in)
+    cots.start()
     mine.wait()
     for copy in out:
         copy.wait_recv()
     finish(down_in)
     for copy in out:
         copy.wait_send()
-    cots.start()
 
     spot = spots[...]
     starting = spot == 0

time: 719 us -> 713 us (level)
  no operation moved by 1% of the time
where the time goes in v7:
time: 713 us; the launch traced here: 708 us
  Pallas kernels  667 us (94%)
  local copies, waits for them, and re-layouts  24 us (3%)
  other arithmetic  15.4 us (2%)
    pallas_call x6, Pallas kernels, call(): pl.pallas_call(kernel, in_specs=[VMEM if inside else ANY for _, inside in...  667 us

profile of v7, /device:TPU:0, one launch (start us, length us, event | category | flops | bytes accessed | tf_op | source)
XLA Modules:
  0.0 707.6 jit_solution(5521186355091590422)
XLA Ops:
  0.7 1.3 convert_element_type.58
  2.1 0.3 slice_bitcast_fusion.27
  2.4 1.2 maximum_maximum_fusion.wxy
  3.5 0.6 copy-done
  4.1 0.1 convert_element_type.62
  4.2 0.3 slice_bitcast_fusion.11
  4.6 1.4 copy-done.1
  5.9 0.1 convert_element_type.61
  6.0 0.3 slice_bitcast_fusion.15
  6.4 1.8 pad_maximum_fusion
  8.3 0.7 fusion.blk
  9.0 0.8 copy.50.spots
  9.8 1.2 convert_element_type.63.wdown
  11.0 0.8 convert_element_type.60.wout
  12.0 0.6 select_maximum_fusion.cvec
  12.7 0.6 pad.17.wvec
  13.3 233.2 %forward.1 = (bf16[1024,2560]{1,0:T(8,128)(2,1)}, bf16[128,2560]{1,0:T(8,128)(2,1)}, bf16[1024,2560]{1,0:T(8,128)(2,1)}, bf16[4,640,640]{2,1,0:T(8,128)(2,1)}, b...) custom-call(bf16[512,640]{1,0:T(8,128)(2,1)} %x.9, ...), custom_call_target="tpu_custom_call" | custom-call | tf_op jit(solution)/shard_map/forward/pallas_call | solution.py:488
  246.6 0.6 pad.18.biases
  247.2 74.0 %feed_forward.1 = (bf16[1024,2560]{1,0:T(8,128)(2,1)}, bf16[4,4,160,960]{3,2,1,0:T(8,128)(2,1)}, bf16[1024,960]{1,0:T(8,128)(2,1)}, bf16[1024,960]{1,0:T(8,128)(...) custom-call(bf16[128,2560]{1,0:T(8,128)(2,1)} %get-tuple-element.74.normed, ...), custom_call_target="tpu_custom_call" | custom-call | tf_op jit(solution)/shard_map/feed_forward/pallas_call | solution.py:488
  321.2 88.8 %second_norm_back.1 = (f32[128,2560]{1,0:T(8,128)}, bf16[1024,640]{1,0:T(8,128)(2,1)}, f32[8,2560]{1,0:T(8,128)}, bf16[2,320,960]{2,1,0:T(8,128)(2,1)}, bf16[1024,2560]{1,0:T(8,128)(2,1)}) custom-call(bf16[1024,960]{1,0:T(8,128)(2,1)} %get-tuple-element.79.grad_gate, bf16[1024,960]{1,0:T(8,128)(2,1)} %get-tuple-element.80.grad_up, ...), custom_call_target="tpu_custom_call" | custom-call | tf_op jit(solution)/shard_map/second_norm_back/pallas_call | solution.py:488
  410.1 99.5 %mixed_and_output.1 = (f32[2,128,1280]{2,1,0:T(8,128)}, bf16[4,128,640]{2,1,0:T(8,128)(2,1)}, bf16[2,320,960]{2,1,0:T(8,128)(2,1)}, bf16[4,160,960]{2,1,0:T(8,12...) custom-call(bf16[1024,640]{1,0:T(8,128)(2,1)} %get-tuple-element.86.grad_all, ...), custom_call_target="tpu_custom_call" | custom-call | tf_op jit(solution)/shard_map/mixed_and_output/pallas_call | solution.py:488
  509.6 54.8 %recurrence_backward.1 = (f32[16,1280]{1,0:T(8,128)}, f32[10,256,256]{2,1,0:T(8,128)}, bf16[4,256,640]{2,1,0:T(8,128)(2,1)}, f32[320,640]{1,0:T(8,128)}, bf16[4,160,960]{2,1,0:T(8,128)(2,1)}) custom-call(f32[264,1280]{1,0:T(8,128)} %get-tuple-element.92.proj_hbm, f32[256,1280]{1,0:T(8,128)} %get-tuple-element.93.side_hbm, ...), custom_call_target="tpu_custom_call" | custom-call | tf_op jit(solution)/shard_map/recurrence_backward/pallas_call | solution.py:488
  564.5 1.9 convert_element_type.64
  566.4 1.2 copy.52
  567.6 0.6 pad.19.refs_2_
  568.2 116.3 %first_norm_back.1 = (bf16[4,128,640]{2,1,0:T(8,128)(2,1)}, bf16[4,160,640]{2,1,0:T(8,128)(2,1)}, f32[960,640]{1,0:T(8,128)}, f32[2,8,640]{2,1,0:T(8,128)}, f32[...) custom-call(bf16[1024,640]{1,0:T(8,128)(2,1)} %bitcast.108, bf16[2560,640]{1,0:T(8,128)(2,1)} %bitcast.102, ...), custom_call_target="tpu_custom_call" | custom-call | tf_op jit(solution)/shard_map/first_norm_back/pallas_call | solution.py:488
  684.5 0.8 fusion.4
  685.3 0.6 fusion.6
  685.9 0.3 convert_element_type.70
  686.2 0.2 slice_bitcast_fusion
  686.4 2.5 concatenate.32
  688.9 1.6 convert_element_type.69
  690.5 0.2 slice_bitcast_fusion.4
  690.7 2.5 concatenate.31
  693.2 0.3 slice_convert_fusion
  693.6 1.1 concatenate.30
  694.7 1.1 concatenate.29
  696.0 0.7 copy.53
  696.7 0.7 copy.54
  697.5 1.2 bitcast_convert_fusion
  698.7 1.6 fusion.2
  700.2 0.6 divide_multiply_fusion
  700.8 1.4 constant_dynamic-slice_fusion
  702.2 1.4 fusion.5
  703.7 0.8 copy.58
  704.5 0.9 copy.59
  705.4 0.5 copy-done.3
  705.9 1.4 copy.60
  (74 shorter events, 0.7 us)
Async XLA Ops:
  0.7 1.4 copy-start.6
  2.1 2.0 copy-start
  4.2 1.7 copy-start.1
  6.4 1.9 copy-start.11
  6.4 1.9 copy-start.12
  6.4 3.4 copy-start.2
  8.3 0.7 copy-start.24
  9.8 1.2 copy-start.7
  9.8 2.0 copy-start.19
  9.8 2.1 copy-start.20
  9.8 2.1 copy-start.21
  9.8 2.1 copy-start.22
  9.8 2.1 copy-start.23
  9.8 2.1 copy-start.16
  9.8 2.1 copy-start.15
  11.0 1.6 copy-start.25
  11.0 1.6 copy-start.26
  11.0 1.6 copy-start.27
  11.0 1.6 copy-start.28
  13.3 233.3 %copy-start.17 = (f32[960]{0:T(1024)S(1)}, f32[960]{0:T(1024)}, u32[]{:S(2)}) copy-start(f32[960]{0:T(1024)} %param.43) | copy-start | bytes 11524
  13.3 233.3 %copy-start.18 = (f32[960]{0:T(1024)S(1)}, f32[960]{0:T(1024)}, u32[]{:S(2)}) copy-start(f32[960]{0:T(1024)} %param.42) | copy-start | bytes 11524
  566.4 1.2 copy-start.14
  568.2 117.7 %copy-start.4 = (bf16[4,160,960]{2,1,0:T(8,128)(2,1)S(1)}, bf16[4,160,960]{2,1,0:T(8,128)(2,1)}, u32[]{:S(2)}) copy-start(bf16[4,160,960]{2,1,0:T(8,128)(2,1)} %get-tuple-element.119) | copy-start | bytes 3686404
  690.7 2.5 copy-start.5
  694.7 1.1 copy-start.13
  695.9 1.6 copy-start.10
  696.7 6.9 copy-start.9
  697.5 7.0 copy-start.8
  703.7 2.2 copy-start.3
